TPU v7x, 32 devices: a whole 2x2x4 slice. The times are simulated.
32 devices in a mesh: img: 4 (over x, core), mlp: 8 (over z, y).
Axes of the slice: x: 2, y: 2, z: 4, core: 2. Of those that a mesh axis runs over, the one named last changes fastest.
Arguments:
- tokens: bfloat16 [64, 14, 14, 384], P(('img', 'mlp')), may hold values from -6 to 6
- ln1_gain: bfloat16 [384], replicated, may hold values from 0.5 to 1.5
- ln1_bias: bfloat16 [384], replicated, may hold values from -1.75 to 1.75
- f_weight: bfloat16 [384, 772], replicated, may hold values from -0.3125 to 0.3125
- f_bias: bfloat16 [772], replicated, may hold values from -1.75 to 1.75
- dw_small: bfloat16 [9, 384], replicated, may hold values from -2 to 2
- dw_middle: bfloat16 [25, 384], replicated, may hold values from -1.25 to 1.25
- dw_large: bfloat16 [49, 384], replicated, may hold values from -0.875 to 0.875
- h_weight: bfloat16 [384, 384], replicated, may hold values from -0.3125 to 0.3125
- h_bias: bfloat16 [384], replicated, may hold values from -1.75 to 1.75
- proj_weight: bfloat16 [384, 384], replicated, may hold values from -0.3125 to 0.3125
- proj_bias: bfloat16 [384], replicated, may hold values from -1.75 to 1.75
- ln2_gain: bfloat16 [384], replicated, may hold values from 0.5 to 1.5
- ln2_bias: bfloat16 [384], replicated, may hold values from -1.75 to 1.75
- fc1_weight: bfloat16 [384, 1536], P(None, 'mlp'), may hold values from -0.3125 to 0.3125
- fc1_bias: bfloat16 [1536], P('mlp'), may hold values from -1.75 to 1.75
- fc2_weight: bfloat16 [1536, 384], P('mlp'), may hold values from -0.15625 to 0.15625
- fc2_bias: bfloat16 [384], replicated, may hold values from -1.75 to 1.75
- out_grad: bfloat16 [64, 14, 14, 384], P(('img', 'mlp')), may hold values from -6 to 6
Outputs:
- block_out: float32 [64, 14, 14, 384], P(('img', 'mlp'))
- tokens_grad: float32 [64, 14, 14, 384], P(('img', 'mlp'))
- ln1_gain_grad: float32 [384], replicated
- ln1_bias_grad: float32 [384], replicated
- f_weight_grad: float32 [384, 772], replicated
- f_bias_grad: float32 [772], replicated
- dw_small_grad: float32 [9, 384], replicated
- dw_middle_grad: float32 [25, 384], replicated
- dw_large_grad: float32 [49, 384], replicated
- h_weight_grad: float32 [384, 384], replicated
- h_bias_grad: float32 [384], replicated
- proj_weight_grad: float32 [384, 384], replicated
- proj_bias_grad: float32 [384], replicated
- ln2_gain_grad: float32 [384], replicated
- ln2_bias_grad: float32 [384], replicated
- fc1_weight_grad: float32 [384, 1536], P(None, 'mlp')
- fc1_bias_grad: float32 [1536], P('mlp')
- fc2_weight_grad: float32 [1536, 384], P('mlp')
- fc2_bias_grad: float32 [384], replicated
All inputs are finite; a program needn't handle non-finite values.
Results may differ from a plain program's by a relative error of at most 0.017.
Values may be sent and summed in bfloat16 or wider, within the bound.
No kernel may reach another device: no remote copies, remote signals or barrier semaphores. Data moves between devices by JAX's collectives and lax.ppermute only.
A program may use at most 128 MiB of HBM per device.

v0:
```python
import math

import jax
import jax.numpy as jnp
from jax import lax
from jax.sharding import PartitionSpec as P

highest = lax.Precision.HIGHEST
epsilon = 1e-05


def layer_norm(values, ln_gain, ln_bias):
    average = jnp.mean(values, axis=-1, keepdims=True)
    centred = values - average
    variance = jnp.mean(centred * centred, axis=-1, keepdims=True)
    return centred * lax.rsqrt(variance + epsilon) * ln_gain + ln_bias


def exact_gelu(values):
    return jax.nn.gelu(values, approximate=False)


def depthwise(values, kernel):
    extent = math.isqrt(kernel.shape[0])
    filters = kernel.reshape(extent, extent, 1, kernel.shape[1])
    return lax.conv_general_dilated(
        values,
        filters,
        (1, 1),
        "SAME",
        dimension_numbers=("NHWC", "HWIO", "NHWC"),
        feature_group_count=values.shape[-1],
        precision=highest,
    )


def context_mix(context, gates, dw_small, dw_middle, dw_large):
    level_one = exact_gelu(depthwise(context, dw_small))
    level_two = exact_gelu(depthwise(level_one, dw_middle))
    level_three = exact_gelu(depthwise(level_two, dw_large))
    global_ctx = exact_gelu(jnp.mean(level_three, axis=(1, 2), keepdims=True))
    return (
        level_one * gates[..., 0:1]
        + level_two * gates[..., 1:2]
        + level_three * gates[..., 2:3]
        + global_ctx * gates[..., 3:4]
    )


def matmul(left, right):
    return jnp.dot(left, right, preferred_element_type=jnp.float32)


def inner_rows(left, right):
    return lax.dot_general(
        left, right, (((0,), (0,)), ((), ())), preferred_element_type=jnp.float32
    )


def outer_cols(left, right):
    return lax.dot_general(
        left, right, (((1,), (1,)), ((), ())), preferred_element_type=jnp.float32
    )


def column_sum(values):
    return jnp.sum(values.astype(jnp.float32), axis=0)


def shards(
    tokens,
    ln1_gain,
    ln1_bias,
    f_weight,
    f_bias,
    dw_small,
    dw_middle,
    dw_large,
    h_weight,
    h_bias,
    proj_weight,
    proj_bias,
    ln2_gain,
    ln2_bias,
    fc1_weight,
    fc1_bias,
    fc2_weight,
    fc2_bias,
    out_grad,
):
    images = tokens.shape[0]
    side = tokens.shape[1]
    width = tokens.shape[3]
    rows = images * side * side
    inputs = tokens.astype(jnp.float32).reshape(rows, width)
    cotangent = out_grad.reshape(rows, width)
    cot_float = cotangent.astype(jnp.float32)
    normed_float, norm_pull = jax.vjp(
        layer_norm, inputs, ln1_gain.astype(jnp.float32), ln1_bias.astype(jnp.float32)
    )
    normed = normed_float.astype(jnp.bfloat16)
    focal = matmul(normed, f_weight) + f_bias.astype(jnp.float32)
    query = focal[:, :width]
    context = focal[:, width : 2 * width].reshape(images, side, side, width)
    gates = focal[:, 2 * width :].reshape(images, side, side, 4)
    kernels = (
        dw_small.astype(jnp.float32),
        dw_middle.astype(jnp.float32),
        dw_large.astype(jnp.float32),
    )
    aggregated_float, mix_pull = jax.vjp(
        context_mix, context, gates, kernels[0], kernels[1], kernels[2]
    )
    aggregated = aggregated_float.reshape(rows, width).astype(jnp.bfloat16)
    modulator = matmul(aggregated, h_weight) + h_bias.astype(jnp.float32)
    mixed = (query * modulator).astype(jnp.bfloat16)
    branch = matmul(mixed, proj_weight) + proj_bias.astype(jnp.float32)
    middle = inputs + branch
    normed_two_float, norm_two_pull = jax.vjp(
        layer_norm, middle, ln2_gain.astype(jnp.float32), ln2_bias.astype(jnp.float32)
    )
    normed_two = normed_two_float.astype(jnp.bfloat16)
    full_first, full_bias, full_second = (
        lax.all_gather(fc1_weight, "mlp", axis=1, tiled=True),
        lax.all_gather(fc1_bias, "mlp", axis=0, tiled=True),
        lax.all_gather(fc2_weight, "mlp", axis=0, tiled=True),
    )
    before = matmul(normed_two, full_first) + full_bias.astype(jnp.float32)
    hidden_float, gelu_pull = jax.vjp(exact_gelu, before)
    hidden = hidden_float.astype(jnp.bfloat16)
    mlp_sum = matmul(hidden, full_second)
    d_hidden = outer_cols(cotangent, full_second)
    d_before = gelu_pull(d_hidden)[0].astype(jnp.bfloat16)
    fc1_weight_grad, fc1_bias_grad, fc2_weight_grad = (
        lax.psum_scatter(
            inner_rows(normed_two, d_before).astype(jnp.bfloat16),
            "mlp",
            scatter_dimension=1,
            tiled=True,
        ).astype(jnp.float32),
        lax.psum_scatter(
            column_sum(d_before).astype(jnp.bfloat16), "mlp", scatter_dimension=0, tiled=True
        ).astype(jnp.float32),
        lax.psum_scatter(
            inner_rows(hidden, cotangent).astype(jnp.bfloat16),
            "mlp",
            scatter_dimension=0,
            tiled=True,
        ).astype(jnp.float32),
    )
    d_normed_two = outer_cols(d_before, full_first)
    fc1_weight_grad, fc1_bias_grad, fc2_weight_grad = (
        lax.psum(fc1_weight_grad.astype(jnp.bfloat16), "img").astype(jnp.float32),
        lax.psum(fc1_bias_grad.astype(jnp.bfloat16), "img").astype(jnp.float32),
        lax.psum(fc2_weight_grad.astype(jnp.bfloat16), "img").astype(jnp.float32),
    )
    block_out = middle + mlp_sum + fc2_bias.astype(jnp.float32)
    fc2_bias_local = column_sum(cot_float)
    d_norm_in, ln2_gain_local, ln2_bias_local = norm_two_pull(d_normed_two)
    d_middle = cot_float + d_norm_in
    d_branch = d_middle.astype(jnp.bfloat16)
    proj_weight_local = inner_rows(mixed, d_branch)
    proj_bias_local = column_sum(d_branch)
    d_mixed = outer_cols(d_branch, proj_weight)
    d_query = d_mixed * modulator
    d_modulator = (d_mixed * query).astype(jnp.bfloat16)
    h_weight_local = inner_rows(aggregated, d_modulator)
    h_bias_local = column_sum(d_modulator)
    d_aggregated = outer_cols(d_modulator, h_weight).reshape(images, side, side, width)
    d_context, d_gates, small_local, middle_local, large_local = mix_pull(d_aggregated)
    d_focal = jnp.concatenate(
        [d_query, d_context.reshape(rows, width), d_gates.reshape(rows, 4)], axis=1
    ).astype(jnp.bfloat16)
    f_weight_local = inner_rows(normed, d_focal)
    f_bias_local = column_sum(d_focal)
    d_normed = outer_cols(d_focal, f_weight)
    d_inputs, ln1_gain_local, ln1_bias_local = norm_pull(d_normed)
    tokens_grad = d_middle + d_inputs
    summed = lax.psum(
        (
            ln1_gain_local,
            ln1_bias_local,
            f_weight_local,
            f_bias_local,
            small_local,
            middle_local,
            large_local,
            h_weight_local,
            h_bias_local,
            proj_weight_local,
            proj_bias_local,
            ln2_gain_local,
            ln2_bias_local,
            fc2_bias_local,
        ),
        ("img", "mlp"),
    )
    block_out = block_out.reshape(images, side, side, width)
    tokens_grad = tokens_grad.reshape(images, side, side, width)
    return (
        block_out,
        tokens_grad,
        summed[0],
        summed[1],
        summed[2],
        summed[3],
        summed[4],
        summed[5],
        summed[6],
        summed[7],
        summed[8],
        summed[9],
        summed[10],
        summed[11],
        summed[12],
        fc1_weight_grad,
        fc1_bias_grad,
        fc2_weight_grad,
        summed[13],
    )


def solution(mesh):
    placed = (
        P(("img", "mlp"), None, None, None),
        P(),
        P(),
        P(),
        P(),
        P(),
        P(),
        P(),
        P(),
        P(),
        P(),
        P(),
        P(),
        P(),
        P(None, "mlp"),
        P("mlp"),
        P("mlp", None),
        P(),
        P(("img", "mlp"), None, None, None),
    )
    return jax.shard_map(
        shards,
        mesh=mesh,
        in_specs=placed,
        out_specs=(
            P(("img", "mlp"), None, None, None),
            P(("img", "mlp"), None, None, None),
            P(),
            P(),
            P(),
            P(),
            P(),
            P(),
            P(),
            P(),
            P(),
            P(),
            P(),
            P(),
            P(),
            P(None, "mlp"),
            P("mlp"),
            P("mlp", None),
            P(),
        ),
        check_vma=False,
    )
```

profile of v0, /device:TPU:0, one launch (start us, length us, event | category | flops | bytes accessed | tf_op | source)
XLA Modules:
  0.0 587.4 jit_solution(10257901541677260339)
XLA Ops:
  20.7 2.4 reshape.370
  24.4 2.9 broadcast_multiply_fusion
  33.1 3.8 fusion.78
  36.9 6.0 %multiply_multiply_fusion.10 = (f32[2,14,14,384]{3,0,2,1:T(2,128)S(1)}, f32[2,14,14,384]{3,0,2,1:T(2,128)}) fusion(f32[2,14,14,384]{3,0,2,1:T(2,128)S(1)} %get-tuple-element.146, u16[2,14,384]{2,0,1:T(2,128)(2,1)S(1)} %get-tuple-element.90, u16[2,14,384]{2,0,1:T(2,128)(2,1)S(1)} %get-tuple-element.91, u16[2,14,384]{2,0,1:T(2,128)(2,1)S(1)} %get-tuple-element.89), kind=kLoop, calls=%fused_computation.160 | loop fusion | flops 10687488 | bytes 1870848 | tf_op jit(solution)/shard_map/jvp()/mul | solution.py:20
  43.0 6.1 %fusion.77 = (u16[2,14,384]{2,0,1:T(2,128)(2,1)S(1)}, u16[2,14,384]{2,0,1:T(2,128)(2,1)S(1)}, u16[2,14,384]{2,0,1:T(2,128)(2,1)S(1)}, f32[2,14,14,384]{3,0,2,1:T(2,128)S(1)}) fusion(f32[2,14,14,384]{3,0,2,1:T(2,128)S(1)} %get-tuple-element.126, bf16[7,7,1,384]{3,2,1,0:T(2,128)(2,1)S(1)} %reshape.431), kind=kOutput, calls=%fused_computation.167 | convolution fusion | flops 71139840 | bytes 1306368 | tf_op jit(solution)/shard_map/jvp()/conv_general_dilated | solution.py:26
  49.1 5.5 fusion.93
  57.8 2.1 fusion.73
  62.3 23.6 %all-reduce.4 = bf16[1536]{0:T(1024)(128)(2,1)S(1)} all-reduce(bf16[1536]{0:T(1024)(128)(2,1)S(1)} %dynamic-update-slice), channel_id=1, replica_groups=mesh['img'=4,'mlp'=8] {'mlp'}, use_global_device_ids=true, to_apply=%add.4 | all-reduce | flops 1536 | bytes 6144
  98.8 2.1 bitcast_dynamic-update-slice_fusion
  103.9 2.3 multiply_convert_fusion.3
  108.7 2.3 convolution_add_fusion
  111.1 8.8 %fusion.94 = (bf16[1536]{0:T(1024)(128)(2,1)}, bf16[392,1536]{1,0:T(8,128)(2,1)S(1)}, f32[392,1536]{1,0:T(8,128)}) fusion(f32[392,1536]{1,0:T(8,128)S(1)} %convolution_add_fusion, bf16[392,384]{1,0:T(8,128)(2,1)S(1)} %reshape.353, bf16[1536,384]{1,0:T(8,128)(2,1)} %all-gather.5.cloned.1.call-done), kind=kOutput, calls=%fused_computation.207 | convolution fusion | flops 506374656 | bytes 7504896 | tf_op jit(solution)/shard_map/dot_general | solution.py:61
  121.0 2.1 convolution_convert_fusion.1
  123.1 3.4 multiply_reduce_fusion
  130.3 3.1 convert_reduce_fusion.3
  136.6 4.8 multiply_reduce_fusion.6
  144.8 2.3 multiply_convert_fusion
  148.2 2.1 convolution_convert_fusion
  152.7 7.0 %multiply_add_fusion = f32[2,14,14,384]{3,0,2,1:T(2,128)S(1)} fusion(f32[2,14,14,384]{3,0,2,1:T(2,128)} %get-tuple-element.127, f32[2,14,14,384]{3,0,2,1:T(2,128)} %multiply_add_fusion.1, bf16[7,7,384,1]{2,3,1,0:T(2,128)(2,1)S(1)} %copy-done.64, f32[2,14,14,384]{3,0,2,1:T(2,128)} %copy-done.53, f32[2,14,14]{0,2,1:T(8,128)S(1)} %copy-done.58, ...), kind=kOutput, calls=%fused_computation.142 | convolution fusion | flops 70419456 | bytes 3049760 | tf_op jit(solution)/shard_map/transpose(jvp())/conv_general_dilated | solution.py:26
  159.7 3.5 fusion.62
  168.5 2.8 fusion.91
  173.4 3.4 convolution_reduce_fusion.1
  176.8 4.2 fusion.28
  181.0 8.1 %reduce-scatter.3.cloned.1.call-done = bf16[384,192]{0,1:T(8,128)(2,1)} async-done(((bf16[384,1536]{0,1:T(8,128)(2,1)}), bf16[384,192]{0,1:T(8,128)(2,1)}) %reduce-scatter.3.cloned.1.call-update) | async-done | bytes 147472 | tf_op jit(solution)/shard_map/reduce_scatter | solution.py:135
  189.1 66.3 %reduce-scatter.5.cloned.1.call-done = bf16[192,384]{1,0:T(8,128)(2,1)} async-done(((bf16[1536,384]{1,0:T(8,128)(2,1)}), bf16[192,384]{1,0:T(8,128)(2,1)}) %reduce-scatter.5.cloned.1.call-update) | async-done | bytes 147472 | tf_op jit(solution)/shard_map/reduce_scatter | solution.py:144
  260.7 11.2 %convolution_reduce_fusion = f32[7,7,384]{2,1,0:T(8,128)S(1)} fusion(f32[2,14,14,384]{3,0,2,1:T(2,128)S(1)} %copy-done.18, f32[2,14,14,384]{3,0,2,1:T(2,128)S(1)} %copy-done.54), kind=kOutput, calls=%fused_computation.59 | convolution fusion | flops 68161536 | bytes 1279488 | tf_op jit(solution)/shard_map/transpose(jvp())/conv_general_dilated | solution.py:26
  273.4 3.1 fusion.23
  281.1 19.4 %all-reduce.5 = bf16[1536]{0:T(1024)(128)(2,1)S(1)} all-reduce(bf16[1536]{0:T(1024)(128)(2,1)S(1)} %copy-done.85), channel_id=3, replica_groups=mesh['img'=4,'mlp'=8] {'mlp'}, use_global_device_ids=true, to_apply=%region_37.0.clone | all-reduce | flops 1536 | bytes 6144
  300.6 5.6 psum.133
  310.1 112.6 %all-reduce.13.cloned.1.call-done = (f32[384]{0:T(512)}, f32[384]{0:T(512)}, f32[772]{0:T(1024)}, f32[9,384]{1,0:T(8,128)}, f32[25,384]{1,0:T(8,128)}, /*index=5...) async-done(((f32[384]{0:T(512)}, f32[384]{0:T(512)}, f32[772]{0:T(1024)}, f32[9,384]{1,0:T(8,128)}, f32[25,384]{1,0:T(8,128)}, ...) | async-done | bytes 66080 | tf_op jit(solution)/shard_map/psum | solution.py:179
  422.8 145.4 %all-reduce.15.cloned.1.call-done = (f32[384,772]{0,1:T(8,128)}, f32[49,384]{1,0:T(8,128)}, f32[384,384]{1,0:T(8,128)}, f32[384,384]{1,0:T(8,128)}) async-done(((f32[384,772]{0,1:T(8,128)}, f32[49,384]{1,0:T(8,128)}, f32[384,384]{1,0:T(8,128)}, f32[384,384]{1,0:T(8,128)}), (f32[384,772]{0,1:T(8,128)}, f32[49,384]{1,0:T(8,128)}, f32[384,384]{1,0:T(8,128)}, ...) | async-done | bytes 2440720 | tf_op jit(solution)/shard_map/psum | solution.py:179
  570.7 2.4 copy.259
  (362 shorter events, 89.4 us)
Async XLA Ops:
  7.2 101.5 %all-gather.3.cloned.1.call-start = ((), (), s32[]{:S(2)}) async-start(), calls=%async_computation.2 | async-start | bytes 1327104 | tf_op jit(solution)/shard_map/all_gather | solution.py:124
  8.0 103.1 %all-gather.5.cloned.1.call-start = ((), (), s32[]{:S(2)}) async-start(), calls=%async_computation.3 | async-start | bytes 1327104 | tf_op jit(solution)/shard_map/all_gather | solution.py:126
  8.7 180.3 %reduce-scatter.3.cloned.1.call-start = ((), (), s32[]{:S(2)}) async-start(), calls=%async_computation.4 | async-start | bytes 1327104 | tf_op jit(solution)/shard_map/reduce_scatter | solution.py:135
  13.0 93.3 %copy-start.1 = (f32[392,384]{1,0:T(8,128)}, f32[392,384]{1,0:T(8,128)S(1)}, u32[]{:S(2)}) copy-start(f32[392,384]{1,0:T(8,128)S(1)} %reshape.346) | copy-start | bytes 1806340
  14.8 8.3 %copy-start.11 = (f32[392,772]{1,0:T(8,128)}, f32[392,772]{1,0:T(8,128)S(1)}, u32[]{:S(2)}) copy-start(f32[392,772]{1,0:T(8,128)S(1)} %convolution_add_fusion.1) | copy-start | bytes 3631492
  43.0 14.9 %copy-start.14 = (f32[14,2,16,384]{3,2,1,0:T(8,128)S(1)}, f32[14,2,16,384]{3,2,1,0:T(8,128)}, u32[]{:S(2)}) copy-start(f32[14,2,16,384]{3,2,1,0:T(8,128)} %copy-done.13) | copy-start | bytes 2064388
  49.1 10.8 %copy-start.3 = (f32[2,14,14,384]{3,0,2,1:T(2,128)}, f32[2,14,14,384]{3,0,2,1:T(2,128)S(1)}, u32[]{:S(2)}) copy-start(f32[2,14,14,384]{3,0,2,1:T(2,128)S(1)} %get-tuple-element.147) | copy-start | bytes 1806340
  56.2 29.8 %copy-start.35 = (bf16[2,14,14,384]{3,0,2,1:T(2,128)(2,1)S(1)}, bf16[2,14,14,384]{3,0,2,1:T(2,128)(2,1)}, u32[]{:S(2)}) copy-start(bf16[2,14,14,384]{3,0,2,1:T(2,128)(2,1)} %param.37) | copy-start | bytes 903172
  57.0 28.9 %copy-start.100 = (bf16[384]{0:T(512)(128)(2,1)S(1)}, bf16[384]{0:T(512)(128)(2,1)}, u32[]{:S(2)}) copy-start(bf16[384]{0:T(512)(128)(2,1)} %param.32) | copy-start | bytes 2308
  57.0 28.9 %copy-start.101 = (bf16[384]{0:T(512)(128)(2,1)S(1)}, bf16[384]{0:T(512)(128)(2,1)}, u32[]{:S(2)}) copy-start(bf16[384]{0:T(512)(128)(2,1)} %param.31) | copy-start | bytes 2308
  57.8 28.3 %copy-start.102 = (bf16[384]{0:T(512)(128)(2,1)S(1)}, bf16[384]{0:T(512)(128)(2,1)}, u32[]{:S(2)}) copy-start(bf16[384]{0:T(512)(128)(2,1)} %param.36) | copy-start | bytes 2308
  86.1 41.6 %copy-start.22 = (bf16[392,384]{1,0:T(8,128)(2,1)}, bf16[392,384]{1,0:T(8,128)(2,1)S(1)}, u32[]{:S(2)}) copy-start(bf16[392,384]{1,0:T(8,128)(2,1)S(1)} %reshape.353) | copy-start | bytes 903172
  111.1 9.9 %copy-start.8 = (f32[392,384]{1,0:T(8,128)S(1)}, f32[392,384]{1,0:T(8,128)}, u32[]{:S(2)}) copy-start(f32[392,384]{1,0:T(8,128)} %copy-done.7) | copy-start | bytes 1806340
  127.6 127.7 %reduce-scatter.5.cloned.1.call-start = ((), (), s32[]{:S(2)}) async-start(), calls=%async_computation.5 | async-start | bytes 1327104 | tf_op jit(solution)/shard_map/reduce_scatter | solution.py:144
  134.6 10.2 %copy-start.81 = (f32[2,384]{1,0:T(2,128)S(1)}, f32[2,384]{1,0:T(2,128)}, u32[]{:S(2)}) copy-start(f32[2,384]{1,0:T(2,128)} %get-tuple-element.123) | copy-start | bytes 9220
  152.4 154.5 %all-reduce.17.cloned.1.call-start = ((), (), s32[]{:S(2)}) async-start(), calls=%async_computation.8 | async-start | bytes 589824 | tf_op jit(solution)/shard_map/psum | solution.py:153
  163.6 7.8 %copy-start.60 = (bf16[392,4]{1,0:T(8,128)(2,1)}, bf16[392,4]{1,0:T(8,128)(2,1)S(1)}, u32[]{:S(2)}) copy-start(bf16[392,4]{1,0:T(8,128)(2,1)S(1)} %copy.154) | copy-start | bytes 9412
  176.8 78.6 %copy-start.27 = (bf16[392,384]{1,0:T(8,128)(2,1)S(1)}, bf16[392,384]{1,0:T(8,128)(2,1)}, u32[]{:S(2)}) copy-start(bf16[392,384]{1,0:T(8,128)(2,1)} %copy-done.26) | copy-start | bytes 903172
  176.8 78.6 %copy-start.29 = (bf16[392,384]{1,0:T(8,128)(2,1)S(1)}, bf16[392,384]{1,0:T(8,128)(2,1)}, u32[]{:S(2)}) copy-start(bf16[392,384]{1,0:T(8,128)(2,1)} %copy-done.28) | copy-start | bytes 903172
  176.8 81.8 %copy-start.38 = (bf16[392,384]{1,0:T(8,128)(2,1)S(1)}, bf16[392,384]{1,0:T(8,128)(2,1)}, u32[]{:S(2)}) copy-start(bf16[392,384]{1,0:T(8,128)(2,1)} %reshape.358) | copy-start | bytes 903172
  181.0 79.7 %copy-start.18 = (f32[2,14,14,384]{3,0,2,1:T(2,128)S(1)}, f32[2,14,14,384]{3,0,2,1:T(2,128)}, u32[]{:S(2)}) copy-start(f32[2,14,14,384]{3,0,2,1:T(2,128)} %copy-done.17) | copy-start | bytes 1806340
  181.0 79.7 %copy-start.54 = (f32[2,14,14,384]{3,0,2,1:T(2,128)S(1)}, f32[2,14,14,384]{3,0,2,1:T(2,128)}, u32[]{:S(2)}) copy-start(f32[2,14,14,384]{3,0,2,1:T(2,128)} %multiply_add_fusion.1) | copy-start | bytes 1806340
  255.4 167.4 %all-reduce.13.cloned.1.call-start = ((), (), s32[]{:S(2)}) async-start(), calls=%async_computation.6 | async-start | bytes 184320 | tf_op jit(solution)/shard_map/psum | solution.py:179
  260.4 307.7 %all-reduce.15.cloned.1.call-start = ((), (), s32[]{:S(2)}) async-start(), calls=%async_computation.7 | async-start | bytes 4915200 | tf_op jit(solution)/shard_map/psum | solution.py:179
  422.8 150.4 %copy-start.86 = (f32[772]{0:T(1024)S(1)}, f32[772]{0:T(1024)}, u32[]{:S(2)}) copy-start(f32[772]{0:T(1024)} %get-tuple-element.161) | copy-start | bytes 9268
  422.8 151.0 %copy-start.69 = (f32[9,384]{1,0:T(8,128)S(1)}, f32[9,384]{1,0:T(8,128)}, u32[]{:S(2)}) copy-start(f32[9,384]{1,0:T(8,128)} %get-tuple-element.162) | copy-start | bytes 41476
  422.8 151.6 %copy-start.65 = (f32[25,384]{1,0:T(8,128)S(1)}, f32[25,384]{1,0:T(8,128)}, u32[]{:S(2)}) copy-start(f32[25,384]{1,0:T(8,128)} %get-tuple-element.163) | copy-start | bytes 115204
  422.8 153.6 %copy-start.95 = (f32[384]{0:T(512)S(1)}, f32[384]{0:T(512)}, u32[]{:S(2)}) copy-start(f32[384]{0:T(512)} %get-tuple-element.166) | copy-start | bytes 4612
  568.1 8.8 %copy-start.56 = (f32[384,384]{1,0:T(8,128)S(1)}, f32[384,384]{1,0:T(8,128)}, u32[]{:S(2)}) copy-start(f32[384,384]{1,0:T(8,128)} %get-tuple-element.167) | copy-start | bytes 1769476
  570.7 7.7 %copy-start.93 = (f32[384]{0:T(512)S(1)}, f32[384]{0:T(512)}, u32[]{:S(2)}) copy-start(f32[384]{0:T(512)} %get-tuple-element.169) | copy-start | bytes 4612
  570.7 8.2 %copy-start.92 = (f32[384]{0:T(512)S(1)}, f32[384]{0:T(512)}, u32[]{:S(2)}) copy-start(f32[384]{0:T(512)} %get-tuple-element.170) | copy-start | bytes 4612
  570.7 8.8 %copy-start.91 = (f32[384]{0:T(512)S(1)}, f32[384]{0:T(512)}, u32[]{:S(2)}) copy-start(f32[384]{0:T(512)} %get-tuple-element.174) | copy-start | bytes 4612
  (83 other events, 303.0 us)
Sparse Core Ops, SparseCore 0:
  10.3 43.7 all-gather.2
  56.2 39.8 all-gather.4
  127.7 61.2 reduce-scatter.2
  192.3 62.9 reduce-scatter.4
  257.5 31.2 all-reduce.16
  296.9 125.8 all-reduce.12
  430.9 137.1 all-reduce.14
where the time goes:
time: 597 us; the launch traced here: 587 us
  waiting for transfers between devices  334 us (56%)
  matrix products  79.4 us (13%)
  local copies, waits for them, and re-layouts  62 us (10%)
  blocking collectives  48.6 us (8%)
  other arithmetic  45.5 us (8%)
  between operations  17.3 us (3%)
    psum x2, waiting for transfers between devices, shards(): lax.psum((ln1_gain_local, ln1_bias_local, f_weight_local, f_bias_local, s...  258 us
    reduce_scatter x1, waiting for transfers between devices, shards(): lax.psum_scatter(inner_rows(hidden, cotangent).astype(jnp.bfloat16), 'mlp...  66.3 us
    unnamed x2, blocking collectives  43 us
    conv_general_dilated x9, matrix products, depthwise(): lax.conv_general_dilated(values, filters, (1, 1), 'SAME', dimension_numbe...  42.5 us
    unnamed x236, local copies, waits for them, and re-layouts  21 us
    dot_general x5, matrix products, outer_cols(): lax.dot_general(left, right, (((1,), (1,)), ((), ())), preferred_element_...  18.5 us
  transfers between devices with their start and end apart: 7, of which 4 were waited for; matrix products, arithmetic and copies ran while one was open for 26% of the time, Pallas kernels for 0%

commit v1 on v0

v1 whole, which is shorter than its diff:
```python
import functools
import math

import jax
import jax.numpy as jnp
from jax import lax
from jax.experimental import pallas as pl
from jax.experimental.pallas import tpu as pltpu
from jax.experimental.layout import Layout, with_layout_constraint
from jax.sharding import Mesh
from jax.sharding import PartitionSpec as P

epsilon = 1e-05
lanes = 128
sublanes = 8
edge = 3
extents = (3, 5, 7)
starts = (0, 9, 34)
taps = 83
LN1_GAIN, LN1_BIAS, QUERY_BIAS, CONTEXT_BIAS, GATE_BIAS = 83, 84, 85, 86, 87
H_BIAS, PROJ_BIAS, LN2_GAIN, LN2_BIAS, FC2_BIAS = 88, 89, 90, 91, 92
f32 = jnp.float32
bf16 = jnp.bfloat16


def flip(values, axis="core", size=2, bit=1):
    return lax.ppermute(values, axis, [(place, place ^ bit) for place in range(size)])


def exchange(values, axes):
    return lax.all_to_all(values, axes, split_axis=0, concat_axis=0, tiled=True)


def after(values, *others):
    return lax.optimization_barrier((values,) + others)[0]


def nn(left, right):
    return jnp.dot(left, right, preferred_element_type=f32)


def nt(left, right):
    return lax.dot_general(left, right, (((1,), (1,)), ((), ())), preferred_element_type=f32)


def tn(left, right):
    return lax.dot_general(left, right, (((0,), (0,)), ((), ())), preferred_element_type=f32)


def gelu_pair(values):
    below = 0.5 * (1.0 + lax.erf(values * math.sqrt(0.5)))
    density = jnp.exp(values * values * -0.5) * (1.0 / math.sqrt(2.0 * math.pi))
    return values * below, below + values * density


class Shape:
    def __init__(self, images, side, width):
        self.images, self.side, self.width = images, side, width
        self.tiles = width // lanes
        self.slots = images * self.tiles
        self.patches = side * side
        self.segment = -(-self.patches // 8) * 8
        self.rows = images * self.segment
        self.line = side * sublanes
        self.centre = edge * self.line
        self.grid = (side + 2 * edge) * self.line
        self.inner = side * self.line
        self.packed = self.patches * self.slots
        self.block = next(size for size in (80, 40, 16, 8) if self.rows % size == 0)

    def places(self):
        return [
            (image, tile, tile * self.images + image)
            for image in range(self.images)
            for tile in range(self.tiles)
        ]


def columns(tile):
    return slice(tile * lanes, (tile + 1) * lanes)


def unpack(shape, packed, rows):
    for image, tile, slot in shape.places():
        first = image * shape.segment
        rows[first : first + shape.patches, columns(tile)] = packed[
            pl.ds(slot, shape.patches, stride=shape.slots), :
        ]
    for image in range(shape.images):
        first = image * shape.segment
        spare = shape.segment - shape.patches
        if spare:
            rows[first + shape.patches : first + shape.segment, 0 : shape.width] = jnp.zeros(
                (spare, shape.width), f32
            )


def pack(shape, rows, packed):
    for image, tile, slot in shape.places():
        first = image * shape.segment
        packed[pl.ds(slot, shape.patches, stride=shape.slots), :] = rows[
            first : first + shape.patches, columns(tile)
        ]


def blocks(shape, body, init=None):
    def step(index, carry):
        first = pl.multiple_of(index * shape.block, shape.block)
        return body(pl.ds(first, shape.block), carry)

    return lax.fori_loop(0, shape.rows // shape.block, step, init)


def normalise(values):
    average = jnp.mean(values, axis=-1, keepdims=True)
    centred = values - average
    variance = jnp.mean(centred * centred, axis=-1, keepdims=True)
    scale = lax.rsqrt(variance + epsilon)
    return centred * scale, scale


def norm_back(values, grad, gain):
    unit, scale = normalise(values)
    inner = grad * gain
    first = jnp.mean(inner, axis=-1, keepdims=True)
    second = jnp.mean(inner * unit, axis=-1, keepdims=True)
    return scale * (inner - first - unit * second), grad * unit


def fold(values):
    return jnp.sum(values.reshape(values.shape[0] // 8, 8, values.shape[1]), axis=0)


def row_sum(values):
    return jnp.sum(values, axis=0, keepdims=True)


def spread_taps(shape, small, tap_ref):
    tap_ref[...] = jnp.zeros_like(tap_ref)
    for _, tile, slot in shape.places():
        tap_ref[pl.ds(slot, taps, stride=sublanes), :] = small[0:taps, columns(tile)]


def line_at(shape, ref, line):
    first = pl.multiple_of(line * shape.line, shape.line)
    values = ref[pl.ds(first, shape.line), :]
    return [values[w * sublanes : (w + 1) * sublanes] for w in range(shape.side)]


def correlate(shape, source, tap_ref, level, line, turned):
    extent = extents[level]
    reach = extent // 2
    totals = [None] * shape.side
    for down in range(extent):
        values = line_at(shape, source, line + down + edge - reach)
        for along in range(extent):
            entry = down * extent + along
            if turned:
                entry = extent * extent - 1 - entry
            tap = tap_ref[pl.ds((starts[level] + entry) * sublanes, sublanes), :]
            for w in range(shape.side):
                other = w + along - reach
                if 0 <= other < shape.side:
                    term = values[other] * tap
                    totals[w] = term if totals[w] is None else totals[w] + term
    return jnp.concatenate(totals, axis=0)


def tap_grads(shape, source, grad, level, out):
    extent = extents[level]
    reach = extent // 2
    for down in range(extent):

        def step(line, totals, down=down):
            values = line_at(shape, source, line + down + edge - reach)
            grads = line_at(shape, grad, line + edge)
            result = []
            for along in range(extent):
                total = totals[along]
                for w in range(shape.side):
                    other = w + along - reach
                    if 0 <= other < shape.side:
                        total = total + values[other] * grads[w]
                result.append(total)
            return tuple(result)

        zero = jnp.zeros((sublanes, lanes), f32)
        totals = lax.fori_loop(0, shape.side, step, (zero,) * extent)
        for along in range(extent):
            out[pl.ds((starts[level] + down * extent + along) * sublanes, sublanes), :] = totals[
                along
            ]


def clear_edges(shape, ref):
    zeros = jnp.zeros((shape.centre, lanes), f32)
    ref[0 : shape.centre, :] = zeros
    ref[shape.centre + shape.inner : shape.grid, :] = zeros


def gate_values(shape, normed, f_turned, small, gates):
    weight = f_turned[2 * shape.width : 2 * shape.width + 4, :].astype(f32)
    wide = jnp.concatenate(
        [jnp.broadcast_to(weight[g : g + 1], (lanes, shape.width)) for g in range(4)]
    ).astype(bf16)
    bias = small[GATE_BIAS : GATE_BIAS + 1, :]
    wide_bias = jnp.concatenate(
        [jnp.broadcast_to(bias[:, g : g + 1], (1, lanes)) for g in range(4)], axis=1
    )
    gates[...] = nt(normed[...], wide) + wide_bias


def level_rows(shape, level, image, slot):
    return level[pl.ds(shape.centre + slot, shape.segment, stride=sublanes), :]


def run_levels(shape, moves, chain, tap_ref):
    total = jnp.zeros((sublanes, lanes), f32)
    for level, source, target, slope in chain:
        clear_edges(shape, target)

        def line_step(line, total, level=level, source=source, target=target, slope=slope):
            before = correlate(shape, source, tap_ref, level, line, False)
            value, rise = gelu_pair(before)
            here = pl.multiple_of((line + edge) * shape.line, shape.line)
            target[pl.ds(here, shape.line), :] = value
            slope[pl.ds(pl.multiple_of(line * shape.line, shape.line), shape.line), :] = rise
            if level == 2:
                total = total + fold(value)
            return total

        total = lax.fori_loop(0, shape.side, line_step, total)
        moves.leave(target, slope)
    return total


def entry_kernel(
    shape,
    moves,
    tokens,
    f_turned,
    out_grad,
    dw_small,
    dw_middle,
    dw_large,
    ln1_gain,
    ln1_bias,
    f_bias,
    h_bias,
    proj_bias,
    ln2_gain,
    ln2_bias,
    fc2_bias,
    small,
    cot,
    inputs,
    normed,
    query,
    gates,
    context,
    one,
    slope_one,
    tap_ref,
    packed,
    wide,
):
    width = shape.width
    for source, first in zip((dw_small, dw_middle, dw_large), starts):
        small[first : first + source.shape[0], :] = source[...].astype(f32)
    shared = f_bias[...].astype(f32).reshape(1, 2 * width + 4)
    vectors = {
        QUERY_BIAS: shared[:, 0:width],
        CONTEXT_BIAS: shared[:, width : 2 * width],
        GATE_BIAS: jnp.concatenate(
            [shared[:, 2 * width :], jnp.zeros((1, width - 4), f32)], axis=1
        ),
    }
    for row, source in (
        (LN1_GAIN, ln1_gain),
        (LN1_BIAS, ln1_bias),
        (H_BIAS, h_bias),
        (PROJ_BIAS, proj_bias),
        (LN2_GAIN, ln2_gain),
        (LN2_BIAS, ln2_bias),
        (FC2_BIAS, fc2_bias),
    ):
        vectors[row] = source[...].astype(f32).reshape(1, width)
    for row, value in vectors.items():
        small[row : row + 1, :] = value
    last = FC2_BIAS + 1
    small[last:, :] = jnp.zeros((small.shape[0] - last, width), f32)
    moves.leave(small)
    moves.arrive(tokens)
    packed[...] = tokens[...].astype(f32)
    unpack(shape, packed, inputs)
    moves.leave(inputs)
    spread_taps(shape, small, tap_ref)
    gain = small[LN1_GAIN : LN1_GAIN + 1, :]
    bias = small[LN1_BIAS : LN1_BIAS + 1, :]

    def first_norm(rows, carry):
        unit, _ = normalise(inputs[rows, :])
        normed[rows, :] = (unit * gain + bias).astype(bf16)
        return carry

    blocks(shape, first_norm, 0)
    moves.leave(normed)
    moves.arrive(out_grad)
    packed[...] = out_grad[...].astype(f32)
    unpack(shape, packed, wide)
    cot[...] = wide[...].astype(bf16)
    moves.leave(cot)
    moves.arrive(f_turned)
    wide[...] = (
        nt(normed[...], f_turned[width : 2 * width, :]) + small[CONTEXT_BIAS : CONTEXT_BIAS + 1, :]
    )
    context[...] = jnp.zeros_like(context)
    for image, tile, slot in shape.places():
        first = image * shape.segment
        context[pl.ds(shape.centre + slot, shape.patches, stride=sublanes), :] = wide[
            first : first + shape.patches, columns(tile)
        ]
    moves.leave(context)
    query[...] = nt(normed[...], f_turned[0:width, :]) + small[QUERY_BIAS : QUERY_BIAS + 1, :]
    moves.leave(query)
    gate_values(shape, normed, f_turned, small, gates)
    moves.leave(gates)
    run_levels(shape, moves, ((0, context, one, slope_one),), tap_ref)


def modulation_kernel(
    shape,
    moves,
    one,
    small,
    gates,
    h_weight,
    query,
    inputs,
    proj_weight,
    far_one,
    far_gates,
    far_query,
    modulator,
    aggregated,
    mixed,
    middle,
    normed_two,
    two,
    three,
    slope_two,
    slope_three,
    pooled,
    wide,
    tap_ref,
):
    chain = ((1, one, two, slope_two), (2, two, three, slope_three))
    moves.arrive(small)
    spread_taps(shape, small, tap_ref)
    moves.copy(one, far_one)
    moves.copy(gates, far_gates)
    moves.copy(query, far_query)
    total = run_levels(shape, moves, chain, tap_ref)
    value, rise = gelu_pair(total * (1.0 / shape.patches))
    pooled[0:sublanes, :] = value
    pooled[sublanes : 2 * sublanes, :] = rise * (1.0 / shape.patches)
    moves.leave(pooled)
    moves.arrive(h_weight, proj_weight)
    for image, tile, slot in shape.places():
        rows = pl.ds(image * shape.segment, shape.segment)
        wide[rows, columns(tile)] = (
            level_rows(shape, one, image, slot) * gates[rows, columns(0)]
            + level_rows(shape, two, image, slot) * gates[rows, columns(1)]
            + level_rows(shape, three, image, slot) * gates[rows, columns(2)]
            + value[slot : slot + 1] * gates[rows, columns(3)]
        )
    aggregated[...] = wide[...].astype(bf16)
    moves.leave(aggregated)
    modulator[...] = nn(aggregated[...], h_weight[...]) + small[H_BIAS : H_BIAS + 1, :]

    moves.leave(modulator)

    def mix(rows, carry):
        mixed[rows, :] = (query[rows, :] * modulator[rows, :]).astype(bf16)
        return carry

    blocks(shape, mix, 0)
    moves.leave(mixed)
    middle[...] = (
        inputs[...] + nn(mixed[...], proj_weight[...]) + small[PROJ_BIAS : PROJ_BIAS + 1, :]
    )
    moves.leave(middle)
    gain = small[LN2_GAIN : LN2_GAIN + 1, :]
    bias = small[LN2_BIAS : LN2_BIAS + 1, :]

    def second_norm(rows, carry):
        unit, _ = normalise(middle[rows, :])
        normed_two[rows, :] = (unit * gain + bias).astype(bf16)
        return carry

    blocks(shape, second_norm, 0)


class Moves:
    def __init__(self):
        self.incoming, self.outgoing = {}, {}
        self.started, self.free = [], []

    def copy(self, source, target):
        move = pltpu.make_async_copy(source, target, self.free.pop())
        move.start()
        self.started.append(move)

    def arrive(self, *buffers):
        for buffer in buffers:
            move = self.incoming.pop(id(buffer), None)
            if move is not None:
                move.wait()

    def leave(self, *buffers):
        for buffer in buffers:
            move = self.outgoing.pop(id(buffer), None)
            if move is not None:
                move.start()
                self.started.append(move)

    def finish(self):
        for move in list(self.incoming.values()):
            move.wait()
        for move in list(self.outgoing.values()):
            move.start()
            self.started.append(move)
        for move in self.started:
            move.wait()


def with_moves(kernel, far_in, far_out, extra):
    def run(*refs):
        refs = list(refs)
        ins, refs = refs[: len(far_in)], refs[len(far_in) :]
        outs, refs = refs[: len(far_out)], refs[len(far_out) :]
        semaphores = refs.pop()
        count = sum(far_in) + sum(far_out)
        buffers, scratch = refs[len(refs) - count :], refs[: len(refs) - count]
        moves = Moves()
        moves.free = [semaphores.at[count + spare] for spare in range(extra)]
        index = 0
        for group, flags, table in (
            (ins, far_in, moves.incoming),
            (outs, far_out, moves.outgoing),
        ):
            for place, far in enumerate(flags):
                if far:
                    buffer, outer = buffers[index], group[place]
                    pair = (outer, buffer) if group is ins else (buffer, outer)
                    move = pltpu.make_async_copy(*pair, semaphores.at[index])
                    if group is ins:
                        move.start()
                    table[id(buffer)] = move
                    group[place] = buffer
                    index += 1
        kernel(moves, *ins, *outs, *scratch)
        moves.finish()

    return run


class Units:
    def __init__(self, shards, unit):
        self.shards, self.unit = shards, unit
        self.piece_rows = 2 * unit + 16
        self.total = shards * unit
        self.head_rows, self.late_rows = 40, 16
        self.pieces = 2 * shards
        self.share = self.head_rows + self.late_rows
        self.head_total = 2 * self.pieces * self.head_rows
        self.late_total = 2 * self.pieces * self.late_rows


def sum_kernel(parts, source, out):
    size = out.shape[0]
    block = 16 if size % 16 == 0 else size

    def step(index, carry):
        rows = pl.ds(pl.multiple_of(index * block, block), block)
        total = source[0, rows, :].astype(f32)
        for part in range(1, parts):
            total = total + source[part, rows, :].astype(f32)
        out[rows, :] = total.astype(bf16)
        return carry

    lax.fori_loop(0, size // block, step, 0)


def pair_kernel(first, second, out):
    for part in range(out.shape[0]):
        total = first[part].astype(f32) + second[part].astype(f32)
        out[part] = total.astype(bf16)


def rows_kernel(shape, moves, first, second, arrived, first_out, second_out):
    def step(index, carry):
        rows = pl.ds(pl.multiple_of(index * 16, 16), 16)
        more = pl.ds(pl.multiple_of(index * 16 + shape.rows, 16), 16)
        first_out[rows, :] = (first[rows, :].astype(f32) + arrived[rows, :].astype(f32)).astype(bf16)
        second_out[rows, :] = (second[rows, :].astype(f32) + arrived[more, :].astype(f32)).astype(
            bf16
        )
        return carry

    lax.fori_loop(0, shape.rows // 16, step, 0)


def share_kernel(parts, out):
    total = parts[0].astype(f32)
    for part in range(1, parts.shape[0]):
        total = total + parts[part].astype(f32)
    share = total.astype(bf16)
    for copy in range(out.shape[0]):
        out[copy] = share


def piece_kernel(units, copies, spots, first, second, far_bias, out, own, bias, semaphores):
    unit = units.unit
    width = first.shape[1]
    rows = pl.ds(pl.multiple_of(spots[0] * unit, 16), unit)
    moves = [
        pltpu.make_async_copy(source.at[rows, :], own.at[index], semaphores.at[index])
        for index, source in enumerate((first, second))
    ]
    moves.insert(0, pltpu.make_async_copy(far_bias, bias, semaphores.at[2]))
    for move in moves:
        move.start()
    moves.pop(0).wait()
    shard = spots[1]
    values = bias[...].astype(f32).reshape(1, bias.shape[0])
    values = jnp.concatenate([values, jnp.zeros((1, width - bias.shape[0]), f32)], axis=1)
    values = pltpu.roll(jnp.broadcast_to(values, (8, width)), spots[2], 1)
    lane = lax.broadcasted_iota(jnp.int32, (8, width), 1) - shard * unit
    row = lax.broadcasted_iota(jnp.int32, (8, width), 0)
    values = jnp.where((lane >= 0) & (lane < unit) & (row == 0), values, 0.0)
    line = jnp.concatenate([values, jnp.zeros((8, width), f32)]).astype(bf16)
    for move in moves:
        move.wait()
    for copy in range(copies):
        base = copy * units.piece_rows
        out[base : base + unit, :] = own[0]
        out[base + unit : base + 2 * unit, :] = own[1]
        out[base + 2 * unit : base + units.piece_rows, :] = line


def feed_kernel(shape, units, resumed, moves, weights, *refs):
    refs = list(refs)

    def take(count):
        taken = refs[:count]
        del refs[:count]
        return taken

    groups = 1 if resumed is None else 2
    closing = resumed is not False
    normed, cots = take(groups), take(groups)
    if resumed:
        old_grads, old_bias, *near = take(6)
    if resumed:
        out, d_out, both = take(3)
        outs = [out, both.at[shape.rows : 2 * shape.rows, :]]
        d_outs = [d_out, both.at[0 : shape.rows, :]]
        d_near, out_near = take(2)
    else:
        outs, d_outs = take(groups), take(groups)
    grads = take(1)[0]
    if not closing:
        bias_grad = take(1)[0]
    first_weight, second_weight, total_grads, total_bias = take(4)
    unit, width = units.unit, shape.width
    bias = None
    for shard in range(units.shards):
        base, here = shard * units.piece_rows, shard * unit
        first_weight[here : here + unit, :] = weights[base : base + unit, :]
        second_weight[here : here + unit, :] = weights[base + unit : base + 2 * unit, :]
        term = weights[base + 2 * unit : base + units.piece_rows, :].astype(f32)
        bias = term if bias is None else bias + term
    bias = bias[0:1]
    if resumed:
        moves.arrive(*near)
        for target, own, arrived in ((d_near, near[0], near[1]), (out_near, near[2], near[3])):
            target[...] = own[...].astype(f32) + arrived[...].astype(f32)
            moves.leave(target)
    for group in range(groups):
        moves.arrive(normed[group], cots[group])
        rows, cot = normed[group], cots[group]
        value, rise = gelu_pair(nt(rows[...], first_weight[...]) + bias)
        hidden = value.astype(bf16)
        outs[group][...] = nn(hidden, second_weight[...]).astype(bf16)
        d_before = (nt(cot[...], second_weight[...]) * rise).astype(bf16)
        d_outs[group][...] = nn(d_before, first_weight[...]).astype(bf16)
        moves.leave(outs[group], d_outs[group])
        first, second = tn(d_before, rows[...]), tn(hidden, cot[...])
        line = fold(d_before.astype(f32))
        if group == 0 and not resumed:
            total_grads[0 : units.total, :] = first
            total_grads[units.total :, :] = second
            total_bias[...] = line
        elif group == 0:
            total_grads[0 : units.total, :] = old_grads[0 : units.total, :] + first
            total_grads[units.total :, :] = old_grads[units.total :, :] + second
            total_bias[...] = old_bias[...] + line
        else:
            total_grads[0 : units.total, :] += first
            total_grads[units.total :, :] += second
            total_bias[...] += line
    if not closing:
        grads[...] = total_grads[...]
        bias_grad[...] = total_bias[...]
        return
    row = jnp.concatenate([row_sum(total_bias[...]), jnp.zeros((15, width), f32)])
    for shard in range(units.shards):
        base, here = shard * units.piece_rows, shard * unit
        more = units.total + here
        grads[base : base + units.piece_rows, :] = jnp.concatenate(
            [total_grads[here : here + unit, :], total_grads[more : more + unit, :], row]
        ).astype(bf16)


def heads_kernel(
    shape,
    units,
    moves,
    core,
    small,
    cot,
    middle,
    d_near,
    d_far,
    proj_weight,
    query,
    modulator,
    h_weight,
    normed,
    aggregated,
    mixed,
    *refs,
):
    later, refs = refs[:8], refs[8:]
    d_middle, d_query, d_aggregated, own_rest, other_rest, *refs = refs
    fetched, refs = refs[:8], refs[8:]
    heads_body(
        shape,
        units,
        moves,
        core,
        small,
        cot,
        middle,
        d_near,
        d_far,
        proj_weight,
        query,
        modulator,
        h_weight,
        normed,
        aggregated,
        mixed,
        list(zip(later, fetched)),
        d_middle,
        d_query,
        d_aggregated,
        own_rest,
        other_rest,
        *refs,
    )


def heads_body(
    shape,
    units,
    moves,
    core,
    small,
    cot,
    middle,
    d_near,
    d_far,
    proj_weight,
    query,
    modulator,
    h_weight,
    normed,
    aggregated,
    mixed,
    later,
    d_middle,
    d_query,
    d_aggregated,
    own_rest,
    other_rest,
    d_mixed,
    d_modulator,
    head,
    d_branch,
):
    width = shape.width
    zero = jnp.zeros((8, width), f32)
    moves.arrive(small, cot, middle, d_near)
    for source, target in later:
        moves.copy(source, target)
    gain = small[LN2_GAIN : LN2_GAIN + 1, :]

    def second_norm(rows, carry):
        grads = d_near[rows, :] + d_far[rows, :].astype(f32)
        cots = cot[rows, :].astype(f32)
        d_input, d_gain = norm_back(middle[rows, :], grads, gain)
        d_total = cots + d_input
        d_middle[rows, :] = d_total
        rounded = d_total.astype(bf16)
        d_branch[rows, :] = rounded
        added = (d_gain, grads, rounded.astype(f32), cots)
        return tuple(total + fold(item) for total, item in zip(carry, added))

    d_gain, d_bias, proj_bias, out_bias = blocks(shape, second_norm, (zero,) * 4)
    moves.leave(d_middle)
    moves.arrive(proj_weight)
    d_mixed[...] = nt(d_branch[...], proj_weight[...])
    moves.arrive(query, modulator)

    def split(rows, carry):
        values = d_mixed[rows, :]
        for_query = (values * modulator[rows, :]).astype(bf16)
        for_modulator = (values * query[rows, :]).astype(bf16)
        d_query[rows, :] = for_query
        d_modulator[rows, :] = for_modulator
        return carry[0] + fold(for_query.astype(f32)), carry[1] + fold(for_modulator.astype(f32))

    query_bias, h_bias = blocks(shape, split, (zero, zero))
    moves.leave(d_query)
    moves.arrive(h_weight)
    d_aggregated[...] = nt(d_modulator[...], h_weight[...])
    moves.leave(d_aggregated)
    moves.arrive(normed, aggregated, mixed)
    head[0:width, :] = tn(d_query[...], normed[...])
    head[width : 2 * width, :] = tn(aggregated[...], d_modulator[...])
    head[2 * width : 3 * width, :] = tn(mixed[...], d_branch[...])
    sums = (h_bias, proj_bias, d_gain, d_bias, out_bias, query_bias)
    head[3 * width :, :] = jnp.concatenate(
        [row_sum(item) for item in sums]
        + [jnp.zeros((units.head_total - 3 * width - 6, width), f32)]
    )
    for half, target in enumerate((own_rest, other_rest)):
        absolute = jnp.bitwise_xor(core[0], half)
        for piece in range(units.pieces):
            first = (absolute * units.pieces + piece) * units.head_rows
            target[piece] = head[pl.ds(pl.multiple_of(first, 8), units.head_rows), :].astype(bf16)


def levels_back_kernel(
    shape,
    moves,
    small,
    gates,
    d_aggregated,
    pooled,
    slope_three,
    slope_two,
    slope_one,
    one,
    two,
    three,
    d_one,
    d_two,
    d_three,
    rounded,
    d_gates,
    tap_ref,
    d_levels,
    products,
    d_context,
):
    width = shape.width
    inner = shape.inner
    moves.arrive(small)
    spread_taps(shape, small, tap_ref)
    for ref in (d_one, d_two, d_three):
        clear_edges(shape, ref)
    moves.arrive(gates, d_aggregated, pooled)
    pool_grad = [None] * sublanes
    for image in range(shape.images):
        rows = pl.ds(image * shape.segment, shape.segment)
        for tile in range(shape.tiles):
            slot = tile * shape.images + image
            values = d_aggregated[rows, columns(tile)]
            for level in range(3):
                d_levels[pl.ds(level * inner + slot, shape.patches, stride=sublanes), :] = (
                    values[: shape.patches] * gates[rows, columns(level)][: shape.patches]
                )
            pool_grad[slot] = jnp.sum(values * gates[rows, columns(3)], axis=0, keepdims=True)
    blank = jnp.zeros((1, lanes), f32)
    pool_grad = jnp.concatenate([blank if item is None else item for item in pool_grad])
    pool_grad = pool_grad * pooled[sublanes : 2 * sublanes, :]
    wide_pool = jnp.concatenate([pool_grad] * shape.side)

    def third(line, carry):
        here = pl.multiple_of(line * shape.line, shape.line)
        value = (d_levels[pl.ds(2 * inner + here, shape.line), :] + wide_pool) * slope_three[
            pl.ds(here, shape.line), :
        ]
        d_three[pl.ds(here + shape.centre, shape.line), :] = value
        return carry

    moves.arrive(slope_three)
    lax.fori_loop(0, shape.side, third, 0)
    moves.leave(d_three)
    moves.arrive(slope_two, slope_one)
    for level, source, target, slope in ((2, d_three, d_two, slope_two), (1, d_two, d_one, slope_one)):

        def back(line, carry, level=level, source=source, target=target, slope=slope):
            here = pl.multiple_of(line * shape.line, shape.line)
            value = correlate(shape, source, tap_ref, level, line, True)
            value = (value + d_levels[pl.ds((level - 1) * inner + here, shape.line), :]) * slope[
                pl.ds(here, shape.line), :
            ]
            target[pl.ds(here + shape.centre, shape.line), :] = value
            return carry

        lax.fori_loop(0, shape.side, back, 0)
        moves.leave(target)

    def back_context(line, carry):
        here = pl.multiple_of(line * shape.line, shape.line)
        d_levels[pl.ds(here, shape.line), :] = correlate(shape, d_one, tap_ref, 0, line, True)
        return carry

    lax.fori_loop(0, shape.side, back_context, 0)
    for image, tile, slot in shape.places():
        first = image * shape.segment
        d_context[first : first + shape.patches, columns(tile)] = d_levels[
            pl.ds(slot, shape.patches, stride=sublanes), :
        ]
        if tile == 0 and shape.segment > shape.patches:
            d_context[first + shape.patches : first + shape.segment, :] = jnp.zeros(
                (shape.segment - shape.patches, width), f32
            )
    rounded[...] = d_context[...].astype(bf16)
    moves.leave(rounded)
    moves.arrive(one, two, three)
    for image in range(shape.images):
        rows = pl.ds(image * shape.segment, shape.segment)
        totals = [None] * 4
        for tile in range(shape.tiles):
            slot = tile * shape.images + image
            values = d_aggregated[rows, columns(tile)]
            for level, ref in enumerate((one, two, three)):
                term = values * level_rows(shape, ref, image, slot)
                totals[level] = term if tile == 0 else totals[level] + term
            term = values * pooled[slot : slot + 1, :]
            totals[3] = term if tile == 0 else totals[3] + term
        for gate in range(4):
            products[rows, columns(gate)] = totals[gate]
    chooser = (
        lax.broadcasted_iota(jnp.int32, (4 * lanes, lanes), 0) // lanes
        == lax.broadcasted_iota(jnp.int32, (4 * lanes, lanes), 1)
    ).astype(f32).astype(bf16)
    d_gates[...] = nn(products[...].astype(bf16), chooser).astype(bf16)


def exit_kernel(
    shape,
    units,
    moves,
    core,
    two,
    d_three,
    one,
    d_two,
    context,
    d_one,
    rounded,
    d_gates,
    small,
    normed,
    f_turned,
    d_query,
    tokens,
    d_inputs,
    own_late,
    other_late,
    packed,
    tap_grad,
    inputs,
    d_context,
    gathered,
    gate_rows,
):
    width = shape.width
    moves.arrive(two, d_three)
    tap_grads(shape, two, d_three, 2, tap_grad)
    moves.arrive(one, d_two)
    tap_grads(shape, one, d_two, 1, tap_grad)
    moves.arrive(context, d_one)
    tap_grads(shape, context, d_one, 0, tap_grad)
    moves.arrive(rounded, d_gates, small, normed, f_turned, d_query, tokens)
    gathered[0:width, :] = tn(rounded[...], normed[...])
    gathered[width : width + 8, :] = tn(d_gates[...], normed[...])[0:8]
    for tile in range(shape.tiles):
        total = None
        for image in range(shape.images):
            slot = tile * shape.images + image
            term = tap_grad[pl.ds(slot, taps, stride=sublanes), :]
            total = term if total is None else total + term
        gathered[width + 8 : width + 8 + taps, columns(tile)] = total
    gate_rows[...] = jnp.concatenate(
        [
            f_turned[2 * width : 2 * width + 4, :].astype(f32),
            jnp.zeros((lanes - 4, width), f32),
        ]
    ).astype(bf16)
    d_normed = d_context
    gate_bias = row_sum(fold(d_gates[...].astype(f32)))
    context_bias = row_sum(fold(rounded[...].astype(f32)))
    d_normed[...] = (
        nn(d_query[...], f_turned[0:width, :])
        + nn(rounded[...], f_turned[width : 2 * width, :])
        + nn(d_gates[...], gate_rows[...])
    )
    packed[...] = tokens[...].astype(f32)
    unpack(shape, packed, inputs)
    gain = small[LN1_GAIN : LN1_GAIN + 1, :]
    zero = jnp.zeros((8, width), f32)

    def finish(rows, carry):
        values = d_normed[rows, :]
        d_input, d_gain = norm_back(inputs[rows, :], values, gain)
        d_inputs[rows, :] = d_input
        return carry[0] + fold(d_gain), carry[1] + fold(values)

    d_gain, d_bias = blocks(shape, finish, (zero, zero))
    moves.leave(d_inputs)
    last = width + 8 + taps
    rest = units.late_total - last - 4
    gathered[last:, :] = jnp.concatenate(
        [
            row_sum(d_gain),
            row_sum(d_bias),
            context_bias,
            jnp.concatenate([gate_bias, jnp.zeros((1, width - lanes), f32)], axis=1),
            jnp.zeros((rest, width), f32),
        ]
    )
    for half, target in enumerate((own_late, other_late)):
        absolute = jnp.bitwise_xor(core[0], half)
        for place in range(2):
            for spot in range(units.shards):
                first = ((place * 2 + absolute) * units.shards + spot) * units.late_rows
                target[place * units.shards + spot] = gathered[
                    pl.ds(pl.multiple_of(first, 16), units.late_rows), :
                ].astype(bf16)


def finish_kernel(
    shape,
    moves,
    d_middle,
    d_inputs,
    small,
    middle,
    out_near,
    out_far,
    tokens_grad,
    block_out,
    rows_ref,
):
    moves.arrive(d_middle, d_inputs)

    def add_grads(rows, carry):
        rows_ref[rows, :] = d_middle[rows, :] + d_inputs[rows, :]
        return carry

    blocks(shape, add_grads, 0)
    pack(shape, rows_ref, tokens_grad)
    moves.leave(tokens_grad)
    moves.arrive(small, middle, out_near, out_far)

    def add_outs(rows, carry):
        total = middle[rows, :] + small[FC2_BIAS : FC2_BIAS + 1, :]
        rows_ref[rows, :] = total + out_near[rows, :] + out_far[rows, :].astype(f32)
        return carry

    blocks(shape, add_outs, 0)
    pack(shape, rows_ref, block_out)


def unpack_kernel(
    shape,
    units,
    spots,
    piece,
    piece_x,
    piece_core,
    piece_both,
    late_own,
    late_core,
    own,
    own_b,
    own_x,
    own_both,
    core_own,
    core_b,
    core_x,
    core_both,
    ln1_gain,
    ln1_bias,
    f_grad,
    f_bias,
    small_grad,
    middle_grad,
    large_grad,
    h_grad,
    h_bias,
    proj_grad,
    proj_bias,
    ln2_gain,
    ln2_bias,
    first_grad,
    first_bias,
    second_grad,
    second_bias,
    held,
    held_late,
    head,
    late,
):
    width = shape.width
    unit = units.unit
    size = own.shape[0]
    parts = (own, own_b, own_x, own_both, core_own, core_b, core_x, core_both)
    for index, part in enumerate(parts):
        held[index * size : (index + 1) * size, :] = part[...].astype(f32)
    late_size = late_own.shape[0]
    held_late[0:late_size, :] = late_own[...].astype(f32)
    held_late[late_size : 2 * late_size, :] = late_core[...].astype(f32)
    core, shift = spots[0], spots[2]
    far = units.shards // 2
    for half in range(2):
        late_base = jnp.bitwise_xor(core, half) * late_size
        for place in range(2):
            for close in range(2):
                slot = jnp.bitwise_xor(core, half) * 4 + jnp.bitwise_xor(spots[3], place) * 2
                base = (slot + jnp.bitwise_xor(spots[4], close)) * size
                for away in range(far):
                    here = base + jnp.bitwise_xor(spots[5], away) * units.head_rows
                    to = ((half * 2 + place) * far + away) * 2 + close
                    head[to * units.head_rows : (to + 1) * units.head_rows, :] = held[
                        pl.ds(pl.multiple_of(here, 8), units.head_rows), :
                    ]
                    here = late_base + ((place * far + away) * 2 + close) * units.late_rows
                    to = ((place * 2 + half) * far + away) * 2 + close
                    late[to * units.late_rows : (to + 1) * units.late_rows, :] = held_late[
                        pl.ds(pl.multiple_of(here, 8), units.late_rows), :
                    ]
    total = None
    lane = lax.broadcasted_iota(jnp.int32, (8, width), 1)
    for index, source in enumerate((piece, piece_core, piece_x, piece_both)):
        quarter = jnp.bitwise_xor(spots[1], index)
        to = pl.ds(pl.multiple_of(quarter * unit, 8), unit)
        first_grad[to, :] = source[0:unit, :].astype(f32)
        second_grad[to, :] = source[unit : 2 * unit, :].astype(f32)
        row = source[2 * unit : units.piece_rows, :].astype(f32)[0:8]
        moved = shift + quarter * unit
        moved = jnp.where(moved >= width, moved - width, moved)
        row = pltpu.roll(row, moved, 1)
        row = jnp.where((lane >= quarter * unit) & (lane < (quarter + 1) * unit), row, 0.0)
        total = row if total is None else total + row
    first_bias[...] = total[0:1, 0 : first_bias.shape[0]].reshape(first_bias.shape)
    f_grad[0:width, :] = head[0:width, :]
    f_grad[width : 2 * width + 4, :] = late[0 : width + 4, :]
    h_grad[...] = head[width : 2 * width, :]
    proj_grad[...] = head[2 * width : 3 * width, :]
    first = width + 8
    small_grad[...] = late[first : first + 9, :]
    middle_grad[...] = late[first + 9 : first + 34, :]
    large_grad[...] = late[first + 34 : first + taps, :]
    first = first + taps
    for out, source, row in (
        (h_bias, head, 3 * width),
        (proj_bias, head, 3 * width + 1),
        (ln2_gain, head, 3 * width + 2),
        (ln2_bias, head, 3 * width + 3),
        (second_bias, head, 3 * width + 4),
        (ln1_gain, late, first),
        (ln1_bias, late, first + 1),
    ):
        out[...] = source[row : row + 1, :].reshape(width)
    f_bias[0:width] = head[3 * width + 5 : 3 * width + 6, :].reshape(width)
    f_bias[width : 2 * width] = late[first + 2 : first + 3, :].reshape(width)
    f_bias[2 * width : 2 * width + 4] = late[first + 3 : first + 4, 0:4].reshape(4)


def call(kernel, name, outs, scratch, micros, room, *operands):
    spec = pl.BlockSpec(memory_space=pltpu.VMEM)
    outer = pl.BlockSpec(memory_space=pltpu.HBM)
    far_in = [isinstance(item, Far) for item in operands]
    far_out = [isinstance(item, Far) for item in outs]
    anywhere = [isinstance(item, Anywhere) for item in operands]
    raw = [isinstance(item, Raw) for item in operands]
    operands = [item.value if far else item for item, far in zip(operands, far_in)]
    operands = [
        pltpu.with_memory_space_constraint(item, pltpu.HBM) if far and not free else item
        for item, far, free in zip(operands, far_in, anywhere)
    ]
    raw_out = [isinstance(item, Raw) for item in outs]
    outs = [
        pltpu.HBM(item.value.shape, item.value.dtype) if far else item
        for item, far in zip(outs, far_out)
    ]
    specs = []
    for item, far, free in zip(operands, far_in, anywhere):
        if free:
            specs.append(pl.BlockSpec(memory_space=pl.ANY))
        elif item.dtype == jnp.int32:
            specs.append(pl.BlockSpec(memory_space=pltpu.SMEM))
        else:
            specs.append(outer if far else spec)
    out_specs = [outer if far else spec for far in far_out]
    if name not in plain:
        far_in = [far and not own for far, own in zip(far_in, raw)]
        far_out = [far and not own for far, own in zip(far_out, raw_out)]
        pairs = list(zip(operands, far_in)) + list(zip(outs, far_out))
        buffers = [pltpu.VMEM(item.shape, item.dtype) for item, far in pairs if far]
        extra = sum(raw) + sum(raw_out)
        semaphores = pltpu.SemaphoreType.DMA((max(len(buffers) + extra, 1),))
        scratch = list(scratch) + buffers + [semaphores]
        kernel = with_moves(kernel, far_in, far_out, extra)
    moved = sum(item.size * item.dtype.itemsize for item in operands)
    return pl.pallas_call(
        kernel,
        name=name,
        out_shape=outs,
        in_specs=specs,
        out_specs=out_specs,
        scratch_shapes=scratch,
        compiler_params=pltpu.CompilerParams(vmem_limit_bytes=room * 1024 * 1024),
        cost_estimate=pl.CostEstimate(
            flops=int(micros * 1.1e9), bytes_accessed=moved, transcendentals=0
        ),
    )(*operands)


plain = ("piece", "sum", "pair", "share", "unpack")


class Far:
    def __init__(self, value):
        self.value = value


class Anywhere(Far):
    pass


class Raw(Far):
    pass


def far_array(*dims, kind=jnp.float32):
    return Far(array(*dims, kind=kind))


def array(*dims, kind=jnp.float32):
    return jax.ShapeDtypeStruct(dims, kind)


def to_packed(values, shape):
    moved = with_layout_constraint(values.transpose(1, 2, 0, 3), Layout((0, 1, 2, 3)))
    moved = moved.reshape(shape.patches, shape.images, shape.tiles, lanes)
    moved = with_layout_constraint(moved, Layout((0, 2, 1, 3)))
    return moved.transpose(0, 2, 1, 3).reshape(shape.packed, lanes)


def from_packed(values, shape):
    moved = values.reshape(shape.patches, shape.tiles, shape.images, lanes).transpose(0, 2, 1, 3)
    moved = moved.reshape(shape.side, shape.side, shape.images, shape.width)
    return moved.transpose(2, 0, 1, 3)


everyone = ("x", "core", "a", "b")


def gather_plainly(units, first, bias, second):
    first = lax.all_gather(first, ("a", "b"), axis=0, tiled=True)
    second = lax.all_gather(second, ("a", "b"), axis=0, tiled=True)
    bias = lax.all_gather(bias, ("a", "b"), axis=0, tiled=True)
    width = first.shape[1]
    rows = jnp.pad(bias.reshape(4, 1, 1, width), ((0, 0), (0, units.shards - 1), (0, 15), (0, 0)))
    shape = (4, units.shards, units.unit, width)
    both = jnp.concatenate([first.reshape(shape), second.reshape(shape), rows], axis=2)
    both = both.reshape(4, units.shards * units.piece_rows, width)
    return [both[index] for index in range(4)]


def total_of(values, parts):
    rows = values.shape[0] // parts
    kernel = functools.partial(sum_kernel, parts)
    values = values.reshape(parts, rows, values.shape[1])
    return call(kernel, "sum", [array(rows, values.shape[2], kind=bf16)], [], 1, 4, values)[0]


def reduce_plainly(shape, units, feed, rest, late):
    width = shape.width
    unit = units.unit
    both = jnp.stack(feed).reshape(4, units.shards, units.piece_rows, width)
    first = both[:, :, :unit].reshape(4 * units.total, width)
    second = both[:, :, unit : 2 * unit].reshape(4 * units.total, width)
    bias = both[:, 0, 2 * unit].reshape(4 * units.total, 1)

    def shared(values):
        part = lax.psum_scatter(values, ("a", "b"), scatter_dimension=0, tiled=True)
        return lax.psum(part, ("x", "core")).astype(f32)

    late = jnp.stack(late).reshape(2, 2, units.shards, units.late_rows, width)
    late = late.transpose(1, 0, 2, 3, 4).reshape(units.late_total, width)
    late = lax.psum(late, everyone).astype(f32)
    head = jnp.concatenate(rest).reshape(units.head_total, width)
    head = lax.psum(head, everyone).astype(f32)
    last = width + 8
    vectors = head[3 * width : 3 * width + 8]
    more = late[last + taps : last + taps + 4]
    return (
        more[0],
        more[1],
        jnp.concatenate([head[:width], late[: width + 4]]),
        jnp.concatenate([vectors[5], more[2], more[3, :4]]),
        late[last : last + 9],
        late[last + 9 : last + 34],
        late[last + 34 : last + taps],
        head[width : 2 * width],
        vectors[0],
        head[2 * width : 3 * width],
        vectors[1],
        vectors[2],
        vectors[3],
        shared(first),
        shared(bias)[:, 0],
        shared(second),
        vectors[4],
    )


def shards(
    sizes,
    tokens,
    ln1_gain,
    ln1_bias,
    f_weight,
    f_bias,
    dw_small,
    dw_middle,
    dw_large,
    h_weight,
    h_bias,
    proj_weight,
    proj_bias,
    ln2_gain,
    ln2_bias,
    fc1_weight,
    fc1_bias,
    fc2_weight,
    fc2_bias,
    out_grad,
):
    images, side, _, width = tokens.shape
    shape = Shape(images, side, width)
    rows, grid, inner = shape.rows, shape.grid, shape.inner
    hidden = fc1_weight.shape[1] * sizes["a"] * sizes["b"]
    quick = sizes["x"] == 2 and sizes["a"] * sizes["b"] == 8
    units = Units(8, hidden // 32)
    f_turned = f_weight.T
    first, second = fc1_weight.T, fc2_weight
    scratch = pltpu.VMEM
    core = jnp.zeros((1,), jnp.int32)
    if quick:
        core = lax.axis_index("core").astype(jnp.int32).reshape(1)
        quarter = lax.axis_index("x") * 2 + core[0]
        shard = lax.axis_index("a") * 2 + lax.axis_index("b")
        turn = lax.rem(shard - quarter + units.shards, units.shards) * units.unit
        spots = jnp.stack([quarter, shard, turn]).astype(jnp.int32)
        (pieces,) = call(
            functools.partial(piece_kernel, units, units.shards),
            "piece",
            [array(units.shards * units.piece_rows, width, kind=bf16)],
            [
                scratch((2, units.unit, width), bf16),
                scratch(fc1_bias.shape, bf16),
                pltpu.SemaphoreType.DMA((3,)),
            ],
            1,
            6,
            spots,
            Far(first),
            Far(second),
            Far(fc1_bias),
        )
        weights = exchange(pieces, ("a", "b"))
    tokens_packed = to_packed(tokens, shape)

    def rows_array(kind=bf16):
        return far_array(rows, width, kind=kind)

    small, cot, inputs, normed, query, gates, context, one, slope_one = call(
        functools.partial(entry_kernel, shape),
        "entry",
        [
            far_array(96, width),
            rows_array(),
            array(rows, width),
            rows_array(),
            array(rows, width),
            array(rows, 4 * lanes),
            far_array(grid, lanes),
            array(grid, lanes),
            far_array(inner, lanes),
        ],
        [
            scratch((taps * sublanes, lanes), f32),
            scratch((shape.packed, lanes), f32),
            scratch((rows, width), f32),
        ],
        5,
        16,
        Far(tokens_packed),
        Far(f_turned),
        Far(to_packed(out_grad, shape)),
        dw_small,
        dw_middle,
        dw_large,
        ln1_gain,
        ln1_bias,
        f_bias,
        h_bias,
        proj_bias,
        ln2_gain,
        ln2_bias,
        fc2_bias,
    )
    if quick:
        cot_far = flip(cot, "x")
        cot_core = flip(cot)
    one, gates, query, *results = call(
        functools.partial(modulation_kernel, shape),
        "modulation",
        [
            Raw(array(grid, lanes)),
            Raw(array(rows, 4 * lanes)),
            Raw(array(rows, width)),
            rows_array(f32),
            rows_array(),
            rows_array(),
            rows_array(f32),
            rows_array(),
            far_array(grid, lanes),
            far_array(grid, lanes),
            far_array(inner, lanes),
            far_array(inner, lanes),
            far_array(2 * sublanes, lanes),
        ],
        [scratch((rows, width), f32), scratch((taps * sublanes, lanes), f32)],
        8,
        20,
        one,
        Far(small),
        gates,
        Far(h_weight),
        query,
        inputs,
        Far(proj_weight),
    )
    modulator, aggregated, mixed, middle, normed_two, *results = results
    two, three, slope_two, slope_three, pooled = results

    def feed(resumed, outs, *operands):
        return call(
            functools.partial(feed_kernel, shape, units, resumed),
            "feed",
            outs,
            [
                scratch((units.total, width), bf16),
                scratch((units.total, width), bf16),
                scratch((2 * units.total, width), f32),
                scratch((8, width), f32),
            ],
            6,
            24,
            *operands,
        )

    near_rows = array(rows, width, kind=bf16)
    feed_total = array(units.shards * units.piece_rows, width, kind=bf16)
    if quick:
        cot_both = flip(after(cot_far, middle))
        normed_far = flip(normed_two, "x")
        normed_core = flip(normed_two)
        out_own, out_core, d_own, d_core, *carry = feed(
            False,
            [near_rows] * 4 + [array(2 * units.total, width), array(8, width)],
            weights,
            Far(normed_two),
            normed_core,
            Far(cot),
            cot_core,
        )
        out_core, d_core = flip(out_core), flip(d_core)
        normed_far = after(normed_far, d_own)
        normed_both = flip(normed_far)
        out_far, d_far, both, d_near, out_near, feed_grads = feed(
            True,
            [near_rows] * 2
            + [array(2 * rows, width, kind=bf16), rows_array(f32), rows_array(f32), feed_total],
            weights,
            normed_far,
            normed_both,
            cot_far,
            cot_both,
            *carry,
            d_own,
            d_core,
            out_own,
            out_core,
        )
        arrived = flip(both)
        d_far, out_far = call(
            functools.partial(rows_kernel, shape),
            "rows",
            [near_rows, rows_array()],
            [],
            1,
            8,
            d_far,
            out_far,
            arrived,
        )
        feed_grads = after(feed_grads, d_far)
        d_far = flip(d_far, "x")
        feed_parts = exchange(feed_grads, ("a", "b"))
    else:
        out_far = d_far = jnp.zeros((rows, width), bf16)
        out_near, d_near, feed_grads = jnp.zeros((rows, width), f32), 0.0, []
        for weights in gather_plainly(units, first, fc1_bias, second):
            out, d_out, grads = feed(
                None, [near_rows, near_rows, feed_total], weights, normed_two, cot
            )
            out_near, d_near = out_near + out.astype(f32), d_near + d_out.astype(f32)
            feed_grads.append(grads)
    rest = array(units.pieces, units.head_rows, width, kind=bf16)
    later = [gates, pooled, slope_three, slope_two, slope_one, one, two, three]
    d_middle, d_query, d_aggregated, own_rest, other_rest, *fetched = call(
        functools.partial(heads_kernel, shape, units),
        "heads",
        [rows_array(f32), rows_array(), array(rows, width), rest, rest]
        + [array(*item.shape) for item in later],
        [
            scratch((rows, width), f32),
            scratch((rows, width), bf16),
            scratch((units.head_total, width), f32),
            scratch((rows, width), bf16),
        ],
        5,
        16,
        core,
        Far(small),
        Far(cot),
        Far(middle),
        Far(d_near),
        d_far,
        Far(proj_weight),
        Far(query),
        Far(modulator),
        Far(h_weight),
        Far(normed),
        Far(aggregated),
        Far(mixed),
        *[Raw(item) for item in later],
    )
    if quick:
        out_far = flip(after(out_far, d_middle), "x")
        rest_arrived = flip(other_rest)
    d_one, d_two, d_three, rounded, d_gates = call(
        functools.partial(levels_back_kernel, shape),
        "levels_back",
        [
            far_array(grid, lanes),
            far_array(grid, lanes),
            far_array(grid, lanes),
            rows_array(),
            far_array(rows, lanes, kind=bf16),
        ],
        [
            scratch((taps * sublanes, lanes), f32),
            scratch((3 * inner, lanes), f32),
            scratch((rows, 4 * lanes), f32),
            scratch((rows, width), f32),
        ],
        8,
        24,
        Far(small),
        fetched[0],
        d_aggregated,
        *fetched[1:],
    )
    if quick:
        (rest_half,) = call(pair_kernel, "pair", [rest], [], 1, 4, own_rest, rest_arrived)
        feed_parts = after(feed_parts, d_one)
        piece = total_of(feed_parts, units.shards)
        rest_half = after(rest_half, piece)
        d_one = after(d_one, rest_half, out_far)
        shares = rest_half.shape
        rest_parts = exchange(rest_half.reshape(-1, width), ("x", "a", "b")).reshape(shares)
    late = array(units.pieces, units.late_rows, width, kind=bf16)
    d_inputs, own_late, other_late = call(
        functools.partial(exit_kernel, shape, units),
        "exit",
        [rows_array(f32), late, late],
        [
            scratch((shape.packed, lanes), f32),
            scratch((taps * sublanes, lanes), f32),
            scratch((rows, width), f32),
            scratch((rows, width), f32),
            scratch((units.late_total, width), f32),
            scratch((lanes, width), bf16),
        ],
        9,
        24,
        core,
        Far(two),
        Far(d_three),
        Far(one),
        Far(d_two),
        Far(context),
        Far(d_one),
        Far(rounded),
        Far(d_gates),
        Far(small),
        Far(normed),
        Far(f_turned),
        Far(d_query),
        Far(tokens_packed),
    )
    if quick:
        late_arrived = flip(other_late)
        piece_x = flip(piece, "x")
        piece_core, piece_both = flip(piece), flip(piece_x)
        rest_parts = after(rest_parts, own_late)
        head_sum = total_of(rest_parts.reshape(-1, width), units.pieces)
        (late_half,) = call(pair_kernel, "pair", [late], [], 1, 4, own_late, late_arrived)
        late_half = after(late_half, head_sum)
        shares = late_half.shape
        late_parts = exchange(late_half.reshape(-1, width), ("x", "a", "b")).reshape(shares)
        d_inputs = after(d_inputs, late_half)
    tokens_grad, block_out = call(
        functools.partial(finish_kernel, shape),
        "finish",
        [far_array(shape.packed, lanes), far_array(shape.packed, lanes)],
        [scratch((rows, width), f32)],
        3,
        16,
        Far(d_middle),
        Far(d_inputs),
        Far(small),
        Far(middle),
        Far(out_near),
        Anywhere(out_far),
    )
    if quick:
        steps = [flip(head_sum, "a", sizes["a"], bit) for bit in range(1, sizes["a"])]
        own = jnp.concatenate([head_sum] + steps)
        held_b, held_x = flip(own, "b"), flip(own, "x")
        held_both = flip(held_b, "x")
        held = [own, held_b, held_x, held_both]
        late_parts = after(late_parts, tokens_grad)
        (share,) = call(
            share_kernel,
            "share",
            [array(units.pieces, units.late_rows, width, kind=bf16)],
            [],
            1,
            6,
            late_parts,
        )
        share = after(share, piece_core, piece_both, held_both)
        late_own = exchange(share.reshape(-1, width), ("x", "a", "b"))
        held = [late_own, flip(late_own)] + held + [flip(item) for item in held]
        turn = lax.rem(units.shards - shard, units.shards) * units.unit
        spots = [core[0], quarter, turn] + [lax.axis_index(axis) for axis in ("x", "b", "a")]
        spots = jnp.stack(spots).astype(jnp.int32)
        total = 4 * units.unit
        others = call(
            functools.partial(unpack_kernel, shape, units),
            "unpack",
            [
                array(width),
                array(width),
                array(2 * width + 4, width),
                array(2 * width + 4),
                array(9, width),
                array(25, width),
                array(49, width),
                array(width, width),
                array(width),
                array(width, width),
                array(width),
                array(width),
                array(width),
                array(total, width),
                array(total),
                array(total, width),
                array(width),
            ],
            [
                scratch((units.head_total, width), f32),
                scratch((units.late_total, width), f32),
                scratch((units.head_total, width), f32),
                scratch((units.late_total, width), f32),
            ],
            2,
            16,
            spots,
            piece,
            piece_x,
            piece_core,
            piece_both,
            *held,
        )
    else:
        others = reduce_plainly(
            shape, units, feed_grads, (own_rest, other_rest), (own_late, other_late)
        )
    others = list(others)
    others[2] = others[2].T
    others[13] = others[13].T
    return from_packed(block_out, shape), from_packed(tokens_grad, shape), *others


def solution(mesh):
    img, mlp = mesh.shape["img"], mesh.shape["mlp"]
    sizes = {"x": img // 2, "core": 2, "a": mlp // 2, "b": 2}
    finer = Mesh(mesh.devices.reshape(*sizes.values()), everyone)
    images = P(everyone, None, None, None)
    hidden = ("a", "b")
    return jax.shard_map(
        functools.partial(shards, sizes),
        mesh=finer,
        in_specs=(images,)
        + (P(),) * 13
        + (P(None, hidden), P(hidden), P(hidden, None), P(), images),
        out_specs=(images, images)
        + (P(),) * 13
        + (P(None, hidden), P(hidden), P(hidden, None), P()),
        check_vma=False,
    )
```

time: 597 us -> 133 us (0.22); the launches traced: 587 us -> 132 us
  waiting for transfers between devices: 334 us -> 28.2 us
  matrix products: 79.4 us -> 0 us
  local copies, waits for them, and re-layouts: 62 us -> 0.16 us
  Pallas kernels: 0 us -> 57.4 us
  blocking collectives: 48.6 us -> 0 us
  other arithmetic: 45.5 us -> 0.09 us
  starting transfers between devices: 0.66 us -> 45.3 us
  between operations: 17.3 us -> 1.19 us
    psum x3 -> x0, waiting for transfers between devices: 258 us -> none  [the longest x2 258 us: shards(): lax.psum((ln1_gain_local, ln1_bias_local, f_weight_local, f_bias_local, s...]
    reduce_scatter x2 -> x0, waiting for transfers between devices: 74.3 us -> none  [the longest x1 66.3 us: shards(): lax.psum_scatter(inner_rows(hidden, cotangent).astype(jnp.bfloat16), 'mlp...]
    pallas_call x0 -> x16, Pallas kernels: none -> 57.4 us  [call(): pl.pallas_call(kernel, name=name, out_shape=outs, in_specs=specs, out_spe...]
    unnamed x2 -> x0, blocking collectives: 43 us -> none
    conv_general_dilated x9 -> x0, matrix products: 42.5 us -> none  [depthwise(): lax.conv_general_dilated(values, filters, (1, 1), 'SAME', dimension_numbe...]
    dot_general x15 -> x0, matrix products: 36.9 us -> none  [the longest x5 18.5 us: outer_cols(): lax.dot_general(left, right, (((1,), (1,)), ((), ())), preferred_element_...]
    all_to_all x0 -> x5, starting transfers between devices: none -> 28.7 us  [exchange(): return lax.all_to_all(values, axes, split_axis=0, concat_axis=0, tiled=True)]
    unnamed x236 -> x24, local copies, waits for them, and re-layouts: 21 us -> 0.07 us
  transfers between devices with their start and end apart: 7 -> 32, of which waited for: 4 -> 18; matrix products, arithmetic and copies ran while one was open for 26% -> 0% of each run, Pallas kernels for 0% -> 35%
where the time goes in v1:
time: 133 us; the launch traced here: 132 us
  Pallas kernels  57.4 us (43%)
  starting transfers between devices  45.3 us (34%)
  waiting for transfers between devices  28.2 us (21%)
    pallas_call x16, Pallas kernels, call(): pl.pallas_call(kernel, name=name, out_shape=outs, in_specs=specs, out_spe...  57.4 us
    all_to_all x5, starting transfers between devices, exchange(): return lax.all_to_all(values, axes, split_axis=0, concat_axis=0, tiled=True)  28.7 us
    ppermute x27, starting transfers between devices, flip(): lax.ppermute(values, axis, [(place, place ^ bit) for place in range(size)])  16.7 us
    all_to_all x5, waiting for transfers between devices, exchange(): return lax.all_to_all(values, axes, split_axis=0, concat_axis=0, tiled=True)  14.9 us
    ppermute x27, waiting for transfers between devices, flip(): lax.ppermute(values, axis, [(place, place ^ bit) for place in range(size)])  13.3 us
  transfers between devices with their start and end apart: 32, of which 18 were waited for; matrix products, arithmetic and copies ran while one was open for 0% of the time, Pallas kernels for 35%

profile of v1, /device:TPU:0, one launch (start us, length us, event | category | flops | bytes accessed | tf_op | source)
XLA Modules:
  0.0 132.3 jit_solution(12274646482896551676)
XLA Ops:
  0.7 2.3 %piece.1 = bf16[896,384]{1,0:T(8,128)(2,1)} custom-call(s32[3]{0:T(128)S(1)} %pad_add_fusion.spots, bf16[192,384]{1,0:T(8,128)(2,1)} %bitcast.55, bf16[192,384]{1,0:T(8,128)(2,1)} %second.1, bf16[192]{0:T(256)(128)(2,1)} %far_bias.1), custom_call_target="tpu_custom_call" | custom-call | flops 1100000000 | bytes 295308 | tf_op jit(solution)/shard_map/piece/pallas_call | solution.py:1134
  3.2 7.4 %all-to-all-start = ((bf16[8,112,384]{2,1,0:T(8,128)(2,1)}), bf16[8,112,384]{2,1,0:T(8,128)(2,1)S(1)}, u32[]{:S(2)}, u32[]{:S(2)}) async-start(bf16[8,112,384]{2,1,0:T(8,128)(2,1)} %bitcast.14), calls=%async_computation | async-start | bytes 1376256 | tf_op jit(solution)/shard_map/all_to_all | solution.py:31
  10.7 4.9 %entry.1 = (f32[96,384]{1,0:T(8,128)}, bf16[400,384]{1,0:T(8,128)(2,1)}, f32[400,384]{1,0:T(8,128)S(1)}, bf16[400,384]{1,0:T(8,128)(2,1)}, f32[400,384]{1,0:T(8,...) custom-call(bf16[1176,128]{1,0:T(8,128)(2,1)} %bitcast.53, ...), custom_call_target="tpu_custom_call" | custom-call | flops 5500000256 | bytes 1265672 | tf_op jit(solution)/shard_map/entry/pallas_call | solution.py:1134
  15.6 1.6 %collective-permute-start.4 = (bf16[400,384]{1,0:T(8,128)(2,1)}, bf16[400,384]{1,0:T(8,128)(2,1)S(1)}, u32[]{:S(2)}, u32[]{:S(2)}) collective-permute-start(bf16[400,384]{1,0:T(8,128)(2,1)} %get-tuple-element.108.refs_3_.refs_2_), channel_id=1, source_target_pairs={{0,16},{16,0},{1,17},{17,1},{2,18},{18,2},{3,19},{19,3},{4,20},{20... | collective-permute-start | bytes 921608 | tf_op jit(solution)/shard_map/ppermute | solution.py:27
  17.2 8.9 %modulation.1 = (f32[2240,128]{1,0:T(8,128)}, f32[400,512]{1,0:T(8,128)}, f32[400,384]{1,0:T(8,128)}, f32[400,384]{1,0:T(8,128)}, bf16[400,384]{1,0:T(8,128)(2,1...) custom-call(f32[2240,128]{1,0:T(8,128)S(1)} %get-tuple-element.109.r, ...), custom_call_target="tpu_custom_call" | custom-call | flops 8800000000 | bytes 3932160 | tf_op jit(solution)/shard_map/modulation/pallas_call | solution.py:1134
  28.6 4.1 %feed.2 = (bf16[400,384]{1,0:T(8,128)(2,1)S(1)}, bf16[400,384]{1,0:T(8,128)(2,1)S(1)}, bf16[400,384]{1,0:T(8,128)(2,1)S(1)}, bf16[400,384]{1,0:T(8,128)(2,1)S(1)...) custom-call(bf16[896,384]{1,0:T(8,128)(2,1)S(1)} %bitcast.46, bf16[400,384]{1,0:T(8,128)(2,1)} %get-tuple-element.114.refs_1_, ...), custom_call_target="tpu_custom_call" | custom-call | flops 6600000000 | bytes 1916928 | tf_op jit(solution)/shard_map/feed/pallas_call | solution.py:1134
  32.7 3.4 %collective-permute-done.refs_1_ = bf16[400,384]{1,0:T(8,128)(2,1)S(1)} collective-permute-done((bf16[400,384]{1,0:T(8,128)(2,1)}, bf16[400,384]{1,0:T(8,128)(2,1)S(1)}, u32[]{:S(2)}, u32[]{:S(2)}) %collective-permute-start) | collective-permute-done | bytes 307232 | tf_op jit(solution)/shard_map/ppermute | solution.py:27
  36.6 1.1 collective-permute-done.3.refs_2_
  38.6 5.1 %feed.3 = (bf16[400,384]{1,0:T(8,128)(2,1)S(1)}, bf16[400,384]{1,0:T(8,128)(2,1)S(1)}, bf16[800,384]{1,0:T(8,128)(2,1)S(1)}, f32[400,384]{1,0:T(8,128)}, f32[400,384]{1,0:T(8,128)}, /*index=5*/bf16[896,384]{1,0:T(8,128)(2,1)}) custom-call(bf16[896,384]{1,0:T(8,128)(2,1)S(1)} %bitcast.47, bf16[400,384]{1,0:T(8,128)(2,1)S(1)} %collective-permute-done.refs_1_, ...), custom_call_target="tpu_custom_call" | custom-call | flops 6600000000 | bytes 4337664 | tf_op jit(solution)/shard_map/feed/pallas_call | solution.py:1134
  43.8 1.9 %collective-permute-done.8.refs_2_ = bf16[800,384]{1,0:T(8,128)(2,1)S(1)} collective-permute-done((bf16[800,384]{1,0:T(8,128)(2,1)S(1)}, bf16[800,384]{1,0:T(8,128)(2,1)S(1)}, u32[]{:S(2)}, u32[]{:S(2)}) %collective-permute-start.8) | collective-permute-done | bytes 614432 | tf_op jit(solution)/shard_map/ppermute | solution.py:27
  45.8 1.0 rows.1
  47.4 6.0 %all-to-all-start.1 = ((bf16[8,112,384]{2,1,0:T(8,128)(2,1)}), bf16[8,112,384]{2,1,0:T(8,128)(2,1)S(1)}, u32[]{:S(2)}, u32[]{:S(2)}) async-start(bf16[8,112,384]{2,1,0:T(8,128)(2,1)} %bitcast.16), calls=%async_computation.1 | async-start | bytes 1376256 | tf_op jit(solution)/shard_map/all_to_all | solution.py:31
  53.4 2.8 %collective-permute-done.9.refs_5_ = bf16[400,384]{1,0:T(8,128)(2,1)S(1)} collective-permute-done((bf16[400,384]{1,0:T(8,128)(2,1)S(1)}, bf16[400,384]{1,0:T(8,128)(2,1)S(1)}, u32[]{:S(2)}, u32[]{:S(2)}) %collective-permute-start.9) | collective-permute-done | bytes 307232 | tf_op jit(solution)/shard_map/ppermute | solution.py:27
  56.2 5.1 %heads.1 = (f32[400,384]{1,0:T(8,128)}, bf16[400,384]{1,0:T(8,128)(2,1)}, f32[400,384]{1,0:T(8,128)S(1)}, bf16[16,40,384]{2,1,0:T(8,128)(2,1)S(1)}, bf16[16,40,3...) custom-call(s32[1]{0:T(128)} %bitcast.refs_0_, ...), custom_call_target="tpu_custom_call" | custom-call | flops 5500000256 | bytes 11407364 | tf_op jit(solution)/shard_map/heads/pallas_call | solution.py:1134
  61.9 7.7 %levels_back.1 = (f32[2240,128]{1,0:T(8,128)}, f32[2240,128]{1,0:T(8,128)}, f32[2240,128]{1,0:T(8,128)}, bf16[400,384]{1,0:T(8,128)(2,1)}, bf16[400,128]{1,0:T(8,128)(2,1)}) custom-call(f32[96,384]{1,0:T(8,128)} %get-tuple-element.107.refs_1_.refs_0_.refs_9_.refs_2_, f32[400,512]{1,0:T(8,128)S(1)} %get-tuple-element.142.refs_1_, ...), custom_call_target="tpu_custom_call" | custom-call | flops 8800000000 | bytes 7438336 | tf_op jit(solution)/shard_map/levels_back/pallas_call | solution.py:1134
  69.6 0.9 pair.2
  70.5 0.9 all-to-all-done.1
  71.5 6.1 %all-to-all-start.2 = ((bf16[16,40,384]{2,1,0:T(8,128)(2,1)}), bf16[16,40,384]{2,1,0:T(8,128)(2,1)S(1)}, u32[]{:S(2)}, u32[]{:S(2)}) async-start(bf16[16,40,384]{2,1,0:T(8,128)(2,1)} %pair.2), calls=%async_computation.2 | async-start | bytes 983040 | tf_op jit(solution)/shard_map/all_to_all | solution.py:31
  77.7 10.6 %exit.1 = (f32[400,384]{1,0:T(8,128)}, bf16[16,16,384]{2,1,0:T(8,128)(2,1)S(1)}, bf16[16,16,384]{2,1,0:T(8,128)(2,1)S(1)}) custom-call(s32[1]{0:T(128)} %bitcast.refs_0_, f32[2240,128]{1,0:T(8,128)} %get-tuple-element.139.refs_19_.refs_1_, f32[2240,128]{1,0:T(8,128)} %get-tuple-element.151.refs_2_, f32[2240,128]{1,0:T(8,128)} %get-tuple-element.138.refs_18_.refs_3_, ...), custom_call_target="tpu_custom_call" | custom-call | flops 9900000256 | bytes 8946692 | tf_op jit(solution)/shard_map/exit/pallas_call | solution.py:1134
  88.6 4.2 %all-to-all-done.2.source = bf16[16,40,384]{2,1,0:T(8,128)(2,1)S(1)} async-done(((bf16[16,40,384]{2,1,0:T(8,128)(2,1)}), bf16[16,40,384]{2,1,0:T(8,128)(2,1)S(1)}, u32[]{:S(2)}, u32[]{:S(2)}) %all-to-all-start.2) | async-done | bytes 491552 | tf_op jit(solution)/shard_map/all_to_all | solution.py:31
  92.8 2.0 %collective-permute-start.18 = (bf16[40,384]{1,0:T(8,128)(2,1)S(1)}, bf16[40,384]{1,0:T(8,128)(2,1)S(1)}, u32[]{:S(2)}, u32[]{:S(2)}) collective-permute-start(bf16[40,384]{1,0:T(8,128)(2,1)S(1)} %sum.3), channel_id=1, source_target_pairs={{0,6},{2,4},{4,2},{6,0},{1,7},{3,5},{5,3},{7,1},{8,14},{10,12},{12... | collective-permute-start | bytes 92168 | tf_op jit(solution)/shard_map/ppermute | solution.py:27
  95.4 1.9 %collective-permute-start.16 = (bf16[40,384]{1,0:T(8,128)(2,1)S(1)}, bf16[40,384]{1,0:T(8,128)(2,1)S(1)}, u32[]{:S(2)}, u32[]{:S(2)}) collective-permute-start(bf16[40,384]{1,0:T(8,128)(2,1)S(1)} %sum.3), channel_id=1, source_target_pairs={{0,2},{2,0},{4,6},{6,4},{1,3},{3,1},{5,7},{7,5},{8,10},{10,8},{12,... | collective-permute-start | bytes 92168 | tf_op jit(solution)/shard_map/ppermute | solution.py:27
  97.3 1.3 collective-permute-start.13
  98.7 1.0 collective-permute-done.17
  101.0 4.9 %all-to-all-start.3 = ((bf16[16,16,384]{2,1,0:T(8,128)(2,1)}), bf16[16,16,384]{2,1,0:T(8,128)(2,1)S(1)}, u32[]{:S(2)}, u32[]{:S(2)}) async-start(bf16[16,16,384]{2,1,0:T(8,128)(2,1)} %pair.3), calls=%async_computation.3 | async-start | bytes 393216 | tf_op jit(solution)/shard_map/all_to_all | solution.py:31
  106.5 1.9 %collective-permute-start.20 = (bf16[160,384]{1,0:T(8,128)(2,1)S(1)}, bf16[160,384]{1,0:T(8,128)(2,1)S(1)}, u32[]{:S(2)}, u32[]{:S(2)}) collective-permute-start(bf16[160,384]{1,0:T(8,128)(2,1)S(1)} %collective-permute-done.19.own_b), channel_id=1, source_target_pairs={{0,16},{16,0},{1,17},{17,1},{2,18},{18,2},{3,19},{19,3},{4,20},{20... | collective-permute-start | bytes 368648 | tf_op jit(solution)/shard_map/ppermute | solution.py:27
  108.4 2.7 %finish.1 = (f32[1176,128]{1,0:T(8,128)}, f32[1176,128]{1,0:T(8,128)}) custom-call(f32[400,384]{1,0:T(8,128)} %get-tuple-element.141.refs_0_, f32[400,384]{1,0:T(8,128)} %get-tuple-element.172.refs_1_, f32[96,384]{1,0:T(8,128)} %get-tuple-element.107.refs_1_.refs_0_.refs_9_.refs_2_, f32[400,384]{1,0:T(8,128)} %get-tuple-element.113.refs_3_, ...), custom_call_target="tpu_custom_call" | custom-call | flops 3300000000 | bytes 2912256 | tf_op jit(solution)/shard_map/finish/pallas_call | solution.py:1134
  111.1 3.0 %all-to-all-done.3.parts = bf16[16,16,384]{2,1,0:T(8,128)(2,1)S(1)} async-done(((bf16[16,16,384]{2,1,0:T(8,128)(2,1)}), bf16[16,16,384]{2,1,0:T(8,128)(2,1)S(1)}, u32[]{:S(2)}, u32[]{:S(2)}) %all-to-all-start.3) | async-done | bytes 196640 | tf_op jit(solution)/shard_map/all_to_all | solution.py:31
  114.8 4.2 %all-to-all-start.4 = ((bf16[16,16,384]{2,1,0:T(8,128)(2,1)}), bf16[16,16,384]{2,1,0:T(8,128)(2,1)S(1)}, u32[]{:S(2)}, u32[]{:S(2)}) async-start(bf16[16,16,384]{2,1,0:T(8,128)(2,1)} %share.1), calls=%async_computation.4 | async-start | bytes 393216 | tf_op jit(solution)/shard_map/all_to_all | solution.py:31
  119.1 1.9 %collective-permute-start.22 = (bf16[160,384]{1,0:T(8,128)(2,1)S(1)}, bf16[160,384]{1,0:T(8,128)(2,1)S(1)}, u32[]{:S(2)}, u32[]{:S(2)}) collective-permute-start(bf16[160,384]{1,0:T(8,128)(2,1)S(1)} %pad_maximum_fusion.own), channel_id=1, source_target_pairs={{0,16},{16,0},{1,17},{17,1},{2,18},{18,2},{3,19},{19,3},{4,20},{20... | collective-permute-start | bytes 368648 | tf_op jit(solution)/shard_map/ppermute | solution.py:27
  121.0 6.3 %all-to-all-done.4 = bf16[16,16,384]{2,1,0:T(8,128)(2,1)S(1)} async-done(((bf16[16,16,384]{2,1,0:T(8,128)(2,1)}), bf16[16,16,384]{2,1,0:T(8,128)(2,1)S(1)}, u32[]{:S(2)}, u32[]{:S(2)}) %all-to-all-start.4) | async-done | bytes 196640 | tf_op jit(solution)/shard_map/all_to_all | solution.py:31
  129.7 2.5 %unpack.1 = (f32[384]{0:T(512)}, f32[384]{0:T(512)}, f32[772,384]{1,0:T(8,128)}, f32[772]{0:T(1024)}, f32[9,384]{1,0:T(8,128)}, /*index=5*/f32[25,384]{1,0:T(8,1...) custom-call(s32[6]{0:T(128)S(1)} %stack.36.spots, ...), custom_call_target="tpu_custom_call" | custom-call | flops 2200000000 | bytes 1720344 | tf_op jit(solution)/shard_map/unpack/pallas_call | solution.py:1134
  (75 shorter events, 11.6 us)
Async XLA Ops:
  3.2 25.4 %all-to-all-start = ((bf16[8,112,384]{2,1,0:T(8,128)(2,1)}), bf16[8,112,384]{2,1,0:T(8,128)(2,1)S(1)}, u32[]{:S(2)}, u32[]{:S(2)}) async-start(bf16[8,112,384]{2,1,0:T(8,128)(2,1)} %bitcast.14), calls=%async_computation | async-start | bytes 1376256 | tf_op jit(solution)/shard_map/all_to_all | solution.py:31
  15.6 11.5 %collective-permute-start.4 = (bf16[400,384]{1,0:T(8,128)(2,1)}, bf16[400,384]{1,0:T(8,128)(2,1)S(1)}, u32[]{:S(2)}, u32[]{:S(2)}) collective-permute-start(bf16[400,384]{1,0:T(8,128)(2,1)} %get-tuple-element.108.refs_3_.refs_2_), channel_id=1, source_target_pairs={{0,16},{16,0},{1,17},{17,1},{2,18},{18,2},{3,19},{19,3},{4,20},{20... | collective-permute-start | bytes 921608 | tf_op jit(solution)/shard_map/ppermute | solution.py:27
  17.2 10.0 %collective-permute-start.2 = (bf16[400,384]{1,0:T(8,128)(2,1)}, bf16[400,384]{1,0:T(8,128)(2,1)S(1)}, u32[]{:S(2)}, u32[]{:S(2)}) collective-permute-start(bf16[400,384]{1,0:T(8,128)(2,1)} %get-tuple-element.108.refs_3_.refs_2_), channel_id=1, source_target_pairs={{0,8},{8,0},{1,9},{9,1},{2,10},{10,2},{3,11},{11,3},{4,12},{12,4},... | collective-permute-start | bytes 921608 | tf_op jit(solution)/shard_map/ppermute | solution.py:27
  26.1 2.0 %collective-permute-start.1 = (bf16[400,384]{1,0:T(8,128)(2,1)}, bf16[400,384]{1,0:T(8,128)(2,1)S(1)}, u32[]{:S(2)}, u32[]{:S(2)}) collective-permute-start(bf16[400,384]{1,0:T(8,128)(2,1)} %get-tuple-element.114.refs_1_), channel_id=1, source_target_pairs={{0,8},{8,0},{1,9},{9,1},{2,10},{10,2},{3,11},{11,3},{4,12},{12,4},... | collective-permute-start | bytes 921608 | tf_op jit(solution)/shard_map/ppermute | solution.py:27
  26.6 9.5 %collective-permute-start = (bf16[400,384]{1,0:T(8,128)(2,1)}, bf16[400,384]{1,0:T(8,128)(2,1)S(1)}, u32[]{:S(2)}, u32[]{:S(2)}) collective-permute-start(bf16[400,384]{1,0:T(8,128)(2,1)} %get-tuple-element.114.refs_1_), channel_id=1, source_target_pairs={{0,16},{16,0},{1,17},{17,1},{2,18},{18,2},{3,19},{19,3},{4,20},{20... | collective-permute-start | bytes 921608 | tf_op jit(solution)/shard_map/ppermute | solution.py:27
  27.2 9.4 %collective-permute-start.5 = (bf16[400,384]{1,0:T(8,128)(2,1)S(1)}, bf16[400,384]{1,0:T(8,128)(2,1)S(1)}, u32[]{:S(2)}, u32[]{:S(2)}) collective-permute-start(bf16[400,384]{1,0:T(8,128)(2,1)S(1)} %collective-permute-done.4.refs_3_), channel_id=1, source_target_pairs={{0,8},{8,0},{1,9},{9,1},{2,10},{10,2},{3,11},{11,3},{4,12},{12,4},... | collective-permute-start | bytes 921608 | tf_op jit(solution)/shard_map/ppermute | solution.py:27
  36.1 1.6 %collective-permute-start.3 = (bf16[400,384]{1,0:T(8,128)(2,1)S(1)}, bf16[400,384]{1,0:T(8,128)(2,1)S(1)}, u32[]{:S(2)}, u32[]{:S(2)}) collective-permute-start(bf16[400,384]{1,0:T(8,128)(2,1)S(1)} %collective-permute-done.refs_1_), channel_id=1, source_target_pairs={{0,8},{8,0},{1,9},{9,1},{2,10},{10,2},{3,11},{11,3},{4,12},{12,4},... | collective-permute-start | bytes 921608 | tf_op jit(solution)/shard_map/ppermute | solution.py:27
  36.1 2.0 %collective-permute-start.6 = (bf16[400,384]{1,0:T(8,128)(2,1)S(1)}, bf16[400,384]{1,0:T(8,128)(2,1)S(1)}, u32[]{:S(2)}, u32[]{:S(2)}) collective-permute-start(bf16[400,384]{1,0:T(8,128)(2,1)S(1)} %get-tuple-element.120), channel_id=1, source_target_pairs={{0,8},{8,0},{1,9},{9,1},{2,10},{10,2},{3,11},{11,3},{4,12},{12,4},... | collective-permute-start | bytes 921608 | tf_op jit(solution)/shard_map/ppermute | solution.py:27
  36.6 2.0 %collective-permute-start.7 = (bf16[400,384]{1,0:T(8,128)(2,1)S(1)}, bf16[400,384]{1,0:T(8,128)(2,1)S(1)}, u32[]{:S(2)}, u32[]{:S(2)}) collective-permute-start(bf16[400,384]{1,0:T(8,128)(2,1)S(1)} %get-tuple-element.122), channel_id=1, source_target_pairs={{0,8},{8,0},{1,9},{9,1},{2,10},{10,2},{3,11},{11,3},{4,12},{12,4},... | collective-permute-start | bytes 921608 | tf_op jit(solution)/shard_map/ppermute | solution.py:27
  43.7 2.1 %collective-permute-start.8 = (bf16[800,384]{1,0:T(8,128)(2,1)S(1)}, bf16[800,384]{1,0:T(8,128)(2,1)S(1)}, u32[]{:S(2)}, u32[]{:S(2)}) collective-permute-start(bf16[800,384]{1,0:T(8,128)(2,1)S(1)} %get-tuple-element.126), channel_id=1, source_target_pairs={{0,8},{8,0},{1,9},{9,1},{2,10},{10,2},{3,11},{11,3},{4,12},{12,4},... | collective-permute-start | bytes 1843208 | tf_op jit(solution)/shard_map/ppermute | solution.py:27
  46.8 9.4 %collective-permute-start.9 = (bf16[400,384]{1,0:T(8,128)(2,1)S(1)}, bf16[400,384]{1,0:T(8,128)(2,1)S(1)}, u32[]{:S(2)}, u32[]{:S(2)}) collective-permute-start(bf16[400,384]{1,0:T(8,128)(2,1)S(1)} %get-tuple-element.127), channel_id=1, source_target_pairs={{0,16},{16,0},{1,17},{17,1},{2,18},{18,2},{3,19},{19,3},{4,20},{20... | collective-permute-start | bytes 921608 | tf_op jit(solution)/shard_map/ppermute | solution.py:27
  47.4 24.0 %all-to-all-start.1 = ((bf16[8,112,384]{2,1,0:T(8,128)(2,1)}), bf16[8,112,384]{2,1,0:T(8,128)(2,1)S(1)}, u32[]{:S(2)}, u32[]{:S(2)}) async-start(bf16[8,112,384]{2,1,0:T(8,128)(2,1)} %bitcast.16), calls=%async_computation.1 | async-start | bytes 1376256 | tf_op jit(solution)/shard_map/all_to_all | solution.py:31
  61.3 16.4 %collective-permute-start.11 = (bf16[400,384]{1,0:T(8,128)(2,1)S(1)}, bf16[400,384]{1,0:T(8,128)(2,1)S(1)}, u32[]{:S(2)}, u32[]{:S(2)}) collective-permute-start(bf16[400,384]{1,0:T(8,128)(2,1)S(1)} %copy-done.11), channel_id=1, source_target_pairs={{0,16},{16,0},{1,17},{17,1},{2,18},{18,2},{3,19},{19,3},{4,20},{20... | collective-permute-start | bytes 921608 | tf_op jit(solution)/shard_map/ppermute | solution.py:27
  61.9 7.7 %collective-permute-start.10 = (bf16[16,40,384]{2,1,0:T(8,128)(2,1)S(1)}, bf16[16,40,384]{2,1,0:T(8,128)(2,1)S(1)}, u32[]{:S(2)}, u32[]{:S(2)}) collective-permute-start(bf16[16,40,384]{2,1,0:T(8,128)(2,1)S(1)} %get-tuple-element.156), channel_id=1, source_target_pairs={{0,8},{8,0},{1,9},{9,1},{2,10},{10,2},{3,11},{11,3},{4,12},{12,4},... | collective-permute-start | bytes 1474568 | tf_op jit(solution)/shard_map/ppermute | solution.py:27
  71.5 21.2 %all-to-all-start.2 = ((bf16[16,40,384]{2,1,0:T(8,128)(2,1)}), bf16[16,40,384]{2,1,0:T(8,128)(2,1)S(1)}, u32[]{:S(2)}, u32[]{:S(2)}) async-start(bf16[16,40,384]{2,1,0:T(8,128)(2,1)} %pair.2), calls=%async_computation.2 | async-start | bytes 983040 | tf_op jit(solution)/shard_map/all_to_all | solution.py:31
  88.3 12.1 %collective-permute-start.12 = (bf16[16,16,384]{2,1,0:T(8,128)(2,1)S(1)}, bf16[16,16,384]{2,1,0:T(8,128)(2,1)S(1)}, u32[]{:S(2)}, u32[]{:S(2)}) collective-permute-start(bf16[16,16,384]{2,1,0:T(8,128)(2,1)S(1)} %get-tuple-element.169), channel_id=1, source_target_pairs={{0,8},{8,0},{1,9},{9,1},{2,10},{10,2},{3,11},{11,3},{4,12},{12,4},... | collective-permute-start | bytes 589832 | tf_op jit(solution)/shard_map/ppermute | solution.py:27
  92.8 5.9 %collective-permute-start.18 = (bf16[40,384]{1,0:T(8,128)(2,1)S(1)}, bf16[40,384]{1,0:T(8,128)(2,1)S(1)}, u32[]{:S(2)}, u32[]{:S(2)}) collective-permute-start(bf16[40,384]{1,0:T(8,128)(2,1)S(1)} %sum.3), channel_id=1, source_target_pairs={{0,6},{2,4},{4,2},{6,0},{1,7},{3,5},{5,3},{7,1},{8,14},{10,12},{12... | collective-permute-start | bytes 92168 | tf_op jit(solution)/shard_map/ppermute | solution.py:27
  94.9 4.8 %collective-permute-start.17 = (bf16[40,384]{1,0:T(8,128)(2,1)S(1)}, bf16[40,384]{1,0:T(8,128)(2,1)S(1)}, u32[]{:S(2)}, u32[]{:S(2)}) collective-permute-start(bf16[40,384]{1,0:T(8,128)(2,1)S(1)} %sum.3), channel_id=1, source_target_pairs={{0,4},{2,6},{4,0},{6,2},{1,5},{3,7},{5,1},{7,3},{8,12},{10,14},{12... | collective-permute-start | bytes 92168 | tf_op jit(solution)/shard_map/ppermute | solution.py:27
  95.4 4.2 %collective-permute-start.16 = (bf16[40,384]{1,0:T(8,128)(2,1)S(1)}, bf16[40,384]{1,0:T(8,128)(2,1)S(1)}, u32[]{:S(2)}, u32[]{:S(2)}) collective-permute-start(bf16[40,384]{1,0:T(8,128)(2,1)S(1)} %sum.3), channel_id=1, source_target_pairs={{0,2},{2,0},{4,6},{6,4},{1,3},{3,1},{5,7},{7,5},{8,10},{10,8},{12,... | collective-permute-start | bytes 92168 | tf_op jit(solution)/shard_map/ppermute | solution.py:27
  97.3 8.7 %collective-permute-start.13 = (bf16[112,384]{1,0:T(8,128)(2,1)S(1)}, bf16[112,384]{1,0:T(8,128)(2,1)S(1)}, u32[]{:S(2)}, u32[]{:S(2)}) collective-permute-start(bf16[112,384]{1,0:T(8,128)(2,1)S(1)} %sum.2.piece), channel_id=1, source_target_pairs={{0,16},{16,0},{1,17},{17,1},{2,18},{18,2},{3,19},{19,3},{4,20},{20... | collective-permute-start | bytes 258056 | tf_op jit(solution)/shard_map/ppermute | solution.py:27
  99.7 6.8 %collective-permute-start.19 = (bf16[160,384]{1,0:T(8,128)(2,1)S(1)}, bf16[160,384]{1,0:T(8,128)(2,1)S(1)}, u32[]{:S(2)}, u32[]{:S(2)}) collective-permute-start(bf16[160,384]{1,0:T(8,128)(2,1)S(1)} %pad_maximum_fusion.own), channel_id=1, source_target_pairs={{0,1},{1,0},{2,3},{3,2},{4,5},{5,4},{6,7},{7,6},{8,9},{9,8},{10,11... | collective-permute-start | bytes 368648 | tf_op jit(solution)/shard_map/ppermute | solution.py:27
  101.0 13.1 %all-to-all-start.3 = ((bf16[16,16,384]{2,1,0:T(8,128)(2,1)}), bf16[16,16,384]{2,1,0:T(8,128)(2,1)S(1)}, u32[]{:S(2)}, u32[]{:S(2)}) async-start(bf16[16,16,384]{2,1,0:T(8,128)(2,1)} %pair.3), calls=%async_computation.3 | async-start | bytes 393216 | tf_op jit(solution)/shard_map/all_to_all | solution.py:31
  105.9 8.9 %collective-permute-start.14 = (bf16[112,384]{1,0:T(8,128)(2,1)S(1)}, bf16[112,384]{1,0:T(8,128)(2,1)S(1)}, u32[]{:S(2)}, u32[]{:S(2)}) collective-permute-start(bf16[112,384]{1,0:T(8,128)(2,1)S(1)} %sum.2.piece), channel_id=1, source_target_pairs={{0,8},{8,0},{1,9},{9,1},{2,10},{10,2},{3,11},{11,3},{4,12},{12,4},... | collective-permute-start | bytes 258056 | tf_op jit(solution)/shard_map/ppermute | solution.py:27
  106.0 8.8 %collective-permute-start.15 = (bf16[112,384]{1,0:T(8,128)(2,1)S(1)}, bf16[112,384]{1,0:T(8,128)(2,1)S(1)}, u32[]{:S(2)}, u32[]{:S(2)}) collective-permute-start(bf16[112,384]{1,0:T(8,128)(2,1)S(1)} %collective-permute-done.13.piece_x), channel_id=1, source_target_pairs={{0,8},{8,0},{1,9},{9,1},{2,10},{10,2},{3,11},{11,3},{4,12},{12,4},... | collective-permute-start | bytes 258056 | tf_op jit(solution)/shard_map/ppermute | solution.py:27
  106.5 8.3 %collective-permute-start.20 = (bf16[160,384]{1,0:T(8,128)(2,1)S(1)}, bf16[160,384]{1,0:T(8,128)(2,1)S(1)}, u32[]{:S(2)}, u32[]{:S(2)}) collective-permute-start(bf16[160,384]{1,0:T(8,128)(2,1)S(1)} %collective-permute-done.19.own_b), channel_id=1, source_target_pairs={{0,16},{16,0},{1,17},{17,1},{2,18},{18,2},{3,19},{19,3},{4,20},{20... | collective-permute-start | bytes 368648 | tf_op jit(solution)/shard_map/ppermute | solution.py:27
  114.8 12.5 %all-to-all-start.4 = ((bf16[16,16,384]{2,1,0:T(8,128)(2,1)}), bf16[16,16,384]{2,1,0:T(8,128)(2,1)S(1)}, u32[]{:S(2)}, u32[]{:S(2)}) async-start(bf16[16,16,384]{2,1,0:T(8,128)(2,1)} %share.1), calls=%async_computation.4 | async-start | bytes 393216 | tf_op jit(solution)/shard_map/all_to_all | solution.py:31
  119.1 8.8 %collective-permute-start.22 = (bf16[160,384]{1,0:T(8,128)(2,1)S(1)}, bf16[160,384]{1,0:T(8,128)(2,1)S(1)}, u32[]{:S(2)}, u32[]{:S(2)}) collective-permute-start(bf16[160,384]{1,0:T(8,128)(2,1)S(1)} %pad_maximum_fusion.own), channel_id=1, source_target_pairs={{0,16},{16,0},{1,17},{17,1},{2,18},{18,2},{3,19},{19,3},{4,20},{20... | collective-permute-start | bytes 368648 | tf_op jit(solution)/shard_map/ppermute | solution.py:27
  127.3 2.4 %collective-permute-start.21 = (bf16[256,384]{1,0:T(8,128)(2,1)S(1)}, bf16[256,384]{1,0:T(8,128)(2,1)S(1)}, u32[]{:S(2)}, u32[]{:S(2)}) collective-permute-start(bf16[256,384]{1,0:T(8,128)(2,1)S(1)} %bitcast.48), channel_id=1, source_target_pairs={{0,8},{8,0},{1,9},{9,1},{2,10},{10,2},{3,11},{11,3},{4,12},{12,4},... | collective-permute-start | bytes 589832 | tf_op jit(solution)/shard_map/ppermute | solution.py:27
  127.3 1.6 %collective-permute-start.23 = (bf16[160,384]{1,0:T(8,128)(2,1)S(1)}, bf16[160,384]{1,0:T(8,128)(2,1)S(1)}, u32[]{:S(2)}, u32[]{:S(2)}) collective-permute-start(bf16[160,384]{1,0:T(8,128)(2,1)S(1)} %pad_maximum_fusion.own), channel_id=1, source_target_pairs={{0,8},{8,0},{1,9},{9,1},{2,10},{10,2},{3,11},{11,3},{4,12},{12,4},... | collective-permute-start | bytes 368648 | tf_op jit(solution)/shard_map/ppermute | solution.py:27
  127.8 1.3 %collective-permute-start.25 = (bf16[160,384]{1,0:T(8,128)(2,1)S(1)}, bf16[160,384]{1,0:T(8,128)(2,1)S(1)}, u32[]{:S(2)}, u32[]{:S(2)}) collective-permute-start(bf16[160,384]{1,0:T(8,128)(2,1)S(1)} %collective-permute-done.22.own_x), channel_id=1, source_target_pairs={{0,8},{8,0},{1,9},{9,1},{2,10},{10,2},{3,11},{11,3},{4,12},{12,4},... | collective-permute-start | bytes 368648 | tf_op jit(solution)/shard_map/ppermute | solution.py:27
  127.8 1.5 %collective-permute-start.24 = (bf16[160,384]{1,0:T(8,128)(2,1)S(1)}, bf16[160,384]{1,0:T(8,128)(2,1)S(1)}, u32[]{:S(2)}, u32[]{:S(2)}) collective-permute-start(bf16[160,384]{1,0:T(8,128)(2,1)S(1)} %collective-permute-done.19.own_b), channel_id=1, source_target_pairs={{0,8},{8,0},{1,9},{9,1},{2,10},{10,2},{3,11},{11,3},{4,12},{12,4},... | collective-permute-start | bytes 368648 | tf_op jit(solution)/shard_map/ppermute | solution.py:27
  128.4 1.3 %collective-permute-start.26 = (bf16[160,384]{1,0:T(8,128)(2,1)S(1)}, bf16[160,384]{1,0:T(8,128)(2,1)S(1)}, u32[]{:S(2)}, u32[]{:S(2)}) collective-permute-start(bf16[160,384]{1,0:T(8,128)(2,1)S(1)} %collective-permute-done.20.own_both), channel_id=1, source_target_pairs={{0,8},{8,0},{1,9},{9,1},{2,10},{10,2},{3,11},{11,3},{4,12},{12,4},... | collective-permute-start | bytes 368648 | tf_op jit(solution)/shard_map/ppermute | solution.py:27
  (12 other events, 88.1 us)

commit v2 on v1

--- a/solution.py
+++ b/solution.py
@@ -185,7 +185,8 @@
             return tuple(result)
 
         zero = jnp.zeros((sublanes, lanes), f32)
-        totals = lax.fori_loop(0, shape.side, step, (zero,) * extent)
+        first, last = max(0, reach - down), min(shape.side, shape.side + reach - down)
+        totals = lax.fori_loop(first, last, step, (zero,) * extent)
         for along in range(extent):
             out[pl.ds((starts[level] + down * extent + along) * sublanes, sublanes), :] = totals[
                 along
@@ -338,9 +339,11 @@
     query,
     inputs,
     proj_weight,
+    slope_one,
     far_one,
     far_gates,
     far_query,
+    far_slope,
     modulator,
     aggregated,
     mixed,
@@ -360,6 +363,7 @@
     moves.copy(one, far_one)
     moves.copy(gates, far_gates)
     moves.copy(query, far_query)
+    moves.copy(slope_one, far_slope)
     total = run_levels(shape, moves, chain, tap_ref)
     value, rise = gelu_pair(total * (1.0 / shape.patches))
     pooled[0:sublanes, :] = value
@@ -469,6 +473,7 @@
     def __init__(self, shards, unit):
         self.shards, self.unit = shards, unit
         self.piece_rows = 2 * unit + 16
+        self.feed_rows = 2 * unit
         self.total = shards * unit
         self.head_rows, self.late_rows = 40, 16
         self.pieces = 2 * shards
@@ -511,11 +516,14 @@
     lax.fori_loop(0, shape.rows // 16, step, 0)
 
 
-def share_kernel(parts, out):
-    total = parts[0].astype(f32)
-    for part in range(1, parts.shape[0]):
-        total = total + parts[part].astype(f32)
-    share = total.astype(bf16)
+def share_kernel(head_parts, late_parts, out):
+    sums = []
+    for parts in (head_parts, late_parts):
+        total = parts[0].astype(f32)
+        for part in range(1, parts.shape[0]):
+            total = total + parts[part].astype(f32)
+        sums.append(total)
+    share = jnp.concatenate(sums).astype(bf16)
     for copy in range(out.shape[0]):
         out[copy] = share
 
@@ -569,9 +577,7 @@
         d_near, out_near = take(2)
     else:
         outs, d_outs = take(groups), take(groups)
-    grads = take(1)[0]
-    if not closing:
-        bias_grad = take(1)[0]
+    grads, bias_grad = take(2)
     first_weight, second_weight, total_grads, total_bias = take(4)
     unit, width = units.unit, shape.width
     bias = None
@@ -614,12 +620,12 @@
         grads[...] = total_grads[...]
         bias_grad[...] = total_bias[...]
         return
-    row = jnp.concatenate([row_sum(total_bias[...]), jnp.zeros((15, width), f32)])
+    bias_grad[...] = total_bias[...]
     for shard in range(units.shards):
-        base, here = shard * units.piece_rows, shard * unit
+        base, here = shard * units.feed_rows, shard * unit
         more = units.total + here
-        grads[base : base + units.piece_rows, :] = jnp.concatenate(
-            [total_grads[here : here + unit, :], total_grads[more : more + unit, :], row]
+        grads[base : base + units.feed_rows, :] = jnp.concatenate(
+            [total_grads[here : here + unit, :], total_grads[more : more + unit, :]]
         ).astype(bf16)
 
 
@@ -633,6 +639,7 @@
     middle,
     d_near,
     d_far,
+    bias_grads,
     proj_weight,
     query,
     modulator,
@@ -642,9 +649,9 @@
     mixed,
     *refs,
 ):
-    later, refs = refs[:8], refs[8:]
+    later, refs = refs[:9], refs[9:]
     d_middle, d_query, d_aggregated, own_rest, other_rest, *refs = refs
-    fetched, refs = refs[:8], refs[8:]
+    fetched, refs = refs[:9], refs[9:]
     heads_body(
         shape,
         units,
@@ -655,6 +662,7 @@
         middle,
         d_near,
         d_far,
+        bias_grads,
         proj_weight,
         query,
         modulator,
@@ -682,6 +690,7 @@
     middle,
     d_near,
     d_far,
+    bias_grads,
     proj_weight,
     query,
     modulator,
@@ -744,7 +753,9 @@
     sums = (h_bias, proj_bias, d_gain, d_bias, out_bias, query_bias)
     head[3 * width :, :] = jnp.concatenate(
         [row_sum(item) for item in sums]
-        + [jnp.zeros((units.head_total - 3 * width - 6, width), f32)]
+        + [jnp.zeros((2, width), f32)]
+        + [row_sum(bias_grads[8 * index : 8 * index + 8, :]) for index in range(4)]
+        + [jnp.zeros((units.head_total - 3 * width - 12, width), f32)]
     )
     for half, target in enumerate((own_rest, other_rest)):
         absolute = jnp.bitwise_xor(core[0], half)
@@ -997,8 +1008,6 @@
     piece_x,
     piece_core,
     piece_both,
-    late_own,
-    late_core,
     own,
     own_b,
     own_x,
@@ -1025,7 +1034,6 @@
     second_grad,
     second_bias,
     held,
-    held_late,
     head,
     late,
 ):
@@ -1035,27 +1043,22 @@
     parts = (own, own_b, own_x, own_both, core_own, core_b, core_x, core_both)
     for index, part in enumerate(parts):
         held[index * size : (index + 1) * size, :] = part[...].astype(f32)
-    late_size = late_own.shape[0]
-    held_late[0:late_size, :] = late_own[...].astype(f32)
-    held_late[late_size : 2 * late_size, :] = late_core[...].astype(f32)
     core, shift = spots[0], spots[2]
     far = units.shards // 2
     for half in range(2):
-        late_base = jnp.bitwise_xor(core, half) * late_size
         for place in range(2):
             for close in range(2):
                 slot = jnp.bitwise_xor(core, half) * 4 + jnp.bitwise_xor(spots[3], place) * 2
                 base = (slot + jnp.bitwise_xor(spots[4], close)) * size
                 for away in range(far):
-                    here = base + jnp.bitwise_xor(spots[5], away) * units.head_rows
+                    here = base + away * units.share
                     to = ((half * 2 + place) * far + away) * 2 + close
                     head[to * units.head_rows : (to + 1) * units.head_rows, :] = held[
                         pl.ds(pl.multiple_of(here, 8), units.head_rows), :
                     ]
-                    here = late_base + ((place * far + away) * 2 + close) * units.late_rows
                     to = ((place * 2 + half) * far + away) * 2 + close
-                    late[to * units.late_rows : (to + 1) * units.late_rows, :] = held_late[
-                        pl.ds(pl.multiple_of(here, 8), units.late_rows), :
+                    late[to * units.late_rows : (to + 1) * units.late_rows, :] = held[
+                        pl.ds(pl.multiple_of(here + units.head_rows, 8), units.late_rows), :
                     ]
     total = None
     lane = lax.broadcasted_iota(jnp.int32, (8, width), 1)
@@ -1064,10 +1067,11 @@
         to = pl.ds(pl.multiple_of(quarter * unit, 8), unit)
         first_grad[to, :] = source[0:unit, :].astype(f32)
         second_grad[to, :] = source[unit : 2 * unit, :].astype(f32)
-        row = source[2 * unit : units.piece_rows, :].astype(f32)[0:8]
+    for quarter in range(4):
+        row = head[3 * width + 8 + quarter : 3 * width + 9 + quarter, :]
         moved = shift + quarter * unit
         moved = jnp.where(moved >= width, moved - width, moved)
-        row = pltpu.roll(row, moved, 1)
+        row = pltpu.roll(jnp.broadcast_to(row, (8, width)), moved, 1)
         row = jnp.where((lane >= quarter * unit) & (lane < (quarter + 1) * unit), row, 0.0)
         total = row if total is None else total + row
     first_bias[...] = total[0:1, 0 : first_bias.shape[0]].reshape(first_bias.shape)
@@ -1207,10 +1211,9 @@
 def reduce_plainly(shape, units, feed, rest, late):
     width = shape.width
     unit = units.unit
-    both = jnp.stack(feed).reshape(4, units.shards, units.piece_rows, width)
+    both = jnp.stack(feed).reshape(4, units.shards, units.feed_rows, width)
     first = both[:, :, :unit].reshape(4 * units.total, width)
-    second = both[:, :, unit : 2 * unit].reshape(4 * units.total, width)
-    bias = both[:, 0, 2 * unit].reshape(4 * units.total, 1)
+    second = both[:, :, unit:].reshape(4 * units.total, width)
 
     def shared(values):
         part = lax.psum_scatter(values, ("a", "b"), scatter_dimension=0, tiled=True)
@@ -1221,6 +1224,10 @@
     late = lax.psum(late, everyone).astype(f32)
     head = jnp.concatenate(rest).reshape(units.head_total, width)
     head = lax.psum(head, everyone).astype(f32)
+    bias = head[3 * width + 8 : 3 * width + 12].reshape(-1)
+    place = lax.axis_index("a") * 2 + lax.axis_index("b")
+    size = bias.shape[0] // (lax.axis_size("a") * 2)
+    bias = lax.dynamic_slice_in_dim(bias, place * size, size, 0)
     last = width + 8
     vectors = head[3 * width : 3 * width + 8]
     more = late[last + taps : last + taps + 4]
@@ -1239,7 +1246,7 @@
         vectors[2],
         vectors[3],
         shared(first),
-        shared(bias)[:, 0],
+        bias,
         shared(second),
         vectors[4],
     )
@@ -1317,7 +1324,7 @@
             array(rows, 4 * lanes),
             far_array(grid, lanes),
             array(grid, lanes),
-            far_array(inner, lanes),
+            array(inner, lanes),
         ],
         [
             scratch((taps * sublanes, lanes), f32),
@@ -1326,9 +1333,9 @@
         ],
         5,
         16,
-        Far(tokens_packed),
-        Far(f_turned),
-        Far(to_packed(out_grad, shape)),
+        tokens_packed,
+        f_turned,
+        to_packed(out_grad, shape),
         dw_small,
         dw_middle,
         dw_large,
@@ -1344,13 +1351,14 @@
     if quick:
         cot_far = flip(cot, "x")
         cot_core = flip(cot)
-    one, gates, query, *results = call(
+    one, gates, query, slope_one, *results = call(
         functools.partial(modulation_kernel, shape),
         "modulation",
         [
             Raw(array(grid, lanes)),
             Raw(array(rows, 4 * lanes)),
             Raw(array(rows, width)),
+            Raw(array(inner, lanes)),
             rows_array(f32),
             rows_array(),
             rows_array(),
@@ -1372,6 +1380,7 @@
         query,
         inputs,
         Far(proj_weight),
+        slope_one,
     )
     modulator, aggregated, mixed, middle, normed_two, *results = results
     two, three, slope_two, slope_three, pooled = results
@@ -1393,14 +1402,15 @@
         )
 
     near_rows = array(rows, width, kind=bf16)
-    feed_total = array(units.shards * units.piece_rows, width, kind=bf16)
+    feed_total = array(units.shards * units.feed_rows, width, kind=bf16)
+    bias_total = array(8, width)
     if quick:
         cot_both = flip(after(cot_far, middle))
         normed_far = flip(normed_two, "x")
         normed_core = flip(normed_two)
         out_own, out_core, d_own, d_core, *carry = feed(
             False,
-            [near_rows] * 4 + [array(2 * units.total, width), array(8, width)],
+            [near_rows] * 4 + [array(2 * units.total, width), bias_total],
             weights,
             Far(normed_two),
             normed_core,
@@ -1410,10 +1420,11 @@
         out_core, d_core = flip(out_core), flip(d_core)
         normed_far = after(normed_far, d_own)
         normed_both = flip(normed_far)
-        out_far, d_far, both, d_near, out_near, feed_grads = feed(
+        out_far, d_far, both, d_near, out_near, feed_grads, bias_grad = feed(
             True,
             [near_rows] * 2
-            + [array(2 * rows, width, kind=bf16), rows_array(f32), rows_array(f32), feed_total],
+            + [array(2 * rows, width, kind=bf16), rows_array(f32), rows_array(f32), feed_total]
+            + [bias_total],
             weights,
             normed_far,
             normed_both,
@@ -1440,17 +1451,21 @@
         feed_grads = after(feed_grads, d_far)
         d_far = flip(d_far, "x")
         feed_parts = exchange(feed_grads, ("a", "b"))
+        mine = (jnp.arange(4) == quarter).astype(f32)
+        bias_grads = (mine[:, None, None] * bias_grad).reshape(32, width)
     else:
         out_far = d_far = jnp.zeros((rows, width), bf16)
-        out_near, d_near, feed_grads = jnp.zeros((rows, width), f32), 0.0, []
+        out_near, d_near, feed_grads, bias_grads = jnp.zeros((rows, width), f32), 0.0, [], []
         for weights in gather_plainly(units, first, fc1_bias, second):
-            out, d_out, grads = feed(
-                None, [near_rows, near_rows, feed_total], weights, normed_two, cot
+            out, d_out, grads, bias_grad = feed(
+                None, [near_rows, near_rows, feed_total, bias_total], weights, normed_two, cot
             )
+            bias_grads.append(bias_grad)
             out_near, d_near = out_near + out.astype(f32), d_near + d_out.astype(f32)
             feed_grads.append(grads)
+        bias_grads = jnp.concatenate(bias_grads)
     rest = array(units.pieces, units.head_rows, width, kind=bf16)
-    later = [gates, pooled, slope_three, slope_two, slope_one, one, two, three]
+    later = [small, gates, pooled, slope_three, slope_two, slope_one, one, two, three]
     d_middle, d_query, d_aggregated, own_rest, other_rest, *fetched = call(
         functools.partial(heads_kernel, shape, units),
         "heads",
@@ -1470,6 +1485,7 @@
         Far(middle),
         Far(d_near),
         d_far,
+        bias_grads,
         Far(proj_weight),
         Far(query),
         Far(modulator),
@@ -1500,10 +1516,10 @@
         ],
         8,
         24,
-        Far(small),
         fetched[0],
+        fetched[1],
         d_aggregated,
-        *fetched[1:],
+        *fetched[2:],
     )
     if quick:
         (rest_half,) = call(pair_kernel, "pair", [rest], [], 1, 4, own_rest, rest_arrived)
@@ -1517,7 +1533,7 @@
     d_inputs, own_late, other_late = call(
         functools.partial(exit_kernel, shape, units),
         "exit",
-        [rows_array(f32), late, late],
+        [array(rows, width), late, late],
         [
             scratch((shape.packed, lanes), f32),
             scratch((taps * sublanes, lanes), f32),
@@ -1545,15 +1561,6 @@
     )
     if quick:
         late_arrived = flip(other_late)
-        piece_x = flip(piece, "x")
-        piece_core, piece_both = flip(piece), flip(piece_x)
-        rest_parts = after(rest_parts, own_late)
-        head_sum = total_of(rest_parts.reshape(-1, width), units.pieces)
-        (late_half,) = call(pair_kernel, "pair", [late], [], 1, 4, own_late, late_arrived)
-        late_half = after(late_half, head_sum)
-        shares = late_half.shape
-        late_parts = exchange(late_half.reshape(-1, width), ("x", "a", "b")).reshape(shares)
-        d_inputs = after(d_inputs, late_half)
     tokens_grad, block_out = call(
         functools.partial(finish_kernel, shape),
         "finish",
@@ -1562,33 +1569,39 @@
         3,
         16,
         Far(d_middle),
-        Far(d_inputs),
+        d_inputs,
         Far(small),
         Far(middle),
         Far(out_near),
         Anywhere(out_far),
     )
     if quick:
-        steps = [flip(head_sum, "a", sizes["a"], bit) for bit in range(1, sizes["a"])]
-        own = jnp.concatenate([head_sum] + steps)
+        rest_parts = after(rest_parts, tokens_grad)
+        (late_half,) = call(pair_kernel, "pair", [late], [], 1, 4, own_late, late_arrived)
+        late_half, rest_parts = lax.optimization_barrier((late_half, rest_parts))
+        shares = late_half.shape
+        late_parts = exchange(late_half.reshape(-1, width), ("x", "a", "b")).reshape(shares)
+        piece = after(piece, late_half)
+        piece_x = flip(piece, "x")
+        piece_core, piece_both = flip(piece), flip(piece_x)
+        (share,) = call(
+            share_kernel,
+            "share",
+            [array(sizes["a"], units.share, width, kind=bf16)],
+            [],
+            1,
+            6,
+            rest_parts,
+            late_parts,
+        )
+        share = after(share, piece_core, piece_both)
+        own = exchange(share.reshape(-1, width), "a")
         held_b, held_x = flip(own, "b"), flip(own, "x")
         held_both = flip(held_b, "x")
         held = [own, held_b, held_x, held_both]
-        late_parts = after(late_parts, tokens_grad)
-        (share,) = call(
-            share_kernel,
-            "share",
-            [array(units.pieces, units.late_rows, width, kind=bf16)],
-            [],
-            1,
-            6,
-            late_parts,
-        )
-        share = after(share, piece_core, piece_both, held_both)
-        late_own = exchange(share.reshape(-1, width), ("x", "a", "b"))
-        held = [late_own, flip(late_own)] + held + [flip(item) for item in held]
+        held = held + [flip(item) for item in held]
         turn = lax.rem(units.shards - shard, units.shards) * units.unit
-        spots = [core[0], quarter, turn] + [lax.axis_index(axis) for axis in ("x", "b", "a")]
+        spots = [core[0], quarter, turn] + [lax.axis_index(axis) for axis in ("x", "b")]
         spots = jnp.stack(spots).astype(jnp.int32)
         total = 4 * units.unit
         others = call(
@@ -1614,8 +1627,7 @@
                 array(width),
             ],
             [
-                scratch((units.head_total, width), f32),
-                scratch((units.late_total, width), f32),
+                scratch((2 * units.pieces * units.share, width), f32),
                 scratch((units.head_total, width), f32),
                 scratch((units.late_total, width), f32),
             ],

time: 133 us -> 129 us (0.970)
  starting transfers between devices: 45.3 us -> 34.9 us
  blocking collectives: 0 us -> 10.3 us
  Pallas kernels: 57.4 us -> 52 us
  waiting for transfers between devices: 28.2 us -> 29.6 us
    all_to_all x0 -> x1, blocking collectives: none -> 10.3 us  [exchange(): return lax.all_to_all(values, axes, split_axis=0, concat_axis=0, tiled=True)]
    ppermute x27 -> x23, waiting for transfers between devices: 13.3 us -> 21.6 us  [flip(): lax.ppermute(values, axis, [(place, place ^ bit) for place in range(size)])]
    all_to_all x5 -> x4, waiting for transfers between devices: 14.9 us -> 7.95 us  [exchange(): return lax.all_to_all(values, axes, split_axis=0, concat_axis=0, tiled=True)]
    ppermute x27 -> x23, starting transfers between devices: 16.7 us -> 9.98 us  [flip(): lax.ppermute(values, axis, [(place, place ^ bit) for place in range(size)])]
    pallas_call x16 -> x15, Pallas kernels: 57.4 us -> 52 us  [call(): pl.pallas_call(kernel, name=name, out_shape=outs, in_specs=specs, out_spe...]
    all_to_all x5 -> x4, starting transfers between devices: 28.7 us -> 24.9 us  [exchange(): return lax.all_to_all(values, axes, split_axis=0, concat_axis=0, tiled=True)]
  transfers between devices with their start and end apart: 32 -> 27, of which waited for: 18 -> 15; matrix products, arithmetic and copies ran while one was open for 0% -> 0% of each run, Pallas kernels for 35% -> 32%
where the time goes in v2:
time: 129 us; the launch traced here: 128 us
  Pallas kernels  52 us (40%)
  starting transfers between devices  34.9 us (27%)
  waiting for transfers between devices  29.6 us (23%)
  blocking collectives  10.3 us (8%)
    pallas_call x15, Pallas kernels, call(): pl.pallas_call(kernel, name=name, out_shape=outs, in_specs=specs, out_spe...  52 us
    all_to_all x4, starting transfers between devices, exchange(): return lax.all_to_all(values, axes, split_axis=0, concat_axis=0, tiled=True)  24.9 us
    ppermute x23, waiting for transfers between devices, flip(): lax.ppermute(values, axis, [(place, place ^ bit) for place in range(size)])  21.6 us
    all_to_all x1, blocking collectives, exchange(): return lax.all_to_all(values, axes, split_axis=0, concat_axis=0, tiled=True)  10.3 us
    ppermute x23, starting transfers between devices, flip(): lax.ppermute(values, axis, [(place, place ^ bit) for place in range(size)])  9.98 us
    all_to_all x4, waiting for transfers between devices, exchange(): return lax.all_to_all(values, axes, split_axis=0, concat_axis=0, tiled=True)  7.95 us
  transfers between devices with their start and end apart: 27, of which 15 were waited for; matrix products, arithmetic and copies ran while one was open for 0% of the time, Pallas kernels for 32%

profile of v2, /device:TPU:0, one launch (start us, length us, event | category | flops | bytes accessed | tf_op | source)
XLA Modules:
  0.0 128.5 jit_solution(2788454773812946814)
XLA Ops:
  0.7 2.3 %piece.1 = bf16[896,384]{1,0:T(8,128)(2,1)} custom-call(s32[3]{0:T(128)S(1)} %pad_add_fusion.spots, bf16[192,384]{1,0:T(8,128)(2,1)} %bitcast.58, bf16[192,384]{1,0:T(8,128)(2,1)} %second.1, bf16[192]{0:T(256)(128)(2,1)} %far_bias.1), custom_call_target="tpu_custom_call" | custom-call | flops 1100000000 | bytes 295308 | tf_op jit(solution)/shard_map/piece/pallas_call | solution.py:1138
  3.2 7.4 %all-to-all-start = ((bf16[8,112,384]{2,1,0:T(8,128)(2,1)}), bf16[8,112,384]{2,1,0:T(8,128)(2,1)S(1)}, u32[]{:S(2)}, u32[]{:S(2)}) async-start(bf16[8,112,384]{2,1,0:T(8,128)(2,1)} %bitcast.14), calls=%async_computation | async-start | bytes 1376256 | tf_op jit(solution)/shard_map/all_to_all | solution.py:31
  10.8 2.8 %entry.1 = (f32[96,384]{1,0:T(8,128)}, bf16[400,384]{1,0:T(8,128)(2,1)}, f32[400,384]{1,0:T(8,128)S(1)}, bf16[400,384]{1,0:T(8,128)(2,1)}, f32[400,384]{1,0:T(8,...) custom-call(bf16[1176,128]{1,0:T(8,128)(2,1)S(1)} %bitcast.57, ...), custom_call_target="tpu_custom_call" | custom-call | flops 5500000256 | bytes 1265672 | tf_op jit(solution)/shard_map/entry/pallas_call | solution.py:1138
  13.6 1.6 %collective-permute-start.4 = (bf16[400,384]{1,0:T(8,128)(2,1)}, bf16[400,384]{1,0:T(8,128)(2,1)S(1)}, u32[]{:S(2)}, u32[]{:S(2)}) collective-permute-start(bf16[400,384]{1,0:T(8,128)(2,1)} %get-tuple-element.111.refs_3_.refs_2_), channel_id=1, source_target_pairs={{0,16},{16,0},{1,17},{17,1},{2,18},{18,2},{3,19},{19,3},{4,20},{20... | collective-permute-start | bytes 921608 | tf_op jit(solution)/shard_map/ppermute | solution.py:27
  15.2 8.9 %modulation.1 = (f32[2240,128]{1,0:T(8,128)}, f32[400,512]{1,0:T(8,128)}, f32[400,384]{1,0:T(8,128)}, f32[1568,128]{1,0:T(8,128)}, f32[400,384]{1,0:T(8,128)}, /...) custom-call(f32[2240,128]{1,0:T(8,128)S(1)} %get-tuple-element.112.r, ...), custom_call_target="tpu_custom_call" | custom-call | flops 8800000000 | bytes 4734976 | tf_op jit(solution)/shard_map/modulation/pallas_call | solution.py:1138
  26.0 2.6 %all-to-all-done = bf16[8,112,384]{2,1,0:T(8,128)(2,1)S(1)} async-done(((bf16[8,112,384]{2,1,0:T(8,128)(2,1)}), bf16[8,112,384]{2,1,0:T(8,128)(2,1)S(1)}, u32[]{:S(2)}, u32[]{:S(2)}) %all-to-all-start) | async-done | bytes 688160 | tf_op jit(solution)/shard_map/all_to_all | solution.py:31
  28.6 4.1 %feed.2 = (bf16[400,384]{1,0:T(8,128)(2,1)S(1)}, bf16[400,384]{1,0:T(8,128)(2,1)S(1)}, bf16[400,384]{1,0:T(8,128)(2,1)S(1)}, bf16[400,384]{1,0:T(8,128)(2,1)S(1)...) custom-call(bf16[896,384]{1,0:T(8,128)(2,1)S(1)} %bitcast.47, bf16[400,384]{1,0:T(8,128)(2,1)} %get-tuple-element.118.refs_1_, ...), custom_call_target="tpu_custom_call" | custom-call | flops 6600000000 | bytes 1916928 | tf_op jit(solution)/shard_map/feed/pallas_call | solution.py:1138
  32.7 1.3 %collective-permute-done.refs_1_ = bf16[400,384]{1,0:T(8,128)(2,1)S(1)} collective-permute-done((bf16[400,384]{1,0:T(8,128)(2,1)}, bf16[400,384]{1,0:T(8,128)(2,1)S(1)}, u32[]{:S(2)}, u32[]{:S(2)}) %collective-permute-start) | collective-permute-done | bytes 307232 | tf_op jit(solution)/shard_map/ppermute | solution.py:27
  34.6 1.1 collective-permute-done.3.refs_2_
  36.5 5.0 %feed.3 = (bf16[400,384]{1,0:T(8,128)(2,1)S(1)}, bf16[400,384]{1,0:T(8,128)(2,1)S(1)}, bf16[800,384]{1,0:T(8,128)(2,1)S(1)}, f32[400,384]{1,0:T(8,128)}, f32[400...) custom-call(bf16[896,384]{1,0:T(8,128)(2,1)S(1)} %bitcast.48, ...), custom_call_target="tpu_custom_call" | custom-call | flops 6600000000 | bytes 4337664 | tf_op jit(solution)/shard_map/feed/pallas_call | solution.py:1138
  41.7 1.9 %collective-permute-done.8.refs_2_ = bf16[800,384]{1,0:T(8,128)(2,1)S(1)} collective-permute-done((bf16[800,384]{1,0:T(8,128)(2,1)S(1)}, bf16[800,384]{1,0:T(8,128)(2,1)S(1)}, u32[]{:S(2)}, u32[]{:S(2)}) %collective-permute-start.8) | collective-permute-done | bytes 614432 | tf_op jit(solution)/shard_map/ppermute | solution.py:27
  43.6 1.0 rows.1
  45.5 6.0 %all-to-all-start.1 = ((bf16[8,96,384]{2,1,0:T(8,128)(2,1)}), bf16[8,96,384]{2,1,0:T(8,128)(2,1)S(1)}, u32[]{:S(2)}, u32[]{:S(2)}) async-start(bf16[8,96,384]{2,1,0:T(8,128)(2,1)} %bitcast.17), calls=%async_computation.1 | async-start | bytes 1179648 | tf_op jit(solution)/shard_map/all_to_all | solution.py:31
  51.5 2.5 %collective-permute-done.9.refs_5_ = bf16[400,384]{1,0:T(8,128)(2,1)S(1)} collective-permute-done((bf16[400,384]{1,0:T(8,128)(2,1)S(1)}, bf16[400,384]{1,0:T(8,128)(2,1)S(1)}, u32[]{:S(2)}, u32[]{:S(2)}) %collective-permute-start.9) | collective-permute-done | bytes 307232 | tf_op jit(solution)/shard_map/ppermute | solution.py:27
  54.0 5.1 %heads.1 = (f32[400,384]{1,0:T(8,128)}, bf16[400,384]{1,0:T(8,128)(2,1)}, f32[400,384]{1,0:T(8,128)S(1)}, bf16[16,40,384]{2,1,0:T(8,128)(2,1)S(1)}, bf16[16,40,3...) custom-call(s32[1]{0:T(128)} %bitcast.refs_0_, ...), custom_call_target="tpu_custom_call" | custom-call | flops 5500000256 | bytes 11603972 | tf_op jit(solution)/shard_map/heads/pallas_call | solution.py:1138
  59.8 6.8 %levels_back.1 = (f32[2240,128]{1,0:T(8,128)}, f32[2240,128]{1,0:T(8,128)}, f32[2240,128]{1,0:T(8,128)}, bf16[400,384]{1,0:T(8,128)(2,1)}, bf16[400,128]{1,0:T(8,128)(2,1)}) custom-call(f32[96,384]{1,0:T(8,128)S(1)} %get-tuple-element.147.refs_0_, f32[400,512]{1,0:T(8,128)S(1)} %get-tuple-element.148.refs_1_, f32[400,384]{1,0:T(8,128)S(1)} %get-tuple-element.149.refs_2_, ...), custom_call_target="tpu_custom_call" | custom-call | flops 8800000000 | bytes 7438336 | tf_op jit(solution)/shard_map/levels_back/pallas_call | solution.py:1138
  66.6 0.9 pair.2
  67.7 7.0 %all-to-all-start.2 = ((bf16[16,40,384]{2,1,0:T(8,128)(2,1)}), bf16[16,40,384]{2,1,0:T(8,128)(2,1)S(1)}, u32[]{:S(2)}, u32[]{:S(2)}) async-start(bf16[16,40,384]{2,1,0:T(8,128)(2,1)} %pair.2), calls=%async_computation.2 | async-start | bytes 983040 | tf_op jit(solution)/shard_map/all_to_all | solution.py:31
  74.7 9.2 %exit.1 = (f32[400,384]{1,0:T(8,128)S(1)}, bf16[16,16,384]{2,1,0:T(8,128)(2,1)S(1)}, bf16[16,16,384]{2,1,0:T(8,128)(2,1)S(1)}) custom-call(s32[1]{0:T(128)} %bitcast.refs_0_, f32[2240,128]{1,0:T(8,128)} %get-tuple-element.144.refs_21_.refs_1_, f32[2240,128]{1,0:T(8,128)} %get-tuple-element.157.refs_2_, f32[2240,128]{1,0:T(8,128)} %get-tuple-element.143.refs_20_.refs_3_, ...), custom_call_target="tpu_custom_call" | custom-call | flops 9900000256 | bytes 8946692 | tf_op jit(solution)/shard_map/exit/pallas_call | solution.py:1138
  84.2 2.6 %finish.1 = (f32[1176,128]{1,0:T(8,128)}, f32[1176,128]{1,0:T(8,128)}) custom-call(f32[400,384]{1,0:T(8,128)} %get-tuple-element.146.refs_0_, f32[400,384]{1,0:T(8,128)S(1)} %get-tuple-element.173.refs_1_, f32[96,384]{1,0:T(8,128)} %get-tuple-element.110.refs_1_.refs_14_.refs_9_.refs_2_, f32[400,384]{1,0:T(8,128)} %get-tuple-element.117.refs_3_, ...), custom_call_target="tpu_custom_call" | custom-call | flops 3300000000 | bytes 2912256 | tf_op jit(solution)/shard_map/finish/pallas_call | solution.py:1138
  87.5 2.3 %all-to-all-done.2.head_parts = bf16[16,40,384]{2,1,0:T(8,128)(2,1)S(1)} async-done(((bf16[16,40,384]{2,1,0:T(8,128)(2,1)}), bf16[16,40,384]{2,1,0:T(8,128)(2,1)S(1)}, u32[]{:S(2)}, u32[]{:S(2)}) %all-to-all-start.2) | async-done | bytes 491552 | tf_op jit(solution)/shard_map/all_to_all | solution.py:31
  89.8 4.4 %all-to-all-start.3 = ((bf16[16,16,384]{2,1,0:T(8,128)(2,1)}), bf16[16,16,384]{2,1,0:T(8,128)(2,1)S(1)}, u32[]{:S(2)}, u32[]{:S(2)}) async-start(bf16[16,16,384]{2,1,0:T(8,128)(2,1)} %pair.3), calls=%async_computation.3 | async-start | bytes 393216 | tf_op jit(solution)/shard_map/all_to_all | solution.py:31
  94.2 1.9 %collective-permute-start.13 = (bf16[96,384]{1,0:T(8,128)(2,1)S(1)}, bf16[96,384]{1,0:T(8,128)(2,1)S(1)}, u32[]{:S(2)}, u32[]{:S(2)}) collective-permute-start(bf16[96,384]{1,0:T(8,128)(2,1)S(1)} %sum.1.piece), channel_id=1, source_target_pairs={{0,16},{16,0},{1,17},{17,1},{2,18},{18,2},{3,19},{19,3},{4,20},{20... | collective-permute-start | bytes 221192 | tf_op jit(solution)/shard_map/ppermute | solution.py:27
  96.2 4.0 %collective-permute-done.13.piece_x = bf16[96,384]{1,0:T(8,128)(2,1)S(1)} collective-permute-done((bf16[96,384]{1,0:T(8,128)(2,1)S(1)}, bf16[96,384]{1,0:T(8,128)(2,1)S(1)}, u32[]{:S(2)}, u32[]{:S(2)}) %collective-permute-start.13) | collective-permute-done | bytes 73760 | tf_op jit(solution)/shard_map/ppermute | solution.py:27
  100.2 3.1 %all-to-all-done.3.late_parts = bf16[16,16,384]{2,1,0:T(8,128)(2,1)S(1)} async-done(((bf16[16,16,384]{2,1,0:T(8,128)(2,1)}), bf16[16,16,384]{2,1,0:T(8,128)(2,1)S(1)}, u32[]{:S(2)}, u32[]{:S(2)}) %all-to-all-start.3) | async-done | bytes 196640 | tf_op jit(solution)/shard_map/all_to_all | solution.py:31
  103.4 10.3 %all_to_all.43 = bf16[4,56,384]{2,1,0:T(8,128)(2,1)S(1)} all-to-all(bf16[4,56,384]{2,1,0:T(8,128)(2,1)S(1)} %share.1), channel_id=1, replica_groups=mesh['x'=2,'core'=2,'a'=4,'b'=2] {'a'}, dimensions={0} | all-to-all | bytes 344064 | tf_op jit(solution)/shard_map/all_to_all | solution.py:31
  113.6 1.2 collective-permute-start.16
  115.7 3.4 %collective-permute-done.16.own_b = bf16[224,384]{1,0:T(8,128)(2,1)S(1)} collective-permute-done((bf16[224,384]{1,0:T(8,128)(2,1)S(1)}, bf16[224,384]{1,0:T(8,128)(2,1)S(1)}, u32[]{:S(2)}, u32[]{:S(2)}) %collective-permute-start.16) | collective-permute-done | bytes 172064 | tf_op jit(solution)/shard_map/ppermute | solution.py:27
  120.2 1.9 %collective-permute-done.17.own_x = bf16[224,384]{1,0:T(8,128)(2,1)S(1)} collective-permute-done((bf16[224,384]{1,0:T(8,128)(2,1)S(1)}, bf16[224,384]{1,0:T(8,128)(2,1)S(1)}, u32[]{:S(2)}, u32[]{:S(2)}) %collective-permute-start.17) | collective-permute-done | bytes 172064 | tf_op jit(solution)/shard_map/ppermute | solution.py:27
  122.0 2.4 %collective-permute-done.18.own_both = bf16[224,384]{1,0:T(8,128)(2,1)S(1)} collective-permute-done((bf16[224,384]{1,0:T(8,128)(2,1)S(1)}, bf16[224,384]{1,0:T(8,128)(2,1)S(1)}, u32[]{:S(2)}, u32[]{:S(2)}) %collective-permute-start.18) | collective-permute-done | bytes 172064 | tf_op jit(solution)/shard_map/ppermute | solution.py:27
  124.6 1.3 %collective-permute-done.22.core_both = bf16[224,384]{1,0:T(8,128)(2,1)S(1)} collective-permute-done((bf16[224,384]{1,0:T(8,128)(2,1)S(1)}, bf16[224,384]{1,0:T(8,128)(2,1)S(1)}, u32[]{:S(2)}, u32[]{:S(2)}) %collective-permute-start.22) | collective-permute-done | bytes 172064 | tf_op jit(solution)/shard_map/ppermute | solution.py:27
  125.9 2.4 %unpack.1 = (f32[384]{0:T(512)}, f32[384]{0:T(512)}, f32[772,384]{1,0:T(8,128)}, f32[772]{0:T(1024)}, f32[9,384]{1,0:T(8,128)}, /*index=5*/f32[25,384]{1,0:T(8,1...) custom-call(s32[5]{0:T(128)S(1)} %stack.32.spots, ...), custom_call_target="tpu_custom_call" | custom-call | flops 2200000000 | bytes 1671188 | tf_op jit(solution)/shard_map/unpack/pallas_call | solution.py:1138
  (74 shorter events, 8.5 us)
Async XLA Ops:
  3.0 7.6 %copy-start = (bf16[384,772]{0,1:T(8,128)(2,1)S(1)}, bf16[384,772]{0,1:T(8,128)(2,1)}, u32[]{:S(2)}) copy-start(bf16[384,772]{0,1:T(8,128)(2,1)} %param.22) | copy-start | bytes 1778692
  3.1 7.6 %copy-start.1 = (bf16[2,14,14,384]{3,0,2,1:T(2,128)(2,1)S(1)}, bf16[2,14,14,384]{3,0,2,1:T(2,128)(2,1)}, u32[]{:S(2)}) copy-start(bf16[2,14,14,384]{3,0,2,1:T(2,128)(2,1)} %param.37) | copy-start | bytes 903172
  3.1 7.6 %copy-start.2 = (bf16[2,14,14,384]{3,0,2,1:T(2,128)(2,1)S(1)}, bf16[2,14,14,384]{3,0,2,1:T(2,128)(2,1)}, u32[]{:S(2)}) copy-start(bf16[2,14,14,384]{3,0,2,1:T(2,128)(2,1)} %param.19) | copy-start | bytes 903172
  3.1 7.6 %copy-start.3 = (bf16[49,384]{1,0:T(8,128)(2,1)S(1)}, bf16[49,384]{1,0:T(8,128)(2,1)}, u32[]{:S(2)}) copy-start(bf16[49,384]{1,0:T(8,128)(2,1)} %refs_5_.1) | copy-start | bytes 112900
  3.1 7.6 %copy-start.4 = (bf16[25,384]{1,0:T(8,128)(2,1)S(1)}, bf16[25,384]{1,0:T(8,128)(2,1)}, u32[]{:S(2)}) copy-start(bf16[25,384]{1,0:T(8,128)(2,1)} %refs_4_.1) | copy-start | bytes 57604
  3.2 25.4 %all-to-all-start = ((bf16[8,112,384]{2,1,0:T(8,128)(2,1)}), bf16[8,112,384]{2,1,0:T(8,128)(2,1)S(1)}, u32[]{:S(2)}, u32[]{:S(2)}) async-start(bf16[8,112,384]{2,1,0:T(8,128)(2,1)} %bitcast.14), calls=%async_computation | async-start | bytes 1376256 | tf_op jit(solution)/shard_map/all_to_all | solution.py:31
  13.6 11.5 %collective-permute-start.4 = (bf16[400,384]{1,0:T(8,128)(2,1)}, bf16[400,384]{1,0:T(8,128)(2,1)S(1)}, u32[]{:S(2)}, u32[]{:S(2)}) collective-permute-start(bf16[400,384]{1,0:T(8,128)(2,1)} %get-tuple-element.111.refs_3_.refs_2_), channel_id=1, source_target_pairs={{0,16},{16,0},{1,17},{17,1},{2,18},{18,2},{3,19},{19,3},{4,20},{20... | collective-permute-start | bytes 921608 | tf_op jit(solution)/shard_map/ppermute | solution.py:27
  15.2 10.0 %collective-permute-start.2 = (bf16[400,384]{1,0:T(8,128)(2,1)}, bf16[400,384]{1,0:T(8,128)(2,1)S(1)}, u32[]{:S(2)}, u32[]{:S(2)}) collective-permute-start(bf16[400,384]{1,0:T(8,128)(2,1)} %get-tuple-element.111.refs_3_.refs_2_), channel_id=1, source_target_pairs={{0,8},{8,0},{1,9},{9,1},{2,10},{10,2},{3,11},{11,3},{4,12},{12,4},... | collective-permute-start | bytes 921608 | tf_op jit(solution)/shard_map/ppermute | solution.py:27
  24.0 2.0 %collective-permute-start.1 = (bf16[400,384]{1,0:T(8,128)(2,1)}, bf16[400,384]{1,0:T(8,128)(2,1)S(1)}, u32[]{:S(2)}, u32[]{:S(2)}) collective-permute-start(bf16[400,384]{1,0:T(8,128)(2,1)} %get-tuple-element.118.refs_1_), channel_id=1, source_target_pairs={{0,8},{8,0},{1,9},{9,1},{2,10},{10,2},{3,11},{11,3},{4,12},{12,4},... | collective-permute-start | bytes 921608 | tf_op jit(solution)/shard_map/ppermute | solution.py:27
  24.6 9.5 %collective-permute-start = (bf16[400,384]{1,0:T(8,128)(2,1)}, bf16[400,384]{1,0:T(8,128)(2,1)S(1)}, u32[]{:S(2)}, u32[]{:S(2)}) collective-permute-start(bf16[400,384]{1,0:T(8,128)(2,1)} %get-tuple-element.118.refs_1_), channel_id=1, source_target_pairs={{0,16},{16,0},{1,17},{17,1},{2,18},{18,2},{3,19},{19,3},{4,20},{20... | collective-permute-start | bytes 921608 | tf_op jit(solution)/shard_map/ppermute | solution.py:27
  25.1 9.4 %collective-permute-start.5 = (bf16[400,384]{1,0:T(8,128)(2,1)S(1)}, bf16[400,384]{1,0:T(8,128)(2,1)S(1)}, u32[]{:S(2)}, u32[]{:S(2)}) collective-permute-start(bf16[400,384]{1,0:T(8,128)(2,1)S(1)} %collective-permute-done.4.refs_3_), channel_id=1, source_target_pairs={{0,8},{8,0},{1,9},{9,1},{2,10},{10,2},{3,11},{11,3},{4,12},{12,4},... | collective-permute-start | bytes 921608 | tf_op jit(solution)/shard_map/ppermute | solution.py:27
  34.1 1.6 %collective-permute-start.3 = (bf16[400,384]{1,0:T(8,128)(2,1)S(1)}, bf16[400,384]{1,0:T(8,128)(2,1)S(1)}, u32[]{:S(2)}, u32[]{:S(2)}) collective-permute-start(bf16[400,384]{1,0:T(8,128)(2,1)S(1)} %collective-permute-done.refs_1_), channel_id=1, source_target_pairs={{0,8},{8,0},{1,9},{9,1},{2,10},{10,2},{3,11},{11,3},{4,12},{12,4},... | collective-permute-start | bytes 921608 | tf_op jit(solution)/shard_map/ppermute | solution.py:27
  34.1 2.0 %collective-permute-start.6 = (bf16[400,384]{1,0:T(8,128)(2,1)S(1)}, bf16[400,384]{1,0:T(8,128)(2,1)S(1)}, u32[]{:S(2)}, u32[]{:S(2)}) collective-permute-start(bf16[400,384]{1,0:T(8,128)(2,1)S(1)} %get-tuple-element.124), channel_id=1, source_target_pairs={{0,8},{8,0},{1,9},{9,1},{2,10},{10,2},{3,11},{11,3},{4,12},{12,4},... | collective-permute-start | bytes 921608 | tf_op jit(solution)/shard_map/ppermute | solution.py:27
  34.6 2.0 %collective-permute-start.7 = (bf16[400,384]{1,0:T(8,128)(2,1)S(1)}, bf16[400,384]{1,0:T(8,128)(2,1)S(1)}, u32[]{:S(2)}, u32[]{:S(2)}) collective-permute-start(bf16[400,384]{1,0:T(8,128)(2,1)S(1)} %get-tuple-element.126), channel_id=1, source_target_pairs={{0,8},{8,0},{1,9},{9,1},{2,10},{10,2},{3,11},{11,3},{4,12},{12,4},... | collective-permute-start | bytes 921608 | tf_op jit(solution)/shard_map/ppermute | solution.py:27
  41.5 2.1 %collective-permute-start.8 = (bf16[800,384]{1,0:T(8,128)(2,1)S(1)}, bf16[800,384]{1,0:T(8,128)(2,1)S(1)}, u32[]{:S(2)}, u32[]{:S(2)}) collective-permute-start(bf16[800,384]{1,0:T(8,128)(2,1)S(1)} %get-tuple-element.130), channel_id=1, source_target_pairs={{0,8},{8,0},{1,9},{9,1},{2,10},{10,2},{3,11},{11,3},{4,12},{12,4},... | collective-permute-start | bytes 1843208 | tf_op jit(solution)/shard_map/ppermute | solution.py:27
  44.7 9.4 %collective-permute-start.9 = (bf16[400,384]{1,0:T(8,128)(2,1)S(1)}, bf16[400,384]{1,0:T(8,128)(2,1)S(1)}, u32[]{:S(2)}, u32[]{:S(2)}) collective-permute-start(bf16[400,384]{1,0:T(8,128)(2,1)S(1)} %get-tuple-element.131), channel_id=1, source_target_pairs={{0,16},{16,0},{1,17},{17,1},{2,18},{18,2},{3,19},{19,3},{4,20},{20... | collective-permute-start | bytes 921608 | tf_op jit(solution)/shard_map/ppermute | solution.py:27
  45.5 22.0 %all-to-all-start.1 = ((bf16[8,96,384]{2,1,0:T(8,128)(2,1)}), bf16[8,96,384]{2,1,0:T(8,128)(2,1)S(1)}, u32[]{:S(2)}, u32[]{:S(2)}) async-start(bf16[8,96,384]{2,1,0:T(8,128)(2,1)} %bitcast.17), calls=%async_computation.1 | async-start | bytes 1179648 | tf_op jit(solution)/shard_map/all_to_all | solution.py:31
  59.2 15.5 %collective-permute-start.11 = (bf16[400,384]{1,0:T(8,128)(2,1)S(1)}, bf16[400,384]{1,0:T(8,128)(2,1)S(1)}, u32[]{:S(2)}, u32[]{:S(2)}) collective-permute-start(bf16[400,384]{1,0:T(8,128)(2,1)S(1)} %copy-done.14), channel_id=1, source_target_pairs={{0,16},{16,0},{1,17},{17,1},{2,18},{18,2},{3,19},{19,3},{4,20},{20... | collective-permute-start | bytes 921608 | tf_op jit(solution)/shard_map/ppermute | solution.py:27
  59.8 6.8 %collective-permute-start.10 = (bf16[16,40,384]{2,1,0:T(8,128)(2,1)S(1)}, bf16[16,40,384]{2,1,0:T(8,128)(2,1)S(1)}, u32[]{:S(2)}, u32[]{:S(2)}) collective-permute-start(bf16[16,40,384]{2,1,0:T(8,128)(2,1)S(1)} %get-tuple-element.162), channel_id=1, source_target_pairs={{0,8},{8,0},{1,9},{9,1},{2,10},{10,2},{3,11},{11,3},{4,12},{12,4},... | collective-permute-start | bytes 1474568 | tf_op jit(solution)/shard_map/ppermute | solution.py:27
  67.7 22.1 %all-to-all-start.2 = ((bf16[16,40,384]{2,1,0:T(8,128)(2,1)}), bf16[16,40,384]{2,1,0:T(8,128)(2,1)S(1)}, u32[]{:S(2)}, u32[]{:S(2)}) async-start(bf16[16,40,384]{2,1,0:T(8,128)(2,1)} %pair.2), calls=%async_computation.2 | async-start | bytes 983040 | tf_op jit(solution)/shard_map/all_to_all | solution.py:31
  83.9 2.9 %collective-permute-start.12 = (bf16[16,16,384]{2,1,0:T(8,128)(2,1)S(1)}, bf16[16,16,384]{2,1,0:T(8,128)(2,1)S(1)}, u32[]{:S(2)}, u32[]{:S(2)}) collective-permute-start(bf16[16,16,384]{2,1,0:T(8,128)(2,1)S(1)} %get-tuple-element.178), channel_id=1, source_target_pairs={{0,8},{8,0},{1,9},{9,1},{2,10},{10,2},{3,11},{11,3},{4,12},{12,4},... | collective-permute-start | bytes 589832 | tf_op jit(solution)/shard_map/ppermute | solution.py:27
  89.8 13.5 %all-to-all-start.3 = ((bf16[16,16,384]{2,1,0:T(8,128)(2,1)}), bf16[16,16,384]{2,1,0:T(8,128)(2,1)S(1)}, u32[]{:S(2)}, u32[]{:S(2)}) async-start(bf16[16,16,384]{2,1,0:T(8,128)(2,1)} %pair.3), calls=%async_computation.3 | async-start | bytes 393216 | tf_op jit(solution)/shard_map/all_to_all | solution.py:31
  94.2 5.9 %collective-permute-start.13 = (bf16[96,384]{1,0:T(8,128)(2,1)S(1)}, bf16[96,384]{1,0:T(8,128)(2,1)S(1)}, u32[]{:S(2)}, u32[]{:S(2)}) collective-permute-start(bf16[96,384]{1,0:T(8,128)(2,1)S(1)} %sum.1.piece), channel_id=1, source_target_pairs={{0,16},{16,0},{1,17},{17,1},{2,18},{18,2},{3,19},{19,3},{4,20},{20... | collective-permute-start | bytes 221192 | tf_op jit(solution)/shard_map/ppermute | solution.py:27
  96.2 7.2 %collective-permute-start.14 = (bf16[96,384]{1,0:T(8,128)(2,1)S(1)}, bf16[96,384]{1,0:T(8,128)(2,1)S(1)}, u32[]{:S(2)}, u32[]{:S(2)}) collective-permute-start(bf16[96,384]{1,0:T(8,128)(2,1)S(1)} %sum.1.piece), channel_id=1, source_target_pairs={{0,8},{8,0},{1,9},{9,1},{2,10},{10,2},{3,11},{11,3},{4,12},{12,4},... | collective-permute-start | bytes 221192 | tf_op jit(solution)/shard_map/ppermute | solution.py:27
  100.2 3.2 %collective-permute-start.15 = (bf16[96,384]{1,0:T(8,128)(2,1)S(1)}, bf16[96,384]{1,0:T(8,128)(2,1)S(1)}, u32[]{:S(2)}, u32[]{:S(2)}) collective-permute-start(bf16[96,384]{1,0:T(8,128)(2,1)S(1)} %collective-permute-done.13.piece_x), channel_id=1, source_target_pairs={{0,8},{8,0},{1,9},{9,1},{2,10},{10,2},{3,11},{11,3},{4,12},{12,4},... | collective-permute-start | bytes 221192 | tf_op jit(solution)/shard_map/ppermute | solution.py:27
  113.6 5.4 %collective-permute-start.16 = (bf16[224,384]{1,0:T(8,128)(2,1)S(1)}, bf16[224,384]{1,0:T(8,128)(2,1)S(1)}, u32[]{:S(2)}, u32[]{:S(2)}) collective-permute-start(bf16[224,384]{1,0:T(8,128)(2,1)S(1)} %bitcast.49), channel_id=1, source_target_pairs={{0,1},{1,0},{2,3},{3,2},{4,5},{5,4},{6,7},{7,6},{8,9},{9,8},{10,11... | collective-permute-start | bytes 516104 | tf_op jit(solution)/shard_map/ppermute | solution.py:27
  114.9 7.2 %collective-permute-start.17 = (bf16[224,384]{1,0:T(8,128)(2,1)S(1)}, bf16[224,384]{1,0:T(8,128)(2,1)S(1)}, u32[]{:S(2)}, u32[]{:S(2)}) collective-permute-start(bf16[224,384]{1,0:T(8,128)(2,1)S(1)} %bitcast.50), channel_id=1, source_target_pairs={{0,16},{16,0},{1,17},{17,1},{2,18},{18,2},{3,19},{19,3},{4,20},{20... | collective-permute-start | bytes 516104 | tf_op jit(solution)/shard_map/ppermute | solution.py:27
  119.1 5.4 %collective-permute-start.18 = (bf16[224,384]{1,0:T(8,128)(2,1)S(1)}, bf16[224,384]{1,0:T(8,128)(2,1)S(1)}, u32[]{:S(2)}, u32[]{:S(2)}) collective-permute-start(bf16[224,384]{1,0:T(8,128)(2,1)S(1)} %collective-permute-done.16.own_b), channel_id=1, source_target_pairs={{0,16},{16,0},{1,17},{17,1},{2,18},{18,2},{3,19},{19,3},{4,20},{20... | collective-permute-start | bytes 516104 | tf_op jit(solution)/shard_map/ppermute | solution.py:27
  119.7 4.9 %collective-permute-start.19 = (bf16[224,384]{1,0:T(8,128)(2,1)S(1)}, bf16[224,384]{1,0:T(8,128)(2,1)S(1)}, u32[]{:S(2)}, u32[]{:S(2)}) collective-permute-start(bf16[224,384]{1,0:T(8,128)(2,1)S(1)} %bitcast.51), channel_id=1, source_target_pairs={{0,8},{8,0},{1,9},{9,1},{2,10},{10,2},{3,11},{11,3},{4,12},{12,4},... | collective-permute-start | bytes 516104 | tf_op jit(solution)/shard_map/ppermute | solution.py:27
  119.7 4.9 %collective-permute-start.20 = (bf16[224,384]{1,0:T(8,128)(2,1)S(1)}, bf16[224,384]{1,0:T(8,128)(2,1)S(1)}, u32[]{:S(2)}, u32[]{:S(2)}) collective-permute-start(bf16[224,384]{1,0:T(8,128)(2,1)S(1)} %collective-permute-done.16.own_b), channel_id=1, source_target_pairs={{0,8},{8,0},{1,9},{9,1},{2,10},{10,2},{3,11},{11,3},{4,12},{12,4},... | collective-permute-start | bytes 516104 | tf_op jit(solution)/shard_map/ppermute | solution.py:27
  122.0 2.5 %collective-permute-start.21 = (bf16[224,384]{1,0:T(8,128)(2,1)S(1)}, bf16[224,384]{1,0:T(8,128)(2,1)S(1)}, u32[]{:S(2)}, u32[]{:S(2)}) collective-permute-start(bf16[224,384]{1,0:T(8,128)(2,1)S(1)} %collective-permute-done.17.own_x), channel_id=1, source_target_pairs={{0,8},{8,0},{1,9},{9,1},{2,10},{10,2},{3,11},{11,3},{4,12},{12,4},... | collective-permute-start | bytes 516104 | tf_op jit(solution)/shard_map/ppermute | solution.py:27
  124.5 1.4 %collective-permute-start.22 = (bf16[224,384]{1,0:T(8,128)(2,1)S(1)}, bf16[224,384]{1,0:T(8,128)(2,1)S(1)}, u32[]{:S(2)}, u32[]{:S(2)}) collective-permute-start(bf16[224,384]{1,0:T(8,128)(2,1)S(1)} %collective-permute-done.18.own_both), channel_id=1, source_target_pairs={{0,8},{8,0},{1,9},{9,1},{2,10},{10,2},{3,11},{11,3},{4,12},{12,4},... | collective-permute-start | bytes 516104 | tf_op jit(solution)/shard_map/ppermute | solution.py:27
  (10 other events, 73.3 us)

commit v3 on v2

--- a/solution.py
+++ b/solution.py
@@ -19,6 +19,7 @@
 taps = 83
 LN1_GAIN, LN1_BIAS, QUERY_BIAS, CONTEXT_BIAS, GATE_BIAS = 83, 84, 85, 86, 87
 H_BIAS, PROJ_BIAS, LN2_GAIN, LN2_BIAS, FC2_BIAS = 88, 89, 90, 91, 92
+erfc_terms = (0.254829592, -0.284496736, 1.421413741, -1.453152027, 1.061405429)
 f32 = jnp.float32
 bf16 = jnp.bfloat16
 
@@ -48,9 +49,14 @@
 
 
 def gelu_pair(values):
-    below = 0.5 * (1.0 + lax.erf(values * math.sqrt(0.5)))
-    density = jnp.exp(values * values * -0.5) * (1.0 / math.sqrt(2.0 * math.pi))
-    return values * below, below + values * density
+    step = 1.0 / (1.0 + jnp.abs(values) * (0.3275911 * math.sqrt(0.5)))
+    power = jnp.exp(values * values * -0.5)
+    tail = jnp.full_like(values, 0.5 * erfc_terms[-1])
+    for term in erfc_terms[-2::-1]:
+        tail = tail * step + 0.5 * term
+    tail = tail * step * power
+    below = jnp.where(values >= 0.0, 1.0 - tail, tail)
+    return values * below, below + values * power * (1.0 / math.sqrt(2.0 * math.pi))
 
 
 class Shape:

time: 129 us -> 130 us (level)
  Pallas kernels: 52 us -> 53.9 us
    pallas_call x15, Pallas kernels: 52 us -> 53.9 us  [call(): pl.pallas_call(kernel, name=name, out_shape=outs, in_specs=specs, out_spe...]
  transfers between devices with their start and end apart: 27 -> 27, of which waited for: 15 -> 15; matrix products, arithmetic and copies ran while one was open for 0% -> 0% of each run, Pallas kernels for 32% -> 33%
where the time goes in v3:
time: 130 us
  Pallas kernels  53.9 us (41%)
  starting transfers between devices  34.9 us (27%)
  waiting for transfers between devices  29.1 us (22%)
  blocking collectives  10.3 us (8%)
    pallas_call x15, Pallas kernels, call(): pl.pallas_call(kernel, name=name, out_shape=outs, in_specs=specs, out_spe...  53.9 us
    all_to_all x4, starting transfers between devices, exchange(): return lax.all_to_all(values, axes, split_axis=0, concat_axis=0, tiled=True)  24.9 us
    ppermute x23, waiting for transfers between devices, flip(): lax.ppermute(values, axis, [(place, place ^ bit) for place in range(size)])  22.1 us
    all_to_all x1, blocking collectives, exchange(): return lax.all_to_all(values, axes, split_axis=0, concat_axis=0, tiled=True)  10.3 us
    ppermute x23, starting transfers between devices, flip(): lax.ppermute(values, axis, [(place, place ^ bit) for place in range(size)])  9.97 us
    all_to_all x4, waiting for transfers between devices, exchange(): return lax.all_to_all(values, axes, split_axis=0, concat_axis=0, tiled=True)  6.99 us
  transfers between devices with their start and end apart: 27, of which 15 were waited for; matrix products, arithmetic and copies ran while one was open for 0% of the time, Pallas kernels for 33%

profile of v3, /device:TPU:0, one launch (start us, length us, event | category | flops | bytes accessed | tf_op | source)
XLA Modules:
  0.0 129.8 jit_solution(10432433944259308735)
XLA Ops:
  0.7 2.3 %piece.1 = bf16[896,384]{1,0:T(8,128)(2,1)} custom-call(s32[3]{0:T(128)S(1)} %pad_add_fusion.spots, bf16[192,384]{1,0:T(8,128)(2,1)} %bitcast.58, bf16[192,384]{1,0:T(8,128)(2,1)} %second.1, bf16[192]{0:T(256)(128)(2,1)} %far_bias.1), custom_call_target="tpu_custom_call" | custom-call | flops 1100000000 | bytes 295308 | tf_op jit(solution)/shard_map/piece/pallas_call | solution.py:1144
  3.2 7.4 %all-to-all-start = ((bf16[8,112,384]{2,1,0:T(8,128)(2,1)}), bf16[8,112,384]{2,1,0:T(8,128)(2,1)S(1)}, u32[]{:S(2)}, u32[]{:S(2)}) async-start(bf16[8,112,384]{2,1,0:T(8,128)(2,1)} %bitcast.14), calls=%async_computation | async-start | bytes 1376256 | tf_op jit(solution)/shard_map/all_to_all | solution.py:32
  10.8 3.2 %entry.1 = (f32[96,384]{1,0:T(8,128)}, bf16[400,384]{1,0:T(8,128)(2,1)}, f32[400,384]{1,0:T(8,128)S(1)}, bf16[400,384]{1,0:T(8,128)(2,1)}, f32[400,384]{1,0:T(8,...) custom-call(bf16[1176,128]{1,0:T(8,128)(2,1)S(1)} %bitcast.57, ...), custom_call_target="tpu_custom_call" | custom-call | flops 5500000256 | bytes 1265672 | tf_op jit(solution)/shard_map/entry/pallas_call | solution.py:1144
  14.0 1.6 %collective-permute-start.4 = (bf16[400,384]{1,0:T(8,128)(2,1)}, bf16[400,384]{1,0:T(8,128)(2,1)S(1)}, u32[]{:S(2)}, u32[]{:S(2)}) collective-permute-start(bf16[400,384]{1,0:T(8,128)(2,1)} %get-tuple-element.111.refs_3_.refs_2_), channel_id=1, source_target_pairs={{0,16},{16,0},{1,17},{17,1},{2,18},{18,2},{3,19},{19,3},{4,20},{20... | collective-permute-start | bytes 921608 | tf_op jit(solution)/shard_map/ppermute | solution.py:28
  15.5 9.4 %modulation.1 = (f32[2240,128]{1,0:T(8,128)}, f32[400,512]{1,0:T(8,128)}, f32[400,384]{1,0:T(8,128)}, f32[1568,128]{1,0:T(8,128)}, f32[400,384]{1,0:T(8,128)}, /...) custom-call(f32[2240,128]{1,0:T(8,128)S(1)} %get-tuple-element.112.r, ...), custom_call_target="tpu_custom_call" | custom-call | flops 8800000000 | bytes 4734976 | tf_op jit(solution)/shard_map/modulation/pallas_call | solution.py:1144
  27.0 1.6 %all-to-all-done = bf16[8,112,384]{2,1,0:T(8,128)(2,1)S(1)} async-done(((bf16[8,112,384]{2,1,0:T(8,128)(2,1)}), bf16[8,112,384]{2,1,0:T(8,128)(2,1)S(1)}, u32[]{:S(2)}, u32[]{:S(2)}) %all-to-all-start) | async-done | bytes 688160 | tf_op jit(solution)/shard_map/all_to_all | solution.py:32
  28.6 4.6 %feed.2 = (bf16[400,384]{1,0:T(8,128)(2,1)S(1)}, bf16[400,384]{1,0:T(8,128)(2,1)S(1)}, bf16[400,384]{1,0:T(8,128)(2,1)S(1)}, bf16[400,384]{1,0:T(8,128)(2,1)S(1)...) custom-call(bf16[896,384]{1,0:T(8,128)(2,1)S(1)} %bitcast.47, bf16[400,384]{1,0:T(8,128)(2,1)} %get-tuple-element.118.refs_1_, ...), custom_call_target="tpu_custom_call" | custom-call | flops 6600000000 | bytes 1916928 | tf_op jit(solution)/shard_map/feed/pallas_call | solution.py:1144
  33.2 1.8 %collective-permute-done.refs_1_ = bf16[400,384]{1,0:T(8,128)(2,1)S(1)} collective-permute-done((bf16[400,384]{1,0:T(8,128)(2,1)}, bf16[400,384]{1,0:T(8,128)(2,1)S(1)}, u32[]{:S(2)}, u32[]{:S(2)}) %collective-permute-start) | collective-permute-done | bytes 307232 | tf_op jit(solution)/shard_map/ppermute | solution.py:28
  35.5 1.1 collective-permute-done.3.refs_2_
  37.5 5.4 %feed.3 = (bf16[400,384]{1,0:T(8,128)(2,1)S(1)}, bf16[400,384]{1,0:T(8,128)(2,1)S(1)}, bf16[800,384]{1,0:T(8,128)(2,1)S(1)}, f32[400,384]{1,0:T(8,128)}, f32[400...) custom-call(bf16[896,384]{1,0:T(8,128)(2,1)S(1)} %bitcast.48, ...), custom_call_target="tpu_custom_call" | custom-call | flops 6600000000 | bytes 4337664 | tf_op jit(solution)/shard_map/feed/pallas_call | solution.py:1144
  43.1 1.9 %collective-permute-done.8.refs_2_ = bf16[800,384]{1,0:T(8,128)(2,1)S(1)} collective-permute-done((bf16[800,384]{1,0:T(8,128)(2,1)S(1)}, bf16[800,384]{1,0:T(8,128)(2,1)S(1)}, u32[]{:S(2)}, u32[]{:S(2)}) %collective-permute-start.8) | collective-permute-done | bytes 614432 | tf_op jit(solution)/shard_map/ppermute | solution.py:28
  45.0 1.0 rows.1
  46.9 6.0 %all-to-all-start.1 = ((bf16[8,96,384]{2,1,0:T(8,128)(2,1)}), bf16[8,96,384]{2,1,0:T(8,128)(2,1)S(1)}, u32[]{:S(2)}, u32[]{:S(2)}) async-start(bf16[8,96,384]{2,1,0:T(8,128)(2,1)} %bitcast.17), calls=%async_computation.1 | async-start | bytes 1179648 | tf_op jit(solution)/shard_map/all_to_all | solution.py:32
  52.9 2.5 %collective-permute-done.9.refs_5_ = bf16[400,384]{1,0:T(8,128)(2,1)S(1)} collective-permute-done((bf16[400,384]{1,0:T(8,128)(2,1)S(1)}, bf16[400,384]{1,0:T(8,128)(2,1)S(1)}, u32[]{:S(2)}, u32[]{:S(2)}) %collective-permute-start.9) | collective-permute-done | bytes 307232 | tf_op jit(solution)/shard_map/ppermute | solution.py:28
  55.4 5.1 %heads.1 = (f32[400,384]{1,0:T(8,128)}, bf16[400,384]{1,0:T(8,128)(2,1)}, f32[400,384]{1,0:T(8,128)S(1)}, bf16[16,40,384]{2,1,0:T(8,128)(2,1)S(1)}, bf16[16,40,3...) custom-call(s32[1]{0:T(128)} %bitcast.refs_0_, ...), custom_call_target="tpu_custom_call" | custom-call | flops 5500000256 | bytes 11603972 | tf_op jit(solution)/shard_map/heads/pallas_call | solution.py:1144
  61.2 6.8 %levels_back.1 = (f32[2240,128]{1,0:T(8,128)}, f32[2240,128]{1,0:T(8,128)}, f32[2240,128]{1,0:T(8,128)}, bf16[400,384]{1,0:T(8,128)(2,1)}, bf16[400,128]{1,0:T(8,128)(2,1)}) custom-call(f32[96,384]{1,0:T(8,128)S(1)} %get-tuple-element.147.refs_0_, f32[400,512]{1,0:T(8,128)S(1)} %get-tuple-element.148.refs_1_, f32[400,384]{1,0:T(8,128)S(1)} %get-tuple-element.149.refs_2_, ...), custom_call_target="tpu_custom_call" | custom-call | flops 8800000000 | bytes 7438336 | tf_op jit(solution)/shard_map/levels_back/pallas_call | solution.py:1144
  68.0 0.9 pair.2
  69.0 7.0 %all-to-all-start.2 = ((bf16[16,40,384]{2,1,0:T(8,128)(2,1)}), bf16[16,40,384]{2,1,0:T(8,128)(2,1)S(1)}, u32[]{:S(2)}, u32[]{:S(2)}) async-start(bf16[16,40,384]{2,1,0:T(8,128)(2,1)} %pair.2), calls=%async_computation.2 | async-start | bytes 983040 | tf_op jit(solution)/shard_map/all_to_all | solution.py:32
  76.1 9.2 %exit.1 = (f32[400,384]{1,0:T(8,128)S(1)}, bf16[16,16,384]{2,1,0:T(8,128)(2,1)S(1)}, bf16[16,16,384]{2,1,0:T(8,128)(2,1)S(1)}) custom-call(s32[1]{0:T(128)} %bitcast.refs_0_, f32[2240,128]{1,0:T(8,128)} %get-tuple-element.144.refs_21_.refs_1_, f32[2240,128]{1,0:T(8,128)} %get-tuple-element.157.refs_2_, f32[2240,128]{1,0:T(8,128)} %get-tuple-element.143.refs_20_.refs_3_, ...), custom_call_target="tpu_custom_call" | custom-call | flops 9900000256 | bytes 8946692 | tf_op jit(solution)/shard_map/exit/pallas_call | solution.py:1144
  85.6 2.6 %finish.1 = (f32[1176,128]{1,0:T(8,128)}, f32[1176,128]{1,0:T(8,128)}) custom-call(f32[400,384]{1,0:T(8,128)} %get-tuple-element.146.refs_0_, f32[400,384]{1,0:T(8,128)S(1)} %get-tuple-element.173.refs_1_, f32[96,384]{1,0:T(8,128)} %get-tuple-element.110.refs_1_.refs_14_.refs_9_.refs_2_, f32[400,384]{1,0:T(8,128)} %get-tuple-element.117.refs_3_, ...), custom_call_target="tpu_custom_call" | custom-call | flops 3300000000 | bytes 2912256 | tf_op jit(solution)/shard_map/finish/pallas_call | solution.py:1144
  88.9 2.3 %all-to-all-done.2.head_parts = bf16[16,40,384]{2,1,0:T(8,128)(2,1)S(1)} async-done(((bf16[16,40,384]{2,1,0:T(8,128)(2,1)}), bf16[16,40,384]{2,1,0:T(8,128)(2,1)S(1)}, u32[]{:S(2)}, u32[]{:S(2)}) %all-to-all-start.2) | async-done | bytes 491552 | tf_op jit(solution)/shard_map/all_to_all | solution.py:32
  91.2 4.4 %all-to-all-start.3 = ((bf16[16,16,384]{2,1,0:T(8,128)(2,1)}), bf16[16,16,384]{2,1,0:T(8,128)(2,1)S(1)}, u32[]{:S(2)}, u32[]{:S(2)}) async-start(bf16[16,16,384]{2,1,0:T(8,128)(2,1)} %pair.3), calls=%async_computation.3 | async-start | bytes 393216 | tf_op jit(solution)/shard_map/all_to_all | solution.py:32
  95.6 1.9 %collective-permute-start.13 = (bf16[96,384]{1,0:T(8,128)(2,1)S(1)}, bf16[96,384]{1,0:T(8,128)(2,1)S(1)}, u32[]{:S(2)}, u32[]{:S(2)}) collective-permute-start(bf16[96,384]{1,0:T(8,128)(2,1)S(1)} %sum.1.piece), channel_id=1, source_target_pairs={{0,16},{16,0},{1,17},{17,1},{2,18},{18,2},{3,19},{19,3},{4,20},{20... | collective-permute-start | bytes 221192 | tf_op jit(solution)/shard_map/ppermute | solution.py:28
  97.6 4.0 %collective-permute-done.13.piece_x = bf16[96,384]{1,0:T(8,128)(2,1)S(1)} collective-permute-done((bf16[96,384]{1,0:T(8,128)(2,1)S(1)}, bf16[96,384]{1,0:T(8,128)(2,1)S(1)}, u32[]{:S(2)}, u32[]{:S(2)}) %collective-permute-start.13) | collective-permute-done | bytes 73760 | tf_op jit(solution)/shard_map/ppermute | solution.py:28
  101.5 3.1 %all-to-all-done.3.late_parts = bf16[16,16,384]{2,1,0:T(8,128)(2,1)S(1)} async-done(((bf16[16,16,384]{2,1,0:T(8,128)(2,1)}), bf16[16,16,384]{2,1,0:T(8,128)(2,1)S(1)}, u32[]{:S(2)}, u32[]{:S(2)}) %all-to-all-start.3) | async-done | bytes 196640 | tf_op jit(solution)/shard_map/all_to_all | solution.py:32
  104.8 10.3 %all_to_all.43 = bf16[4,56,384]{2,1,0:T(8,128)(2,1)S(1)} all-to-all(bf16[4,56,384]{2,1,0:T(8,128)(2,1)S(1)} %share.1), channel_id=1, replica_groups=mesh['x'=2,'core'=2,'a'=4,'b'=2] {'a'}, dimensions={0} | all-to-all | bytes 344064 | tf_op jit(solution)/shard_map/all_to_all | solution.py:32
  115.0 1.2 collective-permute-start.16
  117.0 3.4 %collective-permute-done.16.own_b = bf16[224,384]{1,0:T(8,128)(2,1)S(1)} collective-permute-done((bf16[224,384]{1,0:T(8,128)(2,1)S(1)}, bf16[224,384]{1,0:T(8,128)(2,1)S(1)}, u32[]{:S(2)}, u32[]{:S(2)}) %collective-permute-start.16) | collective-permute-done | bytes 172064 | tf_op jit(solution)/shard_map/ppermute | solution.py:28
  121.6 1.9 %collective-permute-done.17.own_x = bf16[224,384]{1,0:T(8,128)(2,1)S(1)} collective-permute-done((bf16[224,384]{1,0:T(8,128)(2,1)S(1)}, bf16[224,384]{1,0:T(8,128)(2,1)S(1)}, u32[]{:S(2)}, u32[]{:S(2)}) %collective-permute-start.17) | collective-permute-done | bytes 172064 | tf_op jit(solution)/shard_map/ppermute | solution.py:28
  123.4 2.4 %collective-permute-done.18.own_both = bf16[224,384]{1,0:T(8,128)(2,1)S(1)} collective-permute-done((bf16[224,384]{1,0:T(8,128)(2,1)S(1)}, bf16[224,384]{1,0:T(8,128)(2,1)S(1)}, u32[]{:S(2)}, u32[]{:S(2)}) %collective-permute-start.18) | collective-permute-done | bytes 172064 | tf_op jit(solution)/shard_map/ppermute | solution.py:28
  125.9 1.3 %collective-permute-done.22.core_both = bf16[224,384]{1,0:T(8,128)(2,1)S(1)} collective-permute-done((bf16[224,384]{1,0:T(8,128)(2,1)S(1)}, bf16[224,384]{1,0:T(8,128)(2,1)S(1)}, u32[]{:S(2)}, u32[]{:S(2)}) %collective-permute-start.22) | collective-permute-done | bytes 172064 | tf_op jit(solution)/shard_map/ppermute | solution.py:28
  127.3 2.4 %unpack.1 = (f32[384]{0:T(512)}, f32[384]{0:T(512)}, f32[772,384]{1,0:T(8,128)}, f32[772]{0:T(1024)}, f32[9,384]{1,0:T(8,128)}, /*index=5*/f32[25,384]{1,0:T(8,1...) custom-call(s32[5]{0:T(128)S(1)} %stack.32.spots, ...), custom_call_target="tpu_custom_call" | custom-call | flops 2200000000 | bytes 1671188 | tf_op jit(solution)/shard_map/unpack/pallas_call | solution.py:1144
  (74 shorter events, 8.5 us)
Async XLA Ops:
  3.0 7.6 %copy-start = (bf16[384,772]{0,1:T(8,128)(2,1)S(1)}, bf16[384,772]{0,1:T(8,128)(2,1)}, u32[]{:S(2)}) copy-start(bf16[384,772]{0,1:T(8,128)(2,1)} %param.22) | copy-start | bytes 1778692
  3.1 7.6 %copy-start.1 = (bf16[2,14,14,384]{3,0,2,1:T(2,128)(2,1)S(1)}, bf16[2,14,14,384]{3,0,2,1:T(2,128)(2,1)}, u32[]{:S(2)}) copy-start(bf16[2,14,14,384]{3,0,2,1:T(2,128)(2,1)} %param.37) | copy-start | bytes 903172
  3.1 7.6 %copy-start.2 = (bf16[2,14,14,384]{3,0,2,1:T(2,128)(2,1)S(1)}, bf16[2,14,14,384]{3,0,2,1:T(2,128)(2,1)}, u32[]{:S(2)}) copy-start(bf16[2,14,14,384]{3,0,2,1:T(2,128)(2,1)} %param.19) | copy-start | bytes 903172
  3.1 7.6 %copy-start.3 = (bf16[49,384]{1,0:T(8,128)(2,1)S(1)}, bf16[49,384]{1,0:T(8,128)(2,1)}, u32[]{:S(2)}) copy-start(bf16[49,384]{1,0:T(8,128)(2,1)} %refs_5_.1) | copy-start | bytes 112900
  3.1 7.6 %copy-start.4 = (bf16[25,384]{1,0:T(8,128)(2,1)S(1)}, bf16[25,384]{1,0:T(8,128)(2,1)}, u32[]{:S(2)}) copy-start(bf16[25,384]{1,0:T(8,128)(2,1)} %refs_4_.1) | copy-start | bytes 57604
  3.2 25.4 %all-to-all-start = ((bf16[8,112,384]{2,1,0:T(8,128)(2,1)}), bf16[8,112,384]{2,1,0:T(8,128)(2,1)S(1)}, u32[]{:S(2)}, u32[]{:S(2)}) async-start(bf16[8,112,384]{2,1,0:T(8,128)(2,1)} %bitcast.14), calls=%async_computation | async-start | bytes 1376256 | tf_op jit(solution)/shard_map/all_to_all | solution.py:32
  14.0 12.1 %collective-permute-start.4 = (bf16[400,384]{1,0:T(8,128)(2,1)}, bf16[400,384]{1,0:T(8,128)(2,1)S(1)}, u32[]{:S(2)}, u32[]{:S(2)}) collective-permute-start(bf16[400,384]{1,0:T(8,128)(2,1)} %get-tuple-element.111.refs_3_.refs_2_), channel_id=1, source_target_pairs={{0,16},{16,0},{1,17},{17,1},{2,18},{18,2},{3,19},{19,3},{4,20},{20... | collective-permute-start | bytes 921608 | tf_op jit(solution)/shard_map/ppermute | solution.py:28
  15.5 10.6 %collective-permute-start.2 = (bf16[400,384]{1,0:T(8,128)(2,1)}, bf16[400,384]{1,0:T(8,128)(2,1)S(1)}, u32[]{:S(2)}, u32[]{:S(2)}) collective-permute-start(bf16[400,384]{1,0:T(8,128)(2,1)} %get-tuple-element.111.refs_3_.refs_2_), channel_id=1, source_target_pairs={{0,8},{8,0},{1,9},{9,1},{2,10},{10,2},{3,11},{11,3},{4,12},{12,4},... | collective-permute-start | bytes 921608 | tf_op jit(solution)/shard_map/ppermute | solution.py:28
  25.0 2.0 %collective-permute-start.1 = (bf16[400,384]{1,0:T(8,128)(2,1)}, bf16[400,384]{1,0:T(8,128)(2,1)S(1)}, u32[]{:S(2)}, u32[]{:S(2)}) collective-permute-start(bf16[400,384]{1,0:T(8,128)(2,1)} %get-tuple-element.118.refs_1_), channel_id=1, source_target_pairs={{0,8},{8,0},{1,9},{9,1},{2,10},{10,2},{3,11},{11,3},{4,12},{12,4},... | collective-permute-start | bytes 921608 | tf_op jit(solution)/shard_map/ppermute | solution.py:28
  25.6 9.5 %collective-permute-start = (bf16[400,384]{1,0:T(8,128)(2,1)}, bf16[400,384]{1,0:T(8,128)(2,1)S(1)}, u32[]{:S(2)}, u32[]{:S(2)}) collective-permute-start(bf16[400,384]{1,0:T(8,128)(2,1)} %get-tuple-element.118.refs_1_), channel_id=1, source_target_pairs={{0,16},{16,0},{1,17},{17,1},{2,18},{18,2},{3,19},{19,3},{4,20},{20... | collective-permute-start | bytes 921608 | tf_op jit(solution)/shard_map/ppermute | solution.py:28
  26.1 9.4 %collective-permute-start.5 = (bf16[400,384]{1,0:T(8,128)(2,1)S(1)}, bf16[400,384]{1,0:T(8,128)(2,1)S(1)}, u32[]{:S(2)}, u32[]{:S(2)}) collective-permute-start(bf16[400,384]{1,0:T(8,128)(2,1)S(1)} %collective-permute-done.4.refs_3_), channel_id=1, source_target_pairs={{0,8},{8,0},{1,9},{9,1},{2,10},{10,2},{3,11},{11,3},{4,12},{12,4},... | collective-permute-start | bytes 921608 | tf_op jit(solution)/shard_map/ppermute | solution.py:28
  35.0 1.6 %collective-permute-start.3 = (bf16[400,384]{1,0:T(8,128)(2,1)S(1)}, bf16[400,384]{1,0:T(8,128)(2,1)S(1)}, u32[]{:S(2)}, u32[]{:S(2)}) collective-permute-start(bf16[400,384]{1,0:T(8,128)(2,1)S(1)} %collective-permute-done.refs_1_), channel_id=1, source_target_pairs={{0,8},{8,0},{1,9},{9,1},{2,10},{10,2},{3,11},{11,3},{4,12},{12,4},... | collective-permute-start | bytes 921608 | tf_op jit(solution)/shard_map/ppermute | solution.py:28
  35.0 2.0 %collective-permute-start.6 = (bf16[400,384]{1,0:T(8,128)(2,1)S(1)}, bf16[400,384]{1,0:T(8,128)(2,1)S(1)}, u32[]{:S(2)}, u32[]{:S(2)}) collective-permute-start(bf16[400,384]{1,0:T(8,128)(2,1)S(1)} %get-tuple-element.124), channel_id=1, source_target_pairs={{0,8},{8,0},{1,9},{9,1},{2,10},{10,2},{3,11},{11,3},{4,12},{12,4},... | collective-permute-start | bytes 921608 | tf_op jit(solution)/shard_map/ppermute | solution.py:28
  35.5 2.0 %collective-permute-start.7 = (bf16[400,384]{1,0:T(8,128)(2,1)S(1)}, bf16[400,384]{1,0:T(8,128)(2,1)S(1)}, u32[]{:S(2)}, u32[]{:S(2)}) collective-permute-start(bf16[400,384]{1,0:T(8,128)(2,1)S(1)} %get-tuple-element.126), channel_id=1, source_target_pairs={{0,8},{8,0},{1,9},{9,1},{2,10},{10,2},{3,11},{11,3},{4,12},{12,4},... | collective-permute-start | bytes 921608 | tf_op jit(solution)/shard_map/ppermute | solution.py:28
  42.9 2.1 %collective-permute-start.8 = (bf16[800,384]{1,0:T(8,128)(2,1)S(1)}, bf16[800,384]{1,0:T(8,128)(2,1)S(1)}, u32[]{:S(2)}, u32[]{:S(2)}) collective-permute-start(bf16[800,384]{1,0:T(8,128)(2,1)S(1)} %get-tuple-element.130), channel_id=1, source_target_pairs={{0,8},{8,0},{1,9},{9,1},{2,10},{10,2},{3,11},{11,3},{4,12},{12,4},... | collective-permute-start | bytes 1843208 | tf_op jit(solution)/shard_map/ppermute | solution.py:28
  46.0 9.4 %collective-permute-start.9 = (bf16[400,384]{1,0:T(8,128)(2,1)S(1)}, bf16[400,384]{1,0:T(8,128)(2,1)S(1)}, u32[]{:S(2)}, u32[]{:S(2)}) collective-permute-start(bf16[400,384]{1,0:T(8,128)(2,1)S(1)} %get-tuple-element.131), channel_id=1, source_target_pairs={{0,16},{16,0},{1,17},{17,1},{2,18},{18,2},{3,19},{19,3},{4,20},{20... | collective-permute-start | bytes 921608 | tf_op jit(solution)/shard_map/ppermute | solution.py:28
  46.9 22.0 %all-to-all-start.1 = ((bf16[8,96,384]{2,1,0:T(8,128)(2,1)}), bf16[8,96,384]{2,1,0:T(8,128)(2,1)S(1)}, u32[]{:S(2)}, u32[]{:S(2)}) async-start(bf16[8,96,384]{2,1,0:T(8,128)(2,1)} %bitcast.17), calls=%async_computation.1 | async-start | bytes 1179648 | tf_op jit(solution)/shard_map/all_to_all | solution.py:32
  60.6 15.5 %collective-permute-start.11 = (bf16[400,384]{1,0:T(8,128)(2,1)S(1)}, bf16[400,384]{1,0:T(8,128)(2,1)S(1)}, u32[]{:S(2)}, u32[]{:S(2)}) collective-permute-start(bf16[400,384]{1,0:T(8,128)(2,1)S(1)} %copy-done.14), channel_id=1, source_target_pairs={{0,16},{16,0},{1,17},{17,1},{2,18},{18,2},{3,19},{19,3},{4,20},{20... | collective-permute-start | bytes 921608 | tf_op jit(solution)/shard_map/ppermute | solution.py:28
  61.2 6.8 %collective-permute-start.10 = (bf16[16,40,384]{2,1,0:T(8,128)(2,1)S(1)}, bf16[16,40,384]{2,1,0:T(8,128)(2,1)S(1)}, u32[]{:S(2)}, u32[]{:S(2)}) collective-permute-start(bf16[16,40,384]{2,1,0:T(8,128)(2,1)S(1)} %get-tuple-element.162), channel_id=1, source_target_pairs={{0,8},{8,0},{1,9},{9,1},{2,10},{10,2},{3,11},{11,3},{4,12},{12,4},... | collective-permute-start | bytes 1474568 | tf_op jit(solution)/shard_map/ppermute | solution.py:28
  69.0 22.1 %all-to-all-start.2 = ((bf16[16,40,384]{2,1,0:T(8,128)(2,1)}), bf16[16,40,384]{2,1,0:T(8,128)(2,1)S(1)}, u32[]{:S(2)}, u32[]{:S(2)}) async-start(bf16[16,40,384]{2,1,0:T(8,128)(2,1)} %pair.2), calls=%async_computation.2 | async-start | bytes 983040 | tf_op jit(solution)/shard_map/all_to_all | solution.py:32
  85.3 2.9 %collective-permute-start.12 = (bf16[16,16,384]{2,1,0:T(8,128)(2,1)S(1)}, bf16[16,16,384]{2,1,0:T(8,128)(2,1)S(1)}, u32[]{:S(2)}, u32[]{:S(2)}) collective-permute-start(bf16[16,16,384]{2,1,0:T(8,128)(2,1)S(1)} %get-tuple-element.178), channel_id=1, source_target_pairs={{0,8},{8,0},{1,9},{9,1},{2,10},{10,2},{3,11},{11,3},{4,12},{12,4},... | collective-permute-start | bytes 589832 | tf_op jit(solution)/shard_map/ppermute | solution.py:28
  91.2 13.5 %all-to-all-start.3 = ((bf16[16,16,384]{2,1,0:T(8,128)(2,1)}), bf16[16,16,384]{2,1,0:T(8,128)(2,1)S(1)}, u32[]{:S(2)}, u32[]{:S(2)}) async-start(bf16[16,16,384]{2,1,0:T(8,128)(2,1)} %pair.3), calls=%async_computation.3 | async-start | bytes 393216 | tf_op jit(solution)/shard_map/all_to_all | solution.py:32
  95.6 5.9 %collective-permute-start.13 = (bf16[96,384]{1,0:T(8,128)(2,1)S(1)}, bf16[96,384]{1,0:T(8,128)(2,1)S(1)}, u32[]{:S(2)}, u32[]{:S(2)}) collective-permute-start(bf16[96,384]{1,0:T(8,128)(2,1)S(1)} %sum.1.piece), channel_id=1, source_target_pairs={{0,16},{16,0},{1,17},{17,1},{2,18},{18,2},{3,19},{19,3},{4,20},{20... | collective-permute-start | bytes 221192 | tf_op jit(solution)/shard_map/ppermute | solution.py:28
  97.6 7.2 %collective-permute-start.14 = (bf16[96,384]{1,0:T(8,128)(2,1)S(1)}, bf16[96,384]{1,0:T(8,128)(2,1)S(1)}, u32[]{:S(2)}, u32[]{:S(2)}) collective-permute-start(bf16[96,384]{1,0:T(8,128)(2,1)S(1)} %sum.1.piece), channel_id=1, source_target_pairs={{0,8},{8,0},{1,9},{9,1},{2,10},{10,2},{3,11},{11,3},{4,12},{12,4},... | collective-permute-start | bytes 221192 | tf_op jit(solution)/shard_map/ppermute | solution.py:28
  101.5 3.2 %collective-permute-start.15 = (bf16[96,384]{1,0:T(8,128)(2,1)S(1)}, bf16[96,384]{1,0:T(8,128)(2,1)S(1)}, u32[]{:S(2)}, u32[]{:S(2)}) collective-permute-start(bf16[96,384]{1,0:T(8,128)(2,1)S(1)} %collective-permute-done.13.piece_x), channel_id=1, source_target_pairs={{0,8},{8,0},{1,9},{9,1},{2,10},{10,2},{3,11},{11,3},{4,12},{12,4},... | collective-permute-start | bytes 221192 | tf_op jit(solution)/shard_map/ppermute | solution.py:28
  115.0 5.4 %collective-permute-start.16 = (bf16[224,384]{1,0:T(8,128)(2,1)S(1)}, bf16[224,384]{1,0:T(8,128)(2,1)S(1)}, u32[]{:S(2)}, u32[]{:S(2)}) collective-permute-start(bf16[224,384]{1,0:T(8,128)(2,1)S(1)} %bitcast.49), channel_id=1, source_target_pairs={{0,1},{1,0},{2,3},{3,2},{4,5},{5,4},{6,7},{7,6},{8,9},{9,8},{10,11... | collective-permute-start | bytes 516104 | tf_op jit(solution)/shard_map/ppermute | solution.py:28
  116.3 7.2 %collective-permute-start.17 = (bf16[224,384]{1,0:T(8,128)(2,1)S(1)}, bf16[224,384]{1,0:T(8,128)(2,1)S(1)}, u32[]{:S(2)}, u32[]{:S(2)}) collective-permute-start(bf16[224,384]{1,0:T(8,128)(2,1)S(1)} %bitcast.50), channel_id=1, source_target_pairs={{0,16},{16,0},{1,17},{17,1},{2,18},{18,2},{3,19},{19,3},{4,20},{20... | collective-permute-start | bytes 516104 | tf_op jit(solution)/shard_map/ppermute | solution.py:28
  120.4 5.4 %collective-permute-start.18 = (bf16[224,384]{1,0:T(8,128)(2,1)S(1)}, bf16[224,384]{1,0:T(8,128)(2,1)S(1)}, u32[]{:S(2)}, u32[]{:S(2)}) collective-permute-start(bf16[224,384]{1,0:T(8,128)(2,1)S(1)} %collective-permute-done.16.own_b), channel_id=1, source_target_pairs={{0,16},{16,0},{1,17},{17,1},{2,18},{18,2},{3,19},{19,3},{4,20},{20... | collective-permute-start | bytes 516104 | tf_op jit(solution)/shard_map/ppermute | solution.py:28
  121.0 4.9 %collective-permute-start.19 = (bf16[224,384]{1,0:T(8,128)(2,1)S(1)}, bf16[224,384]{1,0:T(8,128)(2,1)S(1)}, u32[]{:S(2)}, u32[]{:S(2)}) collective-permute-start(bf16[224,384]{1,0:T(8,128)(2,1)S(1)} %bitcast.51), channel_id=1, source_target_pairs={{0,8},{8,0},{1,9},{9,1},{2,10},{10,2},{3,11},{11,3},{4,12},{12,4},... | collective-permute-start | bytes 516104 | tf_op jit(solution)/shard_map/ppermute | solution.py:28
  121.0 4.9 %collective-permute-start.20 = (bf16[224,384]{1,0:T(8,128)(2,1)S(1)}, bf16[224,384]{1,0:T(8,128)(2,1)S(1)}, u32[]{:S(2)}, u32[]{:S(2)}) collective-permute-start(bf16[224,384]{1,0:T(8,128)(2,1)S(1)} %collective-permute-done.16.own_b), channel_id=1, source_target_pairs={{0,8},{8,0},{1,9},{9,1},{2,10},{10,2},{3,11},{11,3},{4,12},{12,4},... | collective-permute-start | bytes 516104 | tf_op jit(solution)/shard_map/ppermute | solution.py:28
  123.4 2.5 %collective-permute-start.21 = (bf16[224,384]{1,0:T(8,128)(2,1)S(1)}, bf16[224,384]{1,0:T(8,128)(2,1)S(1)}, u32[]{:S(2)}, u32[]{:S(2)}) collective-permute-start(bf16[224,384]{1,0:T(8,128)(2,1)S(1)} %collective-permute-done.17.own_x), channel_id=1, source_target_pairs={{0,8},{8,0},{1,9},{9,1},{2,10},{10,2},{3,11},{11,3},{4,12},{12,4},... | collective-permute-start | bytes 516104 | tf_op jit(solution)/shard_map/ppermute | solution.py:28
  125.8 1.4 %collective-permute-start.22 = (bf16[224,384]{1,0:T(8,128)(2,1)S(1)}, bf16[224,384]{1,0:T(8,128)(2,1)S(1)}, u32[]{:S(2)}, u32[]{:S(2)}) collective-permute-start(bf16[224,384]{1,0:T(8,128)(2,1)S(1)} %collective-permute-done.18.own_both), channel_id=1, source_target_pairs={{0,8},{8,0},{1,9},{9,1},{2,10},{10,2},{3,11},{11,3},{4,12},{12,4},... | collective-permute-start | bytes 516104 | tf_op jit(solution)/shard_map/ppermute | solution.py:28
  (10 other events, 73.3 us)

commit v4 on v2

--- a/solution.py
+++ b/solution.py
@@ -959,12 +959,11 @@
     )
     for half, target in enumerate((own_late, other_late)):
         absolute = jnp.bitwise_xor(core[0], half)
-        for place in range(2):
-            for spot in range(units.shards):
-                first = ((place * 2 + absolute) * units.shards + spot) * units.late_rows
-                target[place * units.shards + spot] = gathered[
-                    pl.ds(pl.multiple_of(first, 16), units.late_rows), :
-                ].astype(bf16)
+        for piece in range(units.pieces):
+            first = (absolute * units.pieces + piece) * units.late_rows
+            target[piece] = gathered[
+                pl.ds(pl.multiple_of(first, 16), units.late_rows), :
+            ].astype(bf16)
 
 
 def finish_kernel(
@@ -1050,16 +1049,14 @@
             for close in range(2):
                 slot = jnp.bitwise_xor(core, half) * 4 + jnp.bitwise_xor(spots[3], place) * 2
                 base = (slot + jnp.bitwise_xor(spots[4], close)) * size
-                for away in range(far):
-                    here = base + away * units.share
-                    to = ((half * 2 + place) * far + away) * 2 + close
-                    head[to * units.head_rows : (to + 1) * units.head_rows, :] = held[
-                        pl.ds(pl.multiple_of(here, 8), units.head_rows), :
-                    ]
-                    to = ((place * 2 + half) * far + away) * 2 + close
-                    late[to * units.late_rows : (to + 1) * units.late_rows, :] = held[
-                        pl.ds(pl.multiple_of(here + units.head_rows, 8), units.late_rows), :
-                    ]
+                to = (half * 2 + place) * 2 + close
+                rows = far * units.head_rows
+                head[to * rows : (to + 1) * rows, :] = held[
+                    pl.ds(pl.multiple_of(base, 8), rows), :
+                ]
+                first = pl.multiple_of(base + rows, 8)
+                rows = far * units.late_rows
+                late[to * rows : (to + 1) * rows, :] = held[pl.ds(first, rows), :]
     total = None
     lane = lax.broadcasted_iota(jnp.int32, (8, width), 1)
     for index, source in enumerate((piece, piece_core, piece_x, piece_both)):
@@ -1219,8 +1216,7 @@
         part = lax.psum_scatter(values, ("a", "b"), scatter_dimension=0, tiled=True)
         return lax.psum(part, ("x", "core")).astype(f32)
 
-    late = jnp.stack(late).reshape(2, 2, units.shards, units.late_rows, width)
-    late = late.transpose(1, 0, 2, 3, 4).reshape(units.late_total, width)
+    late = jnp.concatenate(late).reshape(units.late_total, width)
     late = lax.psum(late, everyone).astype(f32)
     head = jnp.concatenate(rest).reshape(units.head_total, width)
     head = lax.psum(head, everyone).astype(f32)
@@ -1528,12 +1524,13 @@
         rest_half = after(rest_half, piece)
         d_one = after(d_one, rest_half, out_far)
         shares = rest_half.shape
-        rest_parts = exchange(rest_half.reshape(-1, width), ("x", "a", "b")).reshape(shares)
+        rest_parts = exchange(rest_half.reshape(-1, width), ("x", "b"))
+        rest_parts = rest_parts.reshape(4, shares[0] * shares[1] // 4, width)
     late = array(units.pieces, units.late_rows, width, kind=bf16)
     d_inputs, own_late, other_late = call(
         functools.partial(exit_kernel, shape, units),
         "exit",
-        [array(rows, width), late, late],
+        [rows_array(f32), late, late],
         [
             scratch((shape.packed, lanes), f32),
             scratch((taps * sublanes, lanes), f32),
@@ -1561,6 +1558,12 @@
     )
     if quick:
         late_arrived = flip(other_late)
+        rest_parts = after(rest_parts, own_late)
+        (late_half,) = call(pair_kernel, "pair", [late], [], 1, 4, own_late, late_arrived)
+        late_half, rest_parts = lax.optimization_barrier((late_half, rest_parts))
+        late_parts = exchange(late_half.reshape(-1, width), ("x", "b"))
+        late_parts = late_parts.reshape(4, units.pieces * units.late_rows // 4, width)
+        d_inputs = after(d_inputs, late_half)
     tokens_grad, block_out = call(
         functools.partial(finish_kernel, shape),
         "finish",
@@ -1569,33 +1572,31 @@
         3,
         16,
         Far(d_middle),
-        d_inputs,
+        Far(d_inputs),
         Far(small),
         Far(middle),
         Far(out_near),
         Anywhere(out_far),
     )
     if quick:
-        rest_parts = after(rest_parts, tokens_grad)
-        (late_half,) = call(pair_kernel, "pair", [late], [], 1, 4, own_late, late_arrived)
-        late_half, rest_parts = lax.optimization_barrier((late_half, rest_parts))
-        shares = late_half.shape
-        late_parts = exchange(late_half.reshape(-1, width), ("x", "a", "b")).reshape(shares)
-        piece = after(piece, late_half)
-        piece_x = flip(piece, "x")
-        piece_core, piece_both = flip(piece), flip(piece_x)
+        late_parts = after(late_parts, tokens_grad)
+        share_rows = units.pieces * units.share // 4
         (share,) = call(
             share_kernel,
             "share",
-            [array(sizes["a"], units.share, width, kind=bf16)],
+            [array(sizes["a"], share_rows, width, kind=bf16)],
             [],
             1,
-            6,
+            8,
             rest_parts,
             late_parts,
         )
-        share = after(share, piece_core, piece_both)
-        own = exchange(share.reshape(-1, width), "a")
+        piece = after(piece, share)
+        piece_x = flip(piece, "x")
+        piece_core, piece_both = flip(piece), flip(piece_x)
+        parts = exchange(share.reshape(-1, width), "a")
+        parts = after(parts, piece_core, piece_both)
+        own = total_of(parts, sizes["a"])
         held_b, held_x = flip(own, "b"), flip(own, "x")
         held_both = flip(held_b, "x")
         held = [own, held_b, held_x, held_both]

time: 129 us -> 132 us (1.023)
  blocking collectives: 10.3 us -> 0 us
  waiting for transfers between devices: 29.6 us -> 39.3 us
  Pallas kernels: 52 us -> 54.1 us
    all_to_all x1 -> x0, blocking collectives: 10.3 us -> none  [exchange(): return lax.all_to_all(values, axes, split_axis=0, concat_axis=0, tiled=True)]
    all_to_all x4 -> x5, waiting for transfers between devices: 7.95 us -> 16.3 us  [exchange(): return lax.all_to_all(values, axes, split_axis=0, concat_axis=0, tiled=True)]
    pallas_call x15 -> x16, Pallas kernels: 52 us -> 54.1 us  [call(): pl.pallas_call(kernel, name=name, out_shape=outs, in_specs=specs, out_spe...]
    all_to_all x4 -> x5, starting transfers between devices: 24.9 us -> 26.3 us  [exchange(): return lax.all_to_all(values, axes, split_axis=0, concat_axis=0, tiled=True)]
  transfers between devices with their start and end apart: 27 -> 28, of which waited for: 15 -> 17; matrix products, arithmetic and copies ran while one was open for 0% -> 0% of each run, Pallas kernels for 32% -> 32%
where the time goes in v4:
time: 132 us; the launch traced here: 131 us
  Pallas kernels  54.1 us (41%)
  waiting for transfers between devices  39.3 us (30%)
  starting transfers between devices  36 us (27%)
    pallas_call x16, Pallas kernels, call(): pl.pallas_call(kernel, name=name, out_shape=outs, in_specs=specs, out_spe...  54.1 us
    all_to_all x5, starting transfers between devices, exchange(): return lax.all_to_all(values, axes, split_axis=0, concat_axis=0, tiled=True)  26.3 us
    ppermute x23, waiting for transfers between devices, flip(): lax.ppermute(values, axis, [(place, place ^ bit) for place in range(size)])  22.9 us
    all_to_all x5, waiting for transfers between devices, exchange(): return lax.all_to_all(values, axes, split_axis=0, concat_axis=0, tiled=True)  16.3 us
    ppermute x23, starting transfers between devices, flip(): lax.ppermute(values, axis, [(place, place ^ bit) for place in range(size)])  9.69 us
  transfers between devices with their start and end apart: 28, of which 17 were waited for; matrix products, arithmetic and copies ran while one was open for 0% of the time, Pallas kernels for 32%

profile of v4, /device:TPU:0, one launch (start us, length us, event | category | flops | bytes accessed | tf_op | source)
XLA Modules:
  0.0 131.0 jit_solution(15487467704791287274)
XLA Ops:
  0.7 2.3 %piece.1 = bf16[896,384]{1,0:T(8,128)(2,1)} custom-call(s32[3]{0:T(128)S(1)} %pad_add_fusion.spots, bf16[192,384]{1,0:T(8,128)(2,1)} %bitcast.57, bf16[192,384]{1,0:T(8,128)(2,1)} %second.1, bf16[192]{0:T(256)(128)(2,1)} %far_bias.1), custom_call_target="tpu_custom_call" | custom-call | flops 1100000000 | bytes 295308 | tf_op jit(solution)/shard_map/piece/pallas_call | solution.py:1135
  3.2 7.4 %all-to-all-start = ((bf16[8,112,384]{2,1,0:T(8,128)(2,1)}), bf16[8,112,384]{2,1,0:T(8,128)(2,1)S(1)}, u32[]{:S(2)}, u32[]{:S(2)}) async-start(bf16[8,112,384]{2,1,0:T(8,128)(2,1)} %bitcast.14), calls=%async_computation | async-start | bytes 1376256 | tf_op jit(solution)/shard_map/all_to_all | solution.py:31
  10.8 2.8 %entry.1 = (f32[96,384]{1,0:T(8,128)}, bf16[400,384]{1,0:T(8,128)(2,1)}, f32[400,384]{1,0:T(8,128)S(1)}, bf16[400,384]{1,0:T(8,128)(2,1)}, f32[400,384]{1,0:T(8,...) custom-call(bf16[1176,128]{1,0:T(8,128)(2,1)S(1)} %bitcast.56, ...), custom_call_target="tpu_custom_call" | custom-call | flops 5500000256 | bytes 1265672 | tf_op jit(solution)/shard_map/entry/pallas_call | solution.py:1135
  13.6 1.6 %collective-permute-start.4 = (bf16[400,384]{1,0:T(8,128)(2,1)}, bf16[400,384]{1,0:T(8,128)(2,1)S(1)}, u32[]{:S(2)}, u32[]{:S(2)}) collective-permute-start(bf16[400,384]{1,0:T(8,128)(2,1)} %get-tuple-element.113.refs_3_.refs_2_), channel_id=1, source_target_pairs={{0,16},{16,0},{1,17},{17,1},{2,18},{18,2},{3,19},{19,3},{4,20},{20... | collective-permute-start | bytes 921608 | tf_op jit(solution)/shard_map/ppermute | solution.py:27
  15.2 8.8 %modulation.1 = (f32[2240,128]{1,0:T(8,128)}, f32[400,512]{1,0:T(8,128)}, f32[400,384]{1,0:T(8,128)}, f32[1568,128]{1,0:T(8,128)}, f32[400,384]{1,0:T(8,128)}, /...) custom-call(f32[2240,128]{1,0:T(8,128)S(1)} %get-tuple-element.114.r, ...), custom_call_target="tpu_custom_call" | custom-call | flops 8800000000 | bytes 4734976 | tf_op jit(solution)/shard_map/modulation/pallas_call | solution.py:1135
  26.0 2.6 %all-to-all-done = bf16[8,112,384]{2,1,0:T(8,128)(2,1)S(1)} async-done(((bf16[8,112,384]{2,1,0:T(8,128)(2,1)}), bf16[8,112,384]{2,1,0:T(8,128)(2,1)S(1)}, u32[]{:S(2)}, u32[]{:S(2)}) %all-to-all-start) | async-done | bytes 688160 | tf_op jit(solution)/shard_map/all_to_all | solution.py:31
  28.6 4.1 %feed.2 = (bf16[400,384]{1,0:T(8,128)(2,1)S(1)}, bf16[400,384]{1,0:T(8,128)(2,1)S(1)}, bf16[400,384]{1,0:T(8,128)(2,1)S(1)}, bf16[400,384]{1,0:T(8,128)(2,1)S(1)...) custom-call(bf16[896,384]{1,0:T(8,128)(2,1)S(1)} %bitcast.50, bf16[400,384]{1,0:T(8,128)(2,1)} %get-tuple-element.120.refs_1_, ...), custom_call_target="tpu_custom_call" | custom-call | flops 6600000000 | bytes 1916928 | tf_op jit(solution)/shard_map/feed/pallas_call | solution.py:1135
  32.7 1.3 %collective-permute-done.refs_1_ = bf16[400,384]{1,0:T(8,128)(2,1)S(1)} collective-permute-done((bf16[400,384]{1,0:T(8,128)(2,1)}, bf16[400,384]{1,0:T(8,128)(2,1)S(1)}, u32[]{:S(2)}, u32[]{:S(2)}) %collective-permute-start) | collective-permute-done | bytes 307232 | tf_op jit(solution)/shard_map/ppermute | solution.py:27
  34.6 1.1 collective-permute-done.3.refs_2_
  36.5 5.0 %feed.3 = (bf16[400,384]{1,0:T(8,128)(2,1)S(1)}, bf16[400,384]{1,0:T(8,128)(2,1)S(1)}, bf16[800,384]{1,0:T(8,128)(2,1)S(1)}, f32[400,384]{1,0:T(8,128)}, f32[400...) custom-call(bf16[896,384]{1,0:T(8,128)(2,1)S(1)} %bitcast.51, ...), custom_call_target="tpu_custom_call" | custom-call | flops 6600000000 | bytes 4337664 | tf_op jit(solution)/shard_map/feed/pallas_call | solution.py:1135
  41.7 1.9 %collective-permute-done.8.refs_2_ = bf16[800,384]{1,0:T(8,128)(2,1)S(1)} collective-permute-done((bf16[800,384]{1,0:T(8,128)(2,1)S(1)}, bf16[800,384]{1,0:T(8,128)(2,1)S(1)}, u32[]{:S(2)}, u32[]{:S(2)}) %collective-permute-start.8) | collective-permute-done | bytes 614432 | tf_op jit(solution)/shard_map/ppermute | solution.py:27
  45.5 6.0 %all-to-all-start.1 = ((bf16[8,96,384]{2,1,0:T(8,128)(2,1)}), bf16[8,96,384]{2,1,0:T(8,128)(2,1)S(1)}, u32[]{:S(2)}, u32[]{:S(2)}) async-start(bf16[8,96,384]{2,1,0:T(8,128)(2,1)} %bitcast.17), calls=%async_computation.1 | async-start | bytes 1179648 | tf_op jit(solution)/shard_map/all_to_all | solution.py:31
  51.5 2.5 %collective-permute-done.9.refs_5_ = bf16[400,384]{1,0:T(8,128)(2,1)S(1)} collective-permute-done((bf16[400,384]{1,0:T(8,128)(2,1)S(1)}, bf16[400,384]{1,0:T(8,128)(2,1)S(1)}, u32[]{:S(2)}, u32[]{:S(2)}) %collective-permute-start.9) | collective-permute-done | bytes 307232 | tf_op jit(solution)/shard_map/ppermute | solution.py:27
  54.0 5.1 %heads.1 = (f32[400,384]{1,0:T(8,128)}, bf16[400,384]{1,0:T(8,128)(2,1)}, f32[400,384]{1,0:T(8,128)S(1)}, bf16[16,40,384]{2,1,0:T(8,128)(2,1)S(1)}, bf16[16,40,3...) custom-call(s32[1]{0:T(128)} %bitcast.refs_0_, ...), custom_call_target="tpu_custom_call" | custom-call | flops 5500000256 | bytes 11603972 | tf_op jit(solution)/shard_map/heads/pallas_call | solution.py:1135
  59.8 6.8 %levels_back.1 = (f32[2240,128]{1,0:T(8,128)}, f32[2240,128]{1,0:T(8,128)}, f32[2240,128]{1,0:T(8,128)}, bf16[400,384]{1,0:T(8,128)(2,1)}, bf16[400,128]{1,0:T(8,128)(2,1)}) custom-call(f32[96,384]{1,0:T(8,128)S(1)} %get-tuple-element.149.refs_0_, f32[400,512]{1,0:T(8,128)S(1)} %get-tuple-element.150.refs_1_, f32[400,384]{1,0:T(8,128)S(1)} %get-tuple-element.151.refs_2_, ...), custom_call_target="tpu_custom_call" | custom-call | flops 8800000000 | bytes 7438336 | tf_op jit(solution)/shard_map/levels_back/pallas_call | solution.py:1135
  67.7 4.1 %all-to-all-start.2 = ((bf16[4,160,384]{2,1,0:T(8,128)(2,1)}), bf16[4,160,384]{2,1,0:T(8,128)(2,1)S(1)}, u32[]{:S(2)}, u32[]{:S(2)}) async-start(bf16[4,160,384]{2,1,0:T(8,128)(2,1)} %bitcast.23), calls=%async_computation.2 | async-start | bytes 983040 | tf_op jit(solution)/shard_map/all_to_all | solution.py:31
  71.9 10.0 %exit.1 = (f32[400,384]{1,0:T(8,128)}, bf16[16,16,384]{2,1,0:T(8,128)(2,1)S(1)}, bf16[16,16,384]{2,1,0:T(8,128)(2,1)S(1)}) custom-call(s32[1]{0:T(128)} %bitcast.refs_0_, f32[2240,128]{1,0:T(8,128)} %get-tuple-element.146.refs_21_.refs_1_, f32[2240,128]{1,0:T(8,128)} %get-tuple-element.159.refs_2_, f32[2240,128]{1,0:T(8,128)} %get-tuple-element.145.refs_20_.refs_3_, ...), custom_call_target="tpu_custom_call" | custom-call | flops 9900000256 | bytes 8946692 | tf_op jit(solution)/shard_map/exit/pallas_call | solution.py:1135
  82.2 1.2 collective-permute-done.12.second
  84.2 4.2 %all-to-all-start.3 = ((bf16[4,64,384]{2,1,0:T(8,128)(2,1)}), bf16[4,64,384]{2,1,0:T(8,128)(2,1)S(1)}, u32[]{:S(2)}, u32[]{:S(2)}) async-start(bf16[4,64,384]{2,1,0:T(8,128)(2,1)} %bitcast.35), calls=%async_computation.3 | async-start | bytes 393216 | tf_op jit(solution)/shard_map/all_to_all | solution.py:31
  88.3 2.7 %finish.1 = (f32[1176,128]{1,0:T(8,128)}, f32[1176,128]{1,0:T(8,128)}) custom-call(f32[400,384]{1,0:T(8,128)} %get-tuple-element.148.refs_0_, f32[400,384]{1,0:T(8,128)} %get-tuple-element.180.refs_1_, f32[96,384]{1,0:T(8,128)} %get-tuple-element.112.refs_1_.refs_14_.refs_9_.refs_2_, f32[400,384]{1,0:T(8,128)} %get-tuple-element.119.refs_3_, ...), custom_call_target="tpu_custom_call" | custom-call | flops 3300000000 | bytes 2912256 | tf_op jit(solution)/shard_map/finish/pallas_call | solution.py:1135
  91.1 2.4 %all-to-all-done.3.late_parts = bf16[4,64,384]{2,1,0:T(8,128)(2,1)S(1)} async-done(((bf16[4,64,384]{2,1,0:T(8,128)(2,1)}), bf16[4,64,384]{2,1,0:T(8,128)(2,1)S(1)}, u32[]{:S(2)}, u32[]{:S(2)}) %all-to-all-start.3) | async-done | bytes 196640 | tf_op jit(solution)/shard_map/all_to_all | solution.py:31
  94.5 4.5 %all-to-all-start.4 = ((bf16[4,224,384]{2,1,0:T(8,128)(2,1)}), bf16[4,224,384]{2,1,0:T(8,128)(2,1)S(1)}, u32[]{:S(2)}, u32[]{:S(2)}) async-start(bf16[4,224,384]{2,1,0:T(8,128)(2,1)} %share.1), calls=%async_computation.4 | async-start | bytes 1376256 | tf_op jit(solution)/shard_map/all_to_all | solution.py:31
  99.0 1.1 collective-permute-start.13
  100.1 3.3 %collective-permute-done.13.piece_x = bf16[96,384]{1,0:T(8,128)(2,1)S(1)} collective-permute-done((bf16[96,384]{1,0:T(8,128)(2,1)S(1)}, bf16[96,384]{1,0:T(8,128)(2,1)S(1)}, u32[]{:S(2)}, u32[]{:S(2)}) %collective-permute-start.13) | collective-permute-done | bytes 73760 | tf_op jit(solution)/shard_map/ppermute | solution.py:27
  103.4 1.3 collective-permute-done.15.piece_both
  104.6 11.3 %all-to-all-done.4 = bf16[4,224,384]{2,1,0:T(8,128)(2,1)S(1)} async-done(((bf16[4,224,384]{2,1,0:T(8,128)(2,1)}), bf16[4,224,384]{2,1,0:T(8,128)(2,1)S(1)}, u32[]{:S(2)}, u32[]{:S(2)}) %all-to-all-start.4) | async-done | bytes 688160 | tf_op jit(solution)/shard_map/all_to_all | solution.py:31
  116.1 1.1 collective-permute-start.16
  118.1 3.5 %collective-permute-done.16.own_b = bf16[224,384]{1,0:T(8,128)(2,1)S(1)} collective-permute-done((bf16[224,384]{1,0:T(8,128)(2,1)S(1)}, bf16[224,384]{1,0:T(8,128)(2,1)S(1)}, u32[]{:S(2)}, u32[]{:S(2)}) %collective-permute-start.16) | collective-permute-done | bytes 172064 | tf_op jit(solution)/shard_map/ppermute | solution.py:27
  121.6 1.2 collective-permute-start.18
  123.3 3.7 %collective-permute-done.18.own_both = bf16[224,384]{1,0:T(8,128)(2,1)S(1)} collective-permute-done((bf16[224,384]{1,0:T(8,128)(2,1)S(1)}, bf16[224,384]{1,0:T(8,128)(2,1)S(1)}, u32[]{:S(2)}, u32[]{:S(2)}) %collective-permute-start.18) | collective-permute-done | bytes 172064 | tf_op jit(solution)/shard_map/ppermute | solution.py:27
  127.1 1.3 collective-permute-done.22.core_both
  128.4 2.4 %unpack.1 = (f32[384]{0:T(512)}, f32[384]{0:T(512)}, f32[772,384]{1,0:T(8,128)}, f32[772]{0:T(1024)}, f32[9,384]{1,0:T(8,128)}, /*index=5*/f32[25,384]{1,0:T(8,1...) custom-call(s32[5]{0:T(128)S(1)} %stack.32.spots, ...), custom_call_target="tpu_custom_call" | custom-call | flops 2200000000 | bytes 1671188 | tf_op jit(solution)/shard_map/unpack/pallas_call | solution.py:1135
  (76 shorter events, 10.9 us)
Async XLA Ops:
  3.0 7.6 %copy-start = (bf16[384,772]{0,1:T(8,128)(2,1)S(1)}, bf16[384,772]{0,1:T(8,128)(2,1)}, u32[]{:S(2)}) copy-start(bf16[384,772]{0,1:T(8,128)(2,1)} %param.22) | copy-start | bytes 1778692
  3.0 7.6 %copy-start.1 = (bf16[2,14,14,384]{3,0,2,1:T(2,128)(2,1)S(1)}, bf16[2,14,14,384]{3,0,2,1:T(2,128)(2,1)}, u32[]{:S(2)}) copy-start(bf16[2,14,14,384]{3,0,2,1:T(2,128)(2,1)} %param.37) | copy-start | bytes 903172
  3.1 7.6 %copy-start.2 = (bf16[2,14,14,384]{3,0,2,1:T(2,128)(2,1)S(1)}, bf16[2,14,14,384]{3,0,2,1:T(2,128)(2,1)}, u32[]{:S(2)}) copy-start(bf16[2,14,14,384]{3,0,2,1:T(2,128)(2,1)} %param.19) | copy-start | bytes 903172
  3.1 7.6 %copy-start.3 = (bf16[49,384]{1,0:T(8,128)(2,1)S(1)}, bf16[49,384]{1,0:T(8,128)(2,1)}, u32[]{:S(2)}) copy-start(bf16[49,384]{1,0:T(8,128)(2,1)} %refs_5_.1) | copy-start | bytes 112900
  3.2 25.4 %all-to-all-start = ((bf16[8,112,384]{2,1,0:T(8,128)(2,1)}), bf16[8,112,384]{2,1,0:T(8,128)(2,1)S(1)}, u32[]{:S(2)}, u32[]{:S(2)}) async-start(bf16[8,112,384]{2,1,0:T(8,128)(2,1)} %bitcast.14), calls=%async_computation | async-start | bytes 1376256 | tf_op jit(solution)/shard_map/all_to_all | solution.py:31
  13.6 11.5 %collective-permute-start.4 = (bf16[400,384]{1,0:T(8,128)(2,1)}, bf16[400,384]{1,0:T(8,128)(2,1)S(1)}, u32[]{:S(2)}, u32[]{:S(2)}) collective-permute-start(bf16[400,384]{1,0:T(8,128)(2,1)} %get-tuple-element.113.refs_3_.refs_2_), channel_id=1, source_target_pairs={{0,16},{16,0},{1,17},{17,1},{2,18},{18,2},{3,19},{19,3},{4,20},{20... | collective-permute-start | bytes 921608 | tf_op jit(solution)/shard_map/ppermute | solution.py:27
  15.1 10.0 %collective-permute-start.2 = (bf16[400,384]{1,0:T(8,128)(2,1)}, bf16[400,384]{1,0:T(8,128)(2,1)S(1)}, u32[]{:S(2)}, u32[]{:S(2)}) collective-permute-start(bf16[400,384]{1,0:T(8,128)(2,1)} %get-tuple-element.113.refs_3_.refs_2_), channel_id=1, source_target_pairs={{0,8},{8,0},{1,9},{9,1},{2,10},{10,2},{3,11},{11,3},{4,12},{12,4},... | collective-permute-start | bytes 921608 | tf_op jit(solution)/shard_map/ppermute | solution.py:27
  24.0 2.0 %collective-permute-start.1 = (bf16[400,384]{1,0:T(8,128)(2,1)}, bf16[400,384]{1,0:T(8,128)(2,1)S(1)}, u32[]{:S(2)}, u32[]{:S(2)}) collective-permute-start(bf16[400,384]{1,0:T(8,128)(2,1)} %get-tuple-element.120.refs_1_), channel_id=1, source_target_pairs={{0,8},{8,0},{1,9},{9,1},{2,10},{10,2},{3,11},{11,3},{4,12},{12,4},... | collective-permute-start | bytes 921608 | tf_op jit(solution)/shard_map/ppermute | solution.py:27
  24.6 9.5 %collective-permute-start = (bf16[400,384]{1,0:T(8,128)(2,1)}, bf16[400,384]{1,0:T(8,128)(2,1)S(1)}, u32[]{:S(2)}, u32[]{:S(2)}) collective-permute-start(bf16[400,384]{1,0:T(8,128)(2,1)} %get-tuple-element.120.refs_1_), channel_id=1, source_target_pairs={{0,16},{16,0},{1,17},{17,1},{2,18},{18,2},{3,19},{19,3},{4,20},{20... | collective-permute-start | bytes 921608 | tf_op jit(solution)/shard_map/ppermute | solution.py:27
  25.1 9.4 %collective-permute-start.5 = (bf16[400,384]{1,0:T(8,128)(2,1)S(1)}, bf16[400,384]{1,0:T(8,128)(2,1)S(1)}, u32[]{:S(2)}, u32[]{:S(2)}) collective-permute-start(bf16[400,384]{1,0:T(8,128)(2,1)S(1)} %collective-permute-done.4.refs_3_), channel_id=1, source_target_pairs={{0,8},{8,0},{1,9},{9,1},{2,10},{10,2},{3,11},{11,3},{4,12},{12,4},... | collective-permute-start | bytes 921608 | tf_op jit(solution)/shard_map/ppermute | solution.py:27
  34.0 1.6 %collective-permute-start.3 = (bf16[400,384]{1,0:T(8,128)(2,1)S(1)}, bf16[400,384]{1,0:T(8,128)(2,1)S(1)}, u32[]{:S(2)}, u32[]{:S(2)}) collective-permute-start(bf16[400,384]{1,0:T(8,128)(2,1)S(1)} %collective-permute-done.refs_1_), channel_id=1, source_target_pairs={{0,8},{8,0},{1,9},{9,1},{2,10},{10,2},{3,11},{11,3},{4,12},{12,4},... | collective-permute-start | bytes 921608 | tf_op jit(solution)/shard_map/ppermute | solution.py:27
  34.1 2.0 %collective-permute-start.6 = (bf16[400,384]{1,0:T(8,128)(2,1)S(1)}, bf16[400,384]{1,0:T(8,128)(2,1)S(1)}, u32[]{:S(2)}, u32[]{:S(2)}) collective-permute-start(bf16[400,384]{1,0:T(8,128)(2,1)S(1)} %get-tuple-element.126), channel_id=1, source_target_pairs={{0,8},{8,0},{1,9},{9,1},{2,10},{10,2},{3,11},{11,3},{4,12},{12,4},... | collective-permute-start | bytes 921608 | tf_op jit(solution)/shard_map/ppermute | solution.py:27
  34.6 2.0 %collective-permute-start.7 = (bf16[400,384]{1,0:T(8,128)(2,1)S(1)}, bf16[400,384]{1,0:T(8,128)(2,1)S(1)}, u32[]{:S(2)}, u32[]{:S(2)}) collective-permute-start(bf16[400,384]{1,0:T(8,128)(2,1)S(1)} %get-tuple-element.128), channel_id=1, source_target_pairs={{0,8},{8,0},{1,9},{9,1},{2,10},{10,2},{3,11},{11,3},{4,12},{12,4},... | collective-permute-start | bytes 921608 | tf_op jit(solution)/shard_map/ppermute | solution.py:27
  41.5 2.1 %collective-permute-start.8 = (bf16[800,384]{1,0:T(8,128)(2,1)S(1)}, bf16[800,384]{1,0:T(8,128)(2,1)S(1)}, u32[]{:S(2)}, u32[]{:S(2)}) collective-permute-start(bf16[800,384]{1,0:T(8,128)(2,1)S(1)} %get-tuple-element.132), channel_id=1, source_target_pairs={{0,8},{8,0},{1,9},{9,1},{2,10},{10,2},{3,11},{11,3},{4,12},{12,4},... | collective-permute-start | bytes 1843208 | tf_op jit(solution)/shard_map/ppermute | solution.py:27
  44.7 9.4 %collective-permute-start.9 = (bf16[400,384]{1,0:T(8,128)(2,1)S(1)}, bf16[400,384]{1,0:T(8,128)(2,1)S(1)}, u32[]{:S(2)}, u32[]{:S(2)}) collective-permute-start(bf16[400,384]{1,0:T(8,128)(2,1)S(1)} %get-tuple-element.133), channel_id=1, source_target_pairs={{0,16},{16,0},{1,17},{17,1},{2,18},{18,2},{3,19},{19,3},{4,20},{20... | collective-permute-start | bytes 921608 | tf_op jit(solution)/shard_map/ppermute | solution.py:27
  45.5 22.0 %all-to-all-start.1 = ((bf16[8,96,384]{2,1,0:T(8,128)(2,1)}), bf16[8,96,384]{2,1,0:T(8,128)(2,1)S(1)}, u32[]{:S(2)}, u32[]{:S(2)}) async-start(bf16[8,96,384]{2,1,0:T(8,128)(2,1)} %bitcast.17), calls=%async_computation.1 | async-start | bytes 1179648 | tf_op jit(solution)/shard_map/all_to_all | solution.py:31
  59.2 8.6 %collective-permute-start.11 = (bf16[400,384]{1,0:T(8,128)(2,1)S(1)}, bf16[400,384]{1,0:T(8,128)(2,1)S(1)}, u32[]{:S(2)}, u32[]{:S(2)}) collective-permute-start(bf16[400,384]{1,0:T(8,128)(2,1)S(1)} %copy-done.14), channel_id=1, source_target_pairs={{0,16},{16,0},{1,17},{17,1},{2,18},{18,2},{3,19},{19,3},{4,20},{20... | collective-permute-start | bytes 921608 | tf_op jit(solution)/shard_map/ppermute | solution.py:27
  59.8 6.8 %collective-permute-start.10 = (bf16[16,40,384]{2,1,0:T(8,128)(2,1)S(1)}, bf16[16,40,384]{2,1,0:T(8,128)(2,1)S(1)}, u32[]{:S(2)}, u32[]{:S(2)}) collective-permute-start(bf16[16,40,384]{2,1,0:T(8,128)(2,1)S(1)} %get-tuple-element.164), channel_id=1, source_target_pairs={{0,8},{8,0},{1,9},{9,1},{2,10},{10,2},{3,11},{11,3},{4,12},{12,4},... | collective-permute-start | bytes 1474568 | tf_op jit(solution)/shard_map/ppermute | solution.py:27
  67.7 16.4 %all-to-all-start.2 = ((bf16[4,160,384]{2,1,0:T(8,128)(2,1)}), bf16[4,160,384]{2,1,0:T(8,128)(2,1)S(1)}, u32[]{:S(2)}, u32[]{:S(2)}) async-start(bf16[4,160,384]{2,1,0:T(8,128)(2,1)} %bitcast.23), calls=%async_computation.2 | async-start | bytes 983040 | tf_op jit(solution)/shard_map/all_to_all | solution.py:31
  81.9 1.5 %collective-permute-start.12 = (bf16[16,16,384]{2,1,0:T(8,128)(2,1)S(1)}, bf16[16,16,384]{2,1,0:T(8,128)(2,1)S(1)}, u32[]{:S(2)}, u32[]{:S(2)}) collective-permute-start(bf16[16,16,384]{2,1,0:T(8,128)(2,1)S(1)} %get-tuple-element.177), channel_id=1, source_target_pairs={{0,8},{8,0},{1,9},{9,1},{2,10},{10,2},{3,11},{11,3},{4,12},{12,4},... | collective-permute-start | bytes 589832 | tf_op jit(solution)/shard_map/ppermute | solution.py:27
  84.2 9.4 %all-to-all-start.3 = ((bf16[4,64,384]{2,1,0:T(8,128)(2,1)}), bf16[4,64,384]{2,1,0:T(8,128)(2,1)S(1)}, u32[]{:S(2)}, u32[]{:S(2)}) async-start(bf16[4,64,384]{2,1,0:T(8,128)(2,1)} %bitcast.35), calls=%async_computation.3 | async-start | bytes 393216 | tf_op jit(solution)/shard_map/all_to_all | solution.py:31
  94.5 21.4 %all-to-all-start.4 = ((bf16[4,224,384]{2,1,0:T(8,128)(2,1)}), bf16[4,224,384]{2,1,0:T(8,128)(2,1)S(1)}, u32[]{:S(2)}, u32[]{:S(2)}) async-start(bf16[4,224,384]{2,1,0:T(8,128)(2,1)} %share.1), calls=%async_computation.4 | async-start | bytes 1376256 | tf_op jit(solution)/shard_map/all_to_all | solution.py:31
  99.0 4.4 %collective-permute-start.13 = (bf16[96,384]{1,0:T(8,128)(2,1)S(1)}, bf16[96,384]{1,0:T(8,128)(2,1)S(1)}, u32[]{:S(2)}, u32[]{:S(2)}) collective-permute-start(bf16[96,384]{1,0:T(8,128)(2,1)S(1)} %sum.2.piece), channel_id=1, source_target_pairs={{0,16},{16,0},{1,17},{17,1},{2,18},{18,2},{3,19},{19,3},{4,20},{20... | collective-permute-start | bytes 221192 | tf_op jit(solution)/shard_map/ppermute | solution.py:27
  100.1 3.3 %collective-permute-start.14 = (bf16[96,384]{1,0:T(8,128)(2,1)S(1)}, bf16[96,384]{1,0:T(8,128)(2,1)S(1)}, u32[]{:S(2)}, u32[]{:S(2)}) collective-permute-start(bf16[96,384]{1,0:T(8,128)(2,1)S(1)} %sum.2.piece), channel_id=1, source_target_pairs={{0,8},{8,0},{1,9},{9,1},{2,10},{10,2},{3,11},{11,3},{4,12},{12,4},... | collective-permute-start | bytes 221192 | tf_op jit(solution)/shard_map/ppermute | solution.py:27
  103.4 1.3 collective-permute-start.15
  116.1 5.5 %collective-permute-start.16 = (bf16[224,384]{1,0:T(8,128)(2,1)S(1)}, bf16[224,384]{1,0:T(8,128)(2,1)S(1)}, u32[]{:S(2)}, u32[]{:S(2)}) collective-permute-start(bf16[224,384]{1,0:T(8,128)(2,1)S(1)} %sum.3.own), channel_id=1, source_target_pairs={{0,1},{1,0},{2,3},{3,2},{4,5},{5,4},{6,7},{7,6},{8,9},{9,8},{10,11... | collective-permute-start | bytes 516104 | tf_op jit(solution)/shard_map/ppermute | solution.py:27
  117.2 6.1 %collective-permute-start.17 = (bf16[224,384]{1,0:T(8,128)(2,1)S(1)}, bf16[224,384]{1,0:T(8,128)(2,1)S(1)}, u32[]{:S(2)}, u32[]{:S(2)}) collective-permute-start(bf16[224,384]{1,0:T(8,128)(2,1)S(1)} %sum.3.own), channel_id=1, source_target_pairs={{0,16},{16,0},{1,17},{17,1},{2,18},{18,2},{3,19},{19,3},{4,20},{20... | collective-permute-start | bytes 516104 | tf_op jit(solution)/shard_map/ppermute | solution.py:27
  121.6 5.4 %collective-permute-start.18 = (bf16[224,384]{1,0:T(8,128)(2,1)S(1)}, bf16[224,384]{1,0:T(8,128)(2,1)S(1)}, u32[]{:S(2)}, u32[]{:S(2)}) collective-permute-start(bf16[224,384]{1,0:T(8,128)(2,1)S(1)} %collective-permute-done.16.own_b), channel_id=1, source_target_pairs={{0,16},{16,0},{1,17},{17,1},{2,18},{18,2},{3,19},{19,3},{4,20},{20... | collective-permute-start | bytes 516104 | tf_op jit(solution)/shard_map/ppermute | solution.py:27
  122.8 4.3 %collective-permute-start.19 = (bf16[224,384]{1,0:T(8,128)(2,1)S(1)}, bf16[224,384]{1,0:T(8,128)(2,1)S(1)}, u32[]{:S(2)}, u32[]{:S(2)}) collective-permute-start(bf16[224,384]{1,0:T(8,128)(2,1)S(1)} %sum.3.own), channel_id=1, source_target_pairs={{0,8},{8,0},{1,9},{9,1},{2,10},{10,2},{3,11},{11,3},{4,12},{12,4},... | collective-permute-start | bytes 516104 | tf_op jit(solution)/shard_map/ppermute | solution.py:27
  122.8 4.3 %collective-permute-start.20 = (bf16[224,384]{1,0:T(8,128)(2,1)S(1)}, bf16[224,384]{1,0:T(8,128)(2,1)S(1)}, u32[]{:S(2)}, u32[]{:S(2)}) collective-permute-start(bf16[224,384]{1,0:T(8,128)(2,1)S(1)} %collective-permute-done.16.own_b), channel_id=1, source_target_pairs={{0,8},{8,0},{1,9},{9,1},{2,10},{10,2},{3,11},{11,3},{4,12},{12,4},... | collective-permute-start | bytes 516104 | tf_op jit(solution)/shard_map/ppermute | solution.py:27
  123.3 3.8 %collective-permute-start.21 = (bf16[224,384]{1,0:T(8,128)(2,1)S(1)}, bf16[224,384]{1,0:T(8,128)(2,1)S(1)}, u32[]{:S(2)}, u32[]{:S(2)}) collective-permute-start(bf16[224,384]{1,0:T(8,128)(2,1)S(1)} %collective-permute-done.17.own_x), channel_id=1, source_target_pairs={{0,8},{8,0},{1,9},{9,1},{2,10},{10,2},{3,11},{11,3},{4,12},{12,4},... | collective-permute-start | bytes 516104 | tf_op jit(solution)/shard_map/ppermute | solution.py:27
  127.0 1.4 %collective-permute-start.22 = (bf16[224,384]{1,0:T(8,128)(2,1)S(1)}, bf16[224,384]{1,0:T(8,128)(2,1)S(1)}, u32[]{:S(2)}, u32[]{:S(2)}) collective-permute-start(bf16[224,384]{1,0:T(8,128)(2,1)S(1)} %collective-permute-done.18.own_both), channel_id=1, source_target_pairs={{0,8},{8,0},{1,9},{9,1},{2,10},{10,2},{3,11},{11,3},{4,12},{12,4},... | collective-permute-start | bytes 516104 | tf_op jit(solution)/shard_map/ppermute | solution.py:27
  (11 other events, 80.9 us)

commit v5 on v4

--- a/solution.py
+++ b/solution.py
@@ -523,9 +523,11 @@
         for part in range(1, parts.shape[0]):
             total = total + parts[part].astype(f32)
         sums.append(total)
-    share = jnp.concatenate(sums).astype(bf16)
-    for copy in range(out.shape[0]):
-        out[copy] = share
+    out[...] = jnp.concatenate(sums).astype(bf16)
+
+
+def add_kernel(first, second, out):
+    out[...] = (first[...].astype(f32) + second[...].astype(f32)).astype(bf16)
 
 
 def piece_kernel(units, copies, spots, first, second, far_bias, out, own, bias, semaphores):
@@ -1146,7 +1148,7 @@
     )(*operands)
 
 
-plain = ("piece", "sum", "pair", "share", "unpack")
+plain = ("piece", "sum", "pair", "share", "add", "unpack")
 
 
 class Far:
@@ -1584,7 +1586,7 @@
         (share,) = call(
             share_kernel,
             "share",
-            [array(sizes["a"], share_rows, width, kind=bf16)],
+            [array(share_rows, width, kind=bf16)],
             [],
             1,
             8,
@@ -1594,9 +1596,14 @@
         piece = after(piece, share)
         piece_x = flip(piece, "x")
         piece_core, piece_both = flip(piece), flip(piece_x)
-        parts = exchange(share.reshape(-1, width), "a")
-        parts = after(parts, piece_core, piece_both)
-        own = total_of(parts, sizes["a"])
+        own = share
+        for bit in (1, 2):
+            arrived = flip(own, "a", sizes["a"], bit)
+            if bit == 2:
+                arrived = after(arrived, piece_core, piece_both)
+            (own,) = call(
+                add_kernel, "add", [array(share_rows, width, kind=bf16)], [], 1, 6, own, arrived
+            )
         held_b, held_x = flip(own, "b"), flip(own, "x")
         held_both = flip(held_b, "x")
         held = [own, held_b, held_x, held_both]

time: 132 us -> 124 us (0.939)
  waiting for transfers between devices: 39.3 us -> 33.1 us
    all_to_all x5 -> x4, waiting for transfers between devices: 16.3 us -> 5.05 us  [exchange(): return lax.all_to_all(values, axes, split_axis=0, concat_axis=0, tiled=True)]
    ppermute x23 -> x25, waiting for transfers between devices: 22.9 us -> 28 us  [flip(): lax.ppermute(values, axis, [(place, place ^ bit) for place in range(size)])]
    all_to_all x5 -> x4, starting transfers between devices: 26.3 us -> 21.7 us  [exchange(): return lax.all_to_all(values, axes, split_axis=0, concat_axis=0, tiled=True)]
    ppermute x23 -> x25, starting transfers between devices: 9.69 us -> 13.5 us  [flip(): lax.ppermute(values, axis, [(place, place ^ bit) for place in range(size)])]
    pallas_call x16 -> x17, Pallas kernels: 54.1 us -> 53.1 us  [call(): pl.pallas_call(kernel, name=name, out_shape=outs, in_specs=specs, out_spe...]
  transfers between devices with their start and end apart: 28 -> 29, of which waited for: 17 -> 18; matrix products, arithmetic and copies ran while one was open for 0% -> 0% of each run, Pallas kernels for 32% -> 34%
where the time goes in v5:
time: 124 us; the launch traced here: 123 us
  Pallas kernels  53.1 us (43%)
  starting transfers between devices  35.3 us (28%)
  waiting for transfers between devices  33.1 us (27%)
    pallas_call x17, Pallas kernels, call(): pl.pallas_call(kernel, name=name, out_shape=outs, in_specs=specs, out_spe...  53.1 us
    ppermute x25, waiting for transfers between devices, flip(): lax.ppermute(values, axis, [(place, place ^ bit) for place in range(size)])  28 us
    all_to_all x4, starting transfers between devices, exchange(): return lax.all_to_all(values, axes, split_axis=0, concat_axis=0, tiled=True)  21.7 us
    ppermute x25, starting transfers between devices, flip(): lax.ppermute(values, axis, [(place, place ^ bit) for place in range(size)])  13.5 us
    all_to_all x4, waiting for transfers between devices, exchange(): return lax.all_to_all(values, axes, split_axis=0, concat_axis=0, tiled=True)  5.05 us
  transfers between devices with their start and end apart: 29, of which 18 were waited for; matrix products, arithmetic and copies ran while one was open for 0% of the time, Pallas kernels for 34%

profile of v5, /device:TPU:0, one launch (start us, length us, event | category | flops | bytes accessed | tf_op | source)
XLA Modules:
  0.0 123.2 jit_solution(6911402678001678473)
XLA Ops:
  0.7 2.3 %piece.1 = bf16[896,384]{1,0:T(8,128)(2,1)} custom-call(s32[3]{0:T(128)S(1)} %pad_add_fusion.spots, bf16[192,384]{1,0:T(8,128)(2,1)} %bitcast.55, bf16[192,384]{1,0:T(8,128)(2,1)} %second.1, bf16[192]{0:T(256)(128)(2,1)} %far_bias.1), custom_call_target="tpu_custom_call" | custom-call | flops 1100000000 | bytes 295308 | tf_op jit(solution)/shard_map/piece/pallas_call | solution.py:1137
  3.2 7.4 %all-to-all-start = ((bf16[8,112,384]{2,1,0:T(8,128)(2,1)}), bf16[8,112,384]{2,1,0:T(8,128)(2,1)S(1)}, u32[]{:S(2)}, u32[]{:S(2)}) async-start(bf16[8,112,384]{2,1,0:T(8,128)(2,1)} %bitcast.14), calls=%async_computation | async-start | bytes 1376256 | tf_op jit(solution)/shard_map/all_to_all | solution.py:31
  10.8 2.8 %entry.1 = (f32[96,384]{1,0:T(8,128)}, bf16[400,384]{1,0:T(8,128)(2,1)}, f32[400,384]{1,0:T(8,128)S(1)}, bf16[400,384]{1,0:T(8,128)(2,1)}, f32[400,384]{1,0:T(8,...) custom-call(bf16[1176,128]{1,0:T(8,128)(2,1)S(1)} %bitcast.54, ...), custom_call_target="tpu_custom_call" | custom-call | flops 5500000256 | bytes 1265672 | tf_op jit(solution)/shard_map/entry/pallas_call | solution.py:1137
  13.6 1.6 %collective-permute-start.4 = (bf16[400,384]{1,0:T(8,128)(2,1)}, bf16[400,384]{1,0:T(8,128)(2,1)S(1)}, u32[]{:S(2)}, u32[]{:S(2)}) collective-permute-start(bf16[400,384]{1,0:T(8,128)(2,1)} %get-tuple-element.113.refs_3_.refs_2_), channel_id=1, source_target_pairs={{0,16},{16,0},{1,17},{17,1},{2,18},{18,2},{3,19},{19,3},{4,20},{20... | collective-permute-start | bytes 921608 | tf_op jit(solution)/shard_map/ppermute | solution.py:27
  15.2 8.8 %modulation.1 = (f32[2240,128]{1,0:T(8,128)}, f32[400,512]{1,0:T(8,128)}, f32[400,384]{1,0:T(8,128)}, f32[1568,128]{1,0:T(8,128)}, f32[400,384]{1,0:T(8,128)}, /...) custom-call(f32[2240,128]{1,0:T(8,128)S(1)} %get-tuple-element.114.r, ...), custom_call_target="tpu_custom_call" | custom-call | flops 8800000000 | bytes 4734976 | tf_op jit(solution)/shard_map/modulation/pallas_call | solution.py:1137
  26.0 2.6 %all-to-all-done = bf16[8,112,384]{2,1,0:T(8,128)(2,1)S(1)} async-done(((bf16[8,112,384]{2,1,0:T(8,128)(2,1)}), bf16[8,112,384]{2,1,0:T(8,128)(2,1)S(1)}, u32[]{:S(2)}, u32[]{:S(2)}) %all-to-all-start) | async-done | bytes 688160 | tf_op jit(solution)/shard_map/all_to_all | solution.py:31
  28.6 4.1 %feed.2 = (bf16[400,384]{1,0:T(8,128)(2,1)S(1)}, bf16[400,384]{1,0:T(8,128)(2,1)S(1)}, bf16[400,384]{1,0:T(8,128)(2,1)S(1)}, bf16[400,384]{1,0:T(8,128)(2,1)S(1)...) custom-call(bf16[896,384]{1,0:T(8,128)(2,1)S(1)} %bitcast.48, bf16[400,384]{1,0:T(8,128)(2,1)} %get-tuple-element.120.refs_1_, ...), custom_call_target="tpu_custom_call" | custom-call | flops 6600000000 | bytes 1916928 | tf_op jit(solution)/shard_map/feed/pallas_call | solution.py:1137
  32.7 1.3 %collective-permute-done.refs_1_ = bf16[400,384]{1,0:T(8,128)(2,1)S(1)} collective-permute-done((bf16[400,384]{1,0:T(8,128)(2,1)}, bf16[400,384]{1,0:T(8,128)(2,1)S(1)}, u32[]{:S(2)}, u32[]{:S(2)}) %collective-permute-start) | collective-permute-done | bytes 307232 | tf_op jit(solution)/shard_map/ppermute | solution.py:27
  36.5 5.0 %feed.3 = (bf16[400,384]{1,0:T(8,128)(2,1)S(1)}, bf16[400,384]{1,0:T(8,128)(2,1)S(1)}, bf16[800,384]{1,0:T(8,128)(2,1)S(1)}, f32[400,384]{1,0:T(8,128)}, f32[400...) custom-call(bf16[896,384]{1,0:T(8,128)(2,1)S(1)} %bitcast.49, ...), custom_call_target="tpu_custom_call" | custom-call | flops 6600000000 | bytes 4337664 | tf_op jit(solution)/shard_map/feed/pallas_call | solution.py:1137
  41.7 1.9 %collective-permute-done.8.refs_2_ = bf16[800,384]{1,0:T(8,128)(2,1)S(1)} collective-permute-done((bf16[800,384]{1,0:T(8,128)(2,1)S(1)}, bf16[800,384]{1,0:T(8,128)(2,1)S(1)}, u32[]{:S(2)}, u32[]{:S(2)}) %collective-permute-start.8) | collective-permute-done | bytes 614432 | tf_op jit(solution)/shard_map/ppermute | solution.py:27
  45.5 6.0 %all-to-all-start.1 = ((bf16[8,96,384]{2,1,0:T(8,128)(2,1)}), bf16[8,96,384]{2,1,0:T(8,128)(2,1)S(1)}, u32[]{:S(2)}, u32[]{:S(2)}) async-start(bf16[8,96,384]{2,1,0:T(8,128)(2,1)} %bitcast.17), calls=%async_computation.1 | async-start | bytes 1179648 | tf_op jit(solution)/shard_map/all_to_all | solution.py:31
  51.5 2.5 %collective-permute-done.9.refs_5_ = bf16[400,384]{1,0:T(8,128)(2,1)S(1)} collective-permute-done((bf16[400,384]{1,0:T(8,128)(2,1)S(1)}, bf16[400,384]{1,0:T(8,128)(2,1)S(1)}, u32[]{:S(2)}, u32[]{:S(2)}) %collective-permute-start.9) | collective-permute-done | bytes 307232 | tf_op jit(solution)/shard_map/ppermute | solution.py:27
  54.0 5.1 %heads.1 = (f32[400,384]{1,0:T(8,128)}, bf16[400,384]{1,0:T(8,128)(2,1)}, f32[400,384]{1,0:T(8,128)S(1)}, bf16[16,40,384]{2,1,0:T(8,128)(2,1)S(1)}, bf16[16,40,3...) custom-call(s32[1]{0:T(128)} %bitcast.refs_0_, ...), custom_call_target="tpu_custom_call" | custom-call | flops 5500000256 | bytes 11603972 | tf_op jit(solution)/shard_map/heads/pallas_call | solution.py:1137
  59.8 6.8 %levels_back.1 = (f32[2240,128]{1,0:T(8,128)}, f32[2240,128]{1,0:T(8,128)}, f32[2240,128]{1,0:T(8,128)}, bf16[400,384]{1,0:T(8,128)(2,1)}, bf16[400,128]{1,0:T(8,128)(2,1)}) custom-call(f32[96,384]{1,0:T(8,128)S(1)} %get-tuple-element.149.refs_0_, f32[400,512]{1,0:T(8,128)S(1)} %get-tuple-element.150.refs_1_, f32[400,384]{1,0:T(8,128)S(1)} %get-tuple-element.151.refs_2_, ...), custom_call_target="tpu_custom_call" | custom-call | flops 8800000000 | bytes 7438336 | tf_op jit(solution)/shard_map/levels_back/pallas_call | solution.py:1137
  67.7 4.1 %all-to-all-start.2 = ((bf16[4,160,384]{2,1,0:T(8,128)(2,1)}), bf16[4,160,384]{2,1,0:T(8,128)(2,1)S(1)}, u32[]{:S(2)}, u32[]{:S(2)}) async-start(bf16[4,160,384]{2,1,0:T(8,128)(2,1)} %bitcast.23), calls=%async_computation.2 | async-start | bytes 983040 | tf_op jit(solution)/shard_map/all_to_all | solution.py:31
  71.9 10.0 %exit.1 = (f32[400,384]{1,0:T(8,128)}, bf16[16,16,384]{2,1,0:T(8,128)(2,1)S(1)}, bf16[16,16,384]{2,1,0:T(8,128)(2,1)S(1)}) custom-call(s32[1]{0:T(128)} %bitcast.refs_0_, f32[2240,128]{1,0:T(8,128)} %get-tuple-element.146.refs_21_.refs_1_, f32[2240,128]{1,0:T(8,128)} %get-tuple-element.159.refs_2_, f32[2240,128]{1,0:T(8,128)} %get-tuple-element.145.refs_20_.refs_3_, ...), custom_call_target="tpu_custom_call" | custom-call | flops 9900000256 | bytes 8946692 | tf_op jit(solution)/shard_map/exit/pallas_call | solution.py:1137
  82.2 1.2 collective-permute-done.12.second
  84.2 4.2 %all-to-all-start.3 = ((bf16[4,64,384]{2,1,0:T(8,128)(2,1)}), bf16[4,64,384]{2,1,0:T(8,128)(2,1)S(1)}, u32[]{:S(2)}, u32[]{:S(2)}) async-start(bf16[4,64,384]{2,1,0:T(8,128)(2,1)} %bitcast.35), calls=%async_computation.3 | async-start | bytes 393216 | tf_op jit(solution)/shard_map/all_to_all | solution.py:31
  88.3 2.7 %finish.1 = (f32[1176,128]{1,0:T(8,128)}, f32[1176,128]{1,0:T(8,128)}) custom-call(f32[400,384]{1,0:T(8,128)} %get-tuple-element.148.refs_0_, f32[400,384]{1,0:T(8,128)} %get-tuple-element.180.refs_1_, f32[96,384]{1,0:T(8,128)} %get-tuple-element.112.refs_1_.refs_14_.refs_9_.refs_2_, f32[400,384]{1,0:T(8,128)} %get-tuple-element.119.refs_3_, ...), custom_call_target="tpu_custom_call" | custom-call | flops 3300000000 | bytes 2912256 | tf_op jit(solution)/shard_map/finish/pallas_call | solution.py:1137
  91.1 2.4 %all-to-all-done.3.late_parts = bf16[4,64,384]{2,1,0:T(8,128)(2,1)S(1)} async-done(((bf16[4,64,384]{2,1,0:T(8,128)(2,1)}), bf16[4,64,384]{2,1,0:T(8,128)(2,1)S(1)}, u32[]{:S(2)}, u32[]{:S(2)}) %all-to-all-start.3) | async-done | bytes 196640 | tf_op jit(solution)/shard_map/all_to_all | solution.py:31
  93.6 1.5 %collective-permute-start.16 = (bf16[224,384]{1,0:T(8,128)(2,1)S(1)}, bf16[224,384]{1,0:T(8,128)(2,1)S(1)}, u32[]{:S(2)}, u32[]{:S(2)}) collective-permute-start(bf16[224,384]{1,0:T(8,128)(2,1)S(1)} %share.1.first), channel_id=1, source_target_pairs={{0,2},{2,0},{4,6},{6,4},{1,3},{3,1},{5,7},{7,5},{8,10},{10,8},{12,... | collective-permute-start | bytes 516104 | tf_op jit(solution)/shard_map/ppermute | solution.py:27
  95.2 3.9 %collective-permute-done.16.second = bf16[224,384]{1,0:T(8,128)(2,1)S(1)} collective-permute-done((bf16[224,384]{1,0:T(8,128)(2,1)S(1)}, bf16[224,384]{1,0:T(8,128)(2,1)S(1)}, u32[]{:S(2)}, u32[]{:S(2)}) %collective-permute-start.16) | collective-permute-done | bytes 172064 | tf_op jit(solution)/shard_map/ppermute | solution.py:27
  99.2 2.4 %collective-permute-start.17 = (bf16[224,384]{1,0:T(8,128)(2,1)S(1)}, bf16[224,384]{1,0:T(8,128)(2,1)S(1)}, u32[]{:S(2)}, u32[]{:S(2)}) collective-permute-start(bf16[224,384]{1,0:T(8,128)(2,1)S(1)} %add.18.first), channel_id=1, source_target_pairs={{0,4},{2,6},{4,0},{6,2},{1,5},{3,7},{5,1},{7,3},{8,12},{10,14},{12... | collective-permute-start | bytes 516104 | tf_op jit(solution)/shard_map/ppermute | solution.py:27
  101.6 1.1 collective-permute-start.13
  102.7 3.3 %collective-permute-done.13.piece_x = bf16[96,384]{1,0:T(8,128)(2,1)S(1)} collective-permute-done((bf16[96,384]{1,0:T(8,128)(2,1)S(1)}, bf16[96,384]{1,0:T(8,128)(2,1)S(1)}, u32[]{:S(2)}, u32[]{:S(2)}) %collective-permute-start.13) | collective-permute-done | bytes 73760 | tf_op jit(solution)/shard_map/ppermute | solution.py:27
  105.9 1.3 %collective-permute-done.15.piece_both = bf16[96,384]{1,0:T(8,128)(2,1)S(1)} collective-permute-done((bf16[96,384]{1,0:T(8,128)(2,1)S(1)}, bf16[96,384]{1,0:T(8,128)(2,1)S(1)}, u32[]{:S(2)}, u32[]{:S(2)}) %collective-permute-start.15) | collective-permute-done | bytes 73760 | tf_op jit(solution)/shard_map/ppermute | solution.py:27
  107.7 1.1 collective-permute-start.18
  109.7 4.1 %collective-permute-done.18.own_b = bf16[224,384]{1,0:T(8,128)(2,1)S(1)} collective-permute-done((bf16[224,384]{1,0:T(8,128)(2,1)S(1)}, bf16[224,384]{1,0:T(8,128)(2,1)S(1)}, u32[]{:S(2)}, u32[]{:S(2)}) %collective-permute-start.18) | collective-permute-done | bytes 172064 | tf_op jit(solution)/shard_map/ppermute | solution.py:27
  113.8 1.1 collective-permute-start.20
  115.4 3.8 %collective-permute-done.20.own_both = bf16[224,384]{1,0:T(8,128)(2,1)S(1)} collective-permute-done((bf16[224,384]{1,0:T(8,128)(2,1)S(1)}, bf16[224,384]{1,0:T(8,128)(2,1)S(1)}, u32[]{:S(2)}, u32[]{:S(2)}) %collective-permute-start.20) | collective-permute-done | bytes 172064 | tf_op jit(solution)/shard_map/ppermute | solution.py:27
  119.3 1.3 %collective-permute-done.24.core_both = bf16[224,384]{1,0:T(8,128)(2,1)S(1)} collective-permute-done((bf16[224,384]{1,0:T(8,128)(2,1)S(1)}, bf16[224,384]{1,0:T(8,128)(2,1)S(1)}, u32[]{:S(2)}, u32[]{:S(2)}) %collective-permute-start.24) | collective-permute-done | bytes 172064 | tf_op jit(solution)/shard_map/ppermute | solution.py:27
  120.6 2.4 %unpack.1 = (f32[384]{0:T(512)}, f32[384]{0:T(512)}, f32[772,384]{1,0:T(8,128)}, f32[772]{0:T(1024)}, f32[9,384]{1,0:T(8,128)}, /*index=5*/f32[25,384]{1,0:T(8,1...) custom-call(s32[5]{0:T(128)S(1)} %stack.32.spots, ...), custom_call_target="tpu_custom_call" | custom-call | flops 2200000000 | bytes 1671188 | tf_op jit(solution)/shard_map/unpack/pallas_call | solution.py:1137
  (79 shorter events, 11.6 us)
Async XLA Ops:
  3.0 7.6 %copy-start = (bf16[384,772]{0,1:T(8,128)(2,1)S(1)}, bf16[384,772]{0,1:T(8,128)(2,1)}, u32[]{:S(2)}) copy-start(bf16[384,772]{0,1:T(8,128)(2,1)} %param.22) | copy-start | bytes 1778692
  3.0 7.6 %copy-start.1 = (bf16[2,14,14,384]{3,0,2,1:T(2,128)(2,1)S(1)}, bf16[2,14,14,384]{3,0,2,1:T(2,128)(2,1)}, u32[]{:S(2)}) copy-start(bf16[2,14,14,384]{3,0,2,1:T(2,128)(2,1)} %param.37) | copy-start | bytes 903172
  3.1 7.6 %copy-start.2 = (bf16[2,14,14,384]{3,0,2,1:T(2,128)(2,1)S(1)}, bf16[2,14,14,384]{3,0,2,1:T(2,128)(2,1)}, u32[]{:S(2)}) copy-start(bf16[2,14,14,384]{3,0,2,1:T(2,128)(2,1)} %param.19) | copy-start | bytes 903172
  3.2 25.4 %all-to-all-start = ((bf16[8,112,384]{2,1,0:T(8,128)(2,1)}), bf16[8,112,384]{2,1,0:T(8,128)(2,1)S(1)}, u32[]{:S(2)}, u32[]{:S(2)}) async-start(bf16[8,112,384]{2,1,0:T(8,128)(2,1)} %bitcast.14), calls=%async_computation | async-start | bytes 1376256 | tf_op jit(solution)/shard_map/all_to_all | solution.py:31
  13.6 11.5 %collective-permute-start.4 = (bf16[400,384]{1,0:T(8,128)(2,1)}, bf16[400,384]{1,0:T(8,128)(2,1)S(1)}, u32[]{:S(2)}, u32[]{:S(2)}) collective-permute-start(bf16[400,384]{1,0:T(8,128)(2,1)} %get-tuple-element.113.refs_3_.refs_2_), channel_id=1, source_target_pairs={{0,16},{16,0},{1,17},{17,1},{2,18},{18,2},{3,19},{19,3},{4,20},{20... | collective-permute-start | bytes 921608 | tf_op jit(solution)/shard_map/ppermute | solution.py:27
  15.1 10.0 %collective-permute-start.2 = (bf16[400,384]{1,0:T(8,128)(2,1)}, bf16[400,384]{1,0:T(8,128)(2,1)S(1)}, u32[]{:S(2)}, u32[]{:S(2)}) collective-permute-start(bf16[400,384]{1,0:T(8,128)(2,1)} %get-tuple-element.113.refs_3_.refs_2_), channel_id=1, source_target_pairs={{0,8},{8,0},{1,9},{9,1},{2,10},{10,2},{3,11},{11,3},{4,12},{12,4},... | collective-permute-start | bytes 921608 | tf_op jit(solution)/shard_map/ppermute | solution.py:27
  24.0 2.0 %collective-permute-start.1 = (bf16[400,384]{1,0:T(8,128)(2,1)}, bf16[400,384]{1,0:T(8,128)(2,1)S(1)}, u32[]{:S(2)}, u32[]{:S(2)}) collective-permute-start(bf16[400,384]{1,0:T(8,128)(2,1)} %get-tuple-element.120.refs_1_), channel_id=1, source_target_pairs={{0,8},{8,0},{1,9},{9,1},{2,10},{10,2},{3,11},{11,3},{4,12},{12,4},... | collective-permute-start | bytes 921608 | tf_op jit(solution)/shard_map/ppermute | solution.py:27
  24.6 9.5 %collective-permute-start = (bf16[400,384]{1,0:T(8,128)(2,1)}, bf16[400,384]{1,0:T(8,128)(2,1)S(1)}, u32[]{:S(2)}, u32[]{:S(2)}) collective-permute-start(bf16[400,384]{1,0:T(8,128)(2,1)} %get-tuple-element.120.refs_1_), channel_id=1, source_target_pairs={{0,16},{16,0},{1,17},{17,1},{2,18},{18,2},{3,19},{19,3},{4,20},{20... | collective-permute-start | bytes 921608 | tf_op jit(solution)/shard_map/ppermute | solution.py:27
  25.1 9.4 %collective-permute-start.5 = (bf16[400,384]{1,0:T(8,128)(2,1)S(1)}, bf16[400,384]{1,0:T(8,128)(2,1)S(1)}, u32[]{:S(2)}, u32[]{:S(2)}) collective-permute-start(bf16[400,384]{1,0:T(8,128)(2,1)S(1)} %collective-permute-done.4.refs_3_), channel_id=1, source_target_pairs={{0,8},{8,0},{1,9},{9,1},{2,10},{10,2},{3,11},{11,3},{4,12},{12,4},... | collective-permute-start | bytes 921608 | tf_op jit(solution)/shard_map/ppermute | solution.py:27
  34.0 1.6 %collective-permute-start.3 = (bf16[400,384]{1,0:T(8,128)(2,1)S(1)}, bf16[400,384]{1,0:T(8,128)(2,1)S(1)}, u32[]{:S(2)}, u32[]{:S(2)}) collective-permute-start(bf16[400,384]{1,0:T(8,128)(2,1)S(1)} %collective-permute-done.refs_1_), channel_id=1, source_target_pairs={{0,8},{8,0},{1,9},{9,1},{2,10},{10,2},{3,11},{11,3},{4,12},{12,4},... | collective-permute-start | bytes 921608 | tf_op jit(solution)/shard_map/ppermute | solution.py:27
  34.1 2.0 %collective-permute-start.6 = (bf16[400,384]{1,0:T(8,128)(2,1)S(1)}, bf16[400,384]{1,0:T(8,128)(2,1)S(1)}, u32[]{:S(2)}, u32[]{:S(2)}) collective-permute-start(bf16[400,384]{1,0:T(8,128)(2,1)S(1)} %get-tuple-element.126), channel_id=1, source_target_pairs={{0,8},{8,0},{1,9},{9,1},{2,10},{10,2},{3,11},{11,3},{4,12},{12,4},... | collective-permute-start | bytes 921608 | tf_op jit(solution)/shard_map/ppermute | solution.py:27
  34.6 2.0 %collective-permute-start.7 = (bf16[400,384]{1,0:T(8,128)(2,1)S(1)}, bf16[400,384]{1,0:T(8,128)(2,1)S(1)}, u32[]{:S(2)}, u32[]{:S(2)}) collective-permute-start(bf16[400,384]{1,0:T(8,128)(2,1)S(1)} %get-tuple-element.128), channel_id=1, source_target_pairs={{0,8},{8,0},{1,9},{9,1},{2,10},{10,2},{3,11},{11,3},{4,12},{12,4},... | collective-permute-start | bytes 921608 | tf_op jit(solution)/shard_map/ppermute | solution.py:27
  41.5 2.1 %collective-permute-start.8 = (bf16[800,384]{1,0:T(8,128)(2,1)S(1)}, bf16[800,384]{1,0:T(8,128)(2,1)S(1)}, u32[]{:S(2)}, u32[]{:S(2)}) collective-permute-start(bf16[800,384]{1,0:T(8,128)(2,1)S(1)} %get-tuple-element.132), channel_id=1, source_target_pairs={{0,8},{8,0},{1,9},{9,1},{2,10},{10,2},{3,11},{11,3},{4,12},{12,4},... | collective-permute-start | bytes 1843208 | tf_op jit(solution)/shard_map/ppermute | solution.py:27
  44.7 9.4 %collective-permute-start.9 = (bf16[400,384]{1,0:T(8,128)(2,1)S(1)}, bf16[400,384]{1,0:T(8,128)(2,1)S(1)}, u32[]{:S(2)}, u32[]{:S(2)}) collective-permute-start(bf16[400,384]{1,0:T(8,128)(2,1)S(1)} %get-tuple-element.133), channel_id=1, source_target_pairs={{0,16},{16,0},{1,17},{17,1},{2,18},{18,2},{3,19},{19,3},{4,20},{20... | collective-permute-start | bytes 921608 | tf_op jit(solution)/shard_map/ppermute | solution.py:27
  45.5 22.0 %all-to-all-start.1 = ((bf16[8,96,384]{2,1,0:T(8,128)(2,1)}), bf16[8,96,384]{2,1,0:T(8,128)(2,1)S(1)}, u32[]{:S(2)}, u32[]{:S(2)}) async-start(bf16[8,96,384]{2,1,0:T(8,128)(2,1)} %bitcast.17), calls=%async_computation.1 | async-start | bytes 1179648 | tf_op jit(solution)/shard_map/all_to_all | solution.py:31
  59.2 8.6 %collective-permute-start.11 = (bf16[400,384]{1,0:T(8,128)(2,1)S(1)}, bf16[400,384]{1,0:T(8,128)(2,1)S(1)}, u32[]{:S(2)}, u32[]{:S(2)}) collective-permute-start(bf16[400,384]{1,0:T(8,128)(2,1)S(1)} %copy-done.14), channel_id=1, source_target_pairs={{0,16},{16,0},{1,17},{17,1},{2,18},{18,2},{3,19},{19,3},{4,20},{20... | collective-permute-start | bytes 921608 | tf_op jit(solution)/shard_map/ppermute | solution.py:27
  59.8 6.8 %collective-permute-start.10 = (bf16[16,40,384]{2,1,0:T(8,128)(2,1)S(1)}, bf16[16,40,384]{2,1,0:T(8,128)(2,1)S(1)}, u32[]{:S(2)}, u32[]{:S(2)}) collective-permute-start(bf16[16,40,384]{2,1,0:T(8,128)(2,1)S(1)} %get-tuple-element.164), channel_id=1, source_target_pairs={{0,8},{8,0},{1,9},{9,1},{2,10},{10,2},{3,11},{11,3},{4,12},{12,4},... | collective-permute-start | bytes 1474568 | tf_op jit(solution)/shard_map/ppermute | solution.py:27
  67.7 16.4 %all-to-all-start.2 = ((bf16[4,160,384]{2,1,0:T(8,128)(2,1)}), bf16[4,160,384]{2,1,0:T(8,128)(2,1)S(1)}, u32[]{:S(2)}, u32[]{:S(2)}) async-start(bf16[4,160,384]{2,1,0:T(8,128)(2,1)} %bitcast.23), calls=%async_computation.2 | async-start | bytes 983040 | tf_op jit(solution)/shard_map/all_to_all | solution.py:31
  81.9 1.5 %collective-permute-start.12 = (bf16[16,16,384]{2,1,0:T(8,128)(2,1)S(1)}, bf16[16,16,384]{2,1,0:T(8,128)(2,1)S(1)}, u32[]{:S(2)}, u32[]{:S(2)}) collective-permute-start(bf16[16,16,384]{2,1,0:T(8,128)(2,1)S(1)} %get-tuple-element.177), channel_id=1, source_target_pairs={{0,8},{8,0},{1,9},{9,1},{2,10},{10,2},{3,11},{11,3},{4,12},{12,4},... | collective-permute-start | bytes 589832 | tf_op jit(solution)/shard_map/ppermute | solution.py:27
  84.2 9.4 %all-to-all-start.3 = ((bf16[4,64,384]{2,1,0:T(8,128)(2,1)}), bf16[4,64,384]{2,1,0:T(8,128)(2,1)S(1)}, u32[]{:S(2)}, u32[]{:S(2)}) async-start(bf16[4,64,384]{2,1,0:T(8,128)(2,1)} %bitcast.35), calls=%async_computation.3 | async-start | bytes 393216 | tf_op jit(solution)/shard_map/all_to_all | solution.py:31
  93.6 5.5 %collective-permute-start.16 = (bf16[224,384]{1,0:T(8,128)(2,1)S(1)}, bf16[224,384]{1,0:T(8,128)(2,1)S(1)}, u32[]{:S(2)}, u32[]{:S(2)}) collective-permute-start(bf16[224,384]{1,0:T(8,128)(2,1)S(1)} %share.1.first), channel_id=1, source_target_pairs={{0,2},{2,0},{4,6},{6,4},{1,3},{3,1},{5,7},{7,5},{8,10},{10,8},{12,... | collective-permute-start | bytes 516104 | tf_op jit(solution)/shard_map/ppermute | solution.py:27
  99.2 8.5 %collective-permute-start.17 = (bf16[224,384]{1,0:T(8,128)(2,1)S(1)}, bf16[224,384]{1,0:T(8,128)(2,1)S(1)}, u32[]{:S(2)}, u32[]{:S(2)}) collective-permute-start(bf16[224,384]{1,0:T(8,128)(2,1)S(1)} %add.18.first), channel_id=1, source_target_pairs={{0,4},{2,6},{4,0},{6,2},{1,5},{3,7},{5,1},{7,3},{8,12},{10,14},{12... | collective-permute-start | bytes 516104 | tf_op jit(solution)/shard_map/ppermute | solution.py:27
  101.6 4.4 %collective-permute-start.13 = (bf16[96,384]{1,0:T(8,128)(2,1)S(1)}, bf16[96,384]{1,0:T(8,128)(2,1)S(1)}, u32[]{:S(2)}, u32[]{:S(2)}) collective-permute-start(bf16[96,384]{1,0:T(8,128)(2,1)S(1)} %sum.1.piece), channel_id=1, source_target_pairs={{0,16},{16,0},{1,17},{17,1},{2,18},{18,2},{3,19},{19,3},{4,20},{20... | collective-permute-start | bytes 221192 | tf_op jit(solution)/shard_map/ppermute | solution.py:27
  102.7 3.3 %collective-permute-start.14 = (bf16[96,384]{1,0:T(8,128)(2,1)S(1)}, bf16[96,384]{1,0:T(8,128)(2,1)S(1)}, u32[]{:S(2)}, u32[]{:S(2)}) collective-permute-start(bf16[96,384]{1,0:T(8,128)(2,1)S(1)} %sum.1.piece), channel_id=1, source_target_pairs={{0,8},{8,0},{1,9},{9,1},{2,10},{10,2},{3,11},{11,3},{4,12},{12,4},... | collective-permute-start | bytes 221192 | tf_op jit(solution)/shard_map/ppermute | solution.py:27
  105.9 1.3 %collective-permute-start.15 = (bf16[96,384]{1,0:T(8,128)(2,1)S(1)}, bf16[96,384]{1,0:T(8,128)(2,1)S(1)}, u32[]{:S(2)}, u32[]{:S(2)}) collective-permute-start(bf16[96,384]{1,0:T(8,128)(2,1)S(1)} %collective-permute-done.13.piece_x), channel_id=1, source_target_pairs={{0,8},{8,0},{1,9},{9,1},{2,10},{10,2},{3,11},{11,3},{4,12},{12,4},... | collective-permute-start | bytes 221192 | tf_op jit(solution)/shard_map/ppermute | solution.py:27
  107.7 6.0 %collective-permute-start.18 = (bf16[224,384]{1,0:T(8,128)(2,1)S(1)}, bf16[224,384]{1,0:T(8,128)(2,1)S(1)}, u32[]{:S(2)}, u32[]{:S(2)}) collective-permute-start(bf16[224,384]{1,0:T(8,128)(2,1)S(1)} %add.19.own), channel_id=1, source_target_pairs={{0,1},{1,0},{2,3},{3,2},{4,5},{5,4},{6,7},{7,6},{8,9},{9,8},{10,11... | collective-permute-start | bytes 516104 | tf_op jit(solution)/shard_map/ppermute | solution.py:27
  108.9 6.5 %collective-permute-start.19 = (bf16[224,384]{1,0:T(8,128)(2,1)S(1)}, bf16[224,384]{1,0:T(8,128)(2,1)S(1)}, u32[]{:S(2)}, u32[]{:S(2)}) collective-permute-start(bf16[224,384]{1,0:T(8,128)(2,1)S(1)} %add.19.own), channel_id=1, source_target_pairs={{0,16},{16,0},{1,17},{17,1},{2,18},{18,2},{3,19},{19,3},{4,20},{20... | collective-permute-start | bytes 516104 | tf_op jit(solution)/shard_map/ppermute | solution.py:27
  113.8 5.4 %collective-permute-start.20 = (bf16[224,384]{1,0:T(8,128)(2,1)S(1)}, bf16[224,384]{1,0:T(8,128)(2,1)S(1)}, u32[]{:S(2)}, u32[]{:S(2)}) collective-permute-start(bf16[224,384]{1,0:T(8,128)(2,1)S(1)} %collective-permute-done.18.own_b), channel_id=1, source_target_pairs={{0,16},{16,0},{1,17},{17,1},{2,18},{18,2},{3,19},{19,3},{4,20},{20... | collective-permute-start | bytes 516104 | tf_op jit(solution)/shard_map/ppermute | solution.py:27
  114.9 4.4 %collective-permute-start.21 = (bf16[224,384]{1,0:T(8,128)(2,1)S(1)}, bf16[224,384]{1,0:T(8,128)(2,1)S(1)}, u32[]{:S(2)}, u32[]{:S(2)}) collective-permute-start(bf16[224,384]{1,0:T(8,128)(2,1)S(1)} %add.19.own), channel_id=1, source_target_pairs={{0,8},{8,0},{1,9},{9,1},{2,10},{10,2},{3,11},{11,3},{4,12},{12,4},... | collective-permute-start | bytes 516104 | tf_op jit(solution)/shard_map/ppermute | solution.py:27
  114.9 4.4 %collective-permute-start.22 = (bf16[224,384]{1,0:T(8,128)(2,1)S(1)}, bf16[224,384]{1,0:T(8,128)(2,1)S(1)}, u32[]{:S(2)}, u32[]{:S(2)}) collective-permute-start(bf16[224,384]{1,0:T(8,128)(2,1)S(1)} %collective-permute-done.18.own_b), channel_id=1, source_target_pairs={{0,8},{8,0},{1,9},{9,1},{2,10},{10,2},{3,11},{11,3},{4,12},{12,4},... | collective-permute-start | bytes 516104 | tf_op jit(solution)/shard_map/ppermute | solution.py:27
  115.4 3.9 %collective-permute-start.23 = (bf16[224,384]{1,0:T(8,128)(2,1)S(1)}, bf16[224,384]{1,0:T(8,128)(2,1)S(1)}, u32[]{:S(2)}, u32[]{:S(2)}) collective-permute-start(bf16[224,384]{1,0:T(8,128)(2,1)S(1)} %collective-permute-done.19.own_x), channel_id=1, source_target_pairs={{0,8},{8,0},{1,9},{9,1},{2,10},{10,2},{3,11},{11,3},{4,12},{12,4},... | collective-permute-start | bytes 516104 | tf_op jit(solution)/shard_map/ppermute | solution.py:27
  119.2 1.4 %collective-permute-start.24 = (bf16[224,384]{1,0:T(8,128)(2,1)S(1)}, bf16[224,384]{1,0:T(8,128)(2,1)S(1)}, u32[]{:S(2)}, u32[]{:S(2)}) collective-permute-start(bf16[224,384]{1,0:T(8,128)(2,1)S(1)} %collective-permute-done.20.own_both), channel_id=1, source_target_pairs={{0,8},{8,0},{1,9},{9,1},{2,10},{10,2},{3,11},{11,3},{4,12},{12,4},... | collective-permute-start | bytes 516104 | tf_op jit(solution)/shard_map/ppermute | solution.py:27
  (12 other events, 88.5 us)

commit v6 on v5

--- a/solution.py
+++ b/solution.py
@@ -962,7 +962,11 @@
     for half, target in enumerate((own_late, other_late)):
         absolute = jnp.bitwise_xor(core[0], half)
         for piece in range(units.pieces):
-            first = (absolute * units.pieces + piece) * units.late_rows
+            far = units.shards // 2
+            column = jnp.bitwise_xor(core[1], piece // (2 * far)) * 2
+            column = column + jnp.bitwise_xor(core[2], piece // far % 2)
+            first = absolute * units.pieces + column * far + piece % far
+            first = first * units.late_rows
             target[piece] = gathered[
                 pl.ds(pl.multiple_of(first, 16), units.late_rows), :
             ].astype(bf16)
@@ -1529,6 +1533,10 @@
         rest_parts = exchange(rest_half.reshape(-1, width), ("x", "b"))
         rest_parts = rest_parts.reshape(4, shares[0] * shares[1] // 4, width)
     late = array(units.pieces, units.late_rows, width, kind=bf16)
+    spot_here = jnp.zeros((3,), jnp.int32)
+    if quick:
+        spot_here = jnp.stack([lax.axis_index(axis) for axis in ("core", "x", "b")])
+        spot_here = spot_here.astype(jnp.int32)
     d_inputs, own_late, other_late = call(
         functools.partial(exit_kernel, shape, units),
         "exit",
@@ -1543,7 +1551,7 @@
         ],
         9,
         24,
-        core,
+        spot_here,
         Far(two),
         Far(d_three),
         Far(one),
@@ -1563,8 +1571,7 @@
         rest_parts = after(rest_parts, own_late)
         (late_half,) = call(pair_kernel, "pair", [late], [], 1, 4, own_late, late_arrived)
         late_half, rest_parts = lax.optimization_barrier((late_half, rest_parts))
-        late_parts = exchange(late_half.reshape(-1, width), ("x", "b"))
-        late_parts = late_parts.reshape(4, units.pieces * units.late_rows // 4, width)
+        late_arrived = flip(late_half[units.pieces // 2 :], "x")
         d_inputs = after(d_inputs, late_half)
     tokens_grad, block_out = call(
         functools.partial(finish_kernel, shape),
@@ -1581,7 +1588,13 @@
         Anywhere(out_far),
     )
     if quick:
-        late_parts = after(late_parts, tokens_grad)
+        late_arrived = after(late_arrived, tokens_grad)
+        for axis in ("b", None):
+            part = array(late_arrived.shape[0], units.late_rows, width, kind=bf16)
+            (late_half,) = call(pair_kernel, "pair", [part], [], 1, 4, late_half, late_arrived)
+            if axis:
+                late_arrived = flip(late_half[late_half.shape[0] // 2 :], axis)
+        late_parts = late_half.reshape(1, -1, width)
         share_rows = units.pieces * units.share // 4
         (share,) = call(
             share_kernel,

time: 124 us -> 124 us (level)
  starting transfers between devices: 35.3 us -> 37.8 us
  waiting for transfers between devices: 33.1 us -> 30.9 us
    ppermute x25 -> x27, starting transfers between devices: 13.5 us -> 20.2 us  [flip(): lax.ppermute(values, axis, [(place, place ^ bit) for place in range(size)])]
    all_to_all x4 -> x3, starting transfers between devices: 21.7 us -> 17.5 us  [exchange(): return lax.all_to_all(values, axes, split_axis=0, concat_axis=0, tiled=True)]
    all_to_all x4 -> x3, waiting for transfers between devices: 5.05 us -> 2.61 us  [exchange(): return lax.all_to_all(values, axes, split_axis=0, concat_axis=0, tiled=True)]
    ppermute x25 -> x27, waiting for transfers between devices: 28 us -> 28.3 us  [flip(): lax.ppermute(values, axis, [(place, place ^ bit) for place in range(size)])]
    pallas_call x17 -> x19, Pallas kernels: 53.1 us -> 53 us  [call(): pl.pallas_call(kernel, name=name, out_shape=outs, in_specs=specs, out_spe...]
  transfers between devices with their start and end apart: 29 -> 30, of which waited for: 18 -> 19; matrix products, arithmetic and copies ran while one was open for 0% -> 0% of each run, Pallas kernels for 34% -> 34%
where the time goes in v6:
time: 124 us; the launch traced here: 123 us
  Pallas kernels  53 us (43%)
  starting transfers between devices  37.8 us (30%)
  waiting for transfers between devices  30.9 us (25%)
  between operations  1.24 us (1%)
    pallas_call x19, Pallas kernels, call(): pl.pallas_call(kernel, name=name, out_shape=outs, in_specs=specs, out_spe...  53 us
    ppermute x27, waiting for transfers between devices, flip(): lax.ppermute(values, axis, [(place, place ^ bit) for place in range(size)])  28.3 us
    ppermute x27, starting transfers between devices, flip(): lax.ppermute(values, axis, [(place, place ^ bit) for place in range(size)])  20.2 us
    all_to_all x3, starting transfers between devices, exchange(): return lax.all_to_all(values, axes, split_axis=0, concat_axis=0, tiled=True)  17.5 us
    all_to_all x3, waiting for transfers between devices, exchange(): return lax.all_to_all(values, axes, split_axis=0, concat_axis=0, tiled=True)  2.61 us
  transfers between devices with their start and end apart: 30, of which 19 were waited for; matrix products, arithmetic and copies ran while one was open for 0% of the time, Pallas kernels for 34%

profile of v6, /device:TPU:0, one launch (start us, length us, event | category | flops | bytes accessed | tf_op | source)
XLA Modules:
  0.0 123.5 jit_solution(1110097877324283743)
XLA Ops:
  0.7 2.3 %piece.1 = bf16[896,384]{1,0:T(8,128)(2,1)} custom-call(s32[3]{0:T(128)S(1)} %pad_add_fusion.spots, bf16[192,384]{1,0:T(8,128)(2,1)} %bitcast.56, bf16[192,384]{1,0:T(8,128)(2,1)} %second.1, bf16[192]{0:T(256)(128)(2,1)} %far_bias.1), custom_call_target="tpu_custom_call" | custom-call | flops 1100000000 | bytes 295308 | tf_op jit(solution)/shard_map/piece/pallas_call | solution.py:1141
  3.2 7.4 %all-to-all-start = ((bf16[8,112,384]{2,1,0:T(8,128)(2,1)}), bf16[8,112,384]{2,1,0:T(8,128)(2,1)S(1)}, u32[]{:S(2)}, u32[]{:S(2)}) async-start(bf16[8,112,384]{2,1,0:T(8,128)(2,1)} %bitcast.14), calls=%async_computation | async-start | bytes 1376256 | tf_op jit(solution)/shard_map/all_to_all | solution.py:31
  10.8 2.8 %entry.1 = (f32[96,384]{1,0:T(8,128)}, bf16[400,384]{1,0:T(8,128)(2,1)}, f32[400,384]{1,0:T(8,128)S(1)}, bf16[400,384]{1,0:T(8,128)(2,1)}, f32[400,384]{1,0:T(8,...) custom-call(bf16[1176,128]{1,0:T(8,128)(2,1)S(1)} %bitcast.54, ...), custom_call_target="tpu_custom_call" | custom-call | flops 5500000256 | bytes 1265672 | tf_op jit(solution)/shard_map/entry/pallas_call | solution.py:1141
  13.6 1.6 %collective-permute-start.4 = (bf16[400,384]{1,0:T(8,128)(2,1)}, bf16[400,384]{1,0:T(8,128)(2,1)S(1)}, u32[]{:S(2)}, u32[]{:S(2)}) collective-permute-start(bf16[400,384]{1,0:T(8,128)(2,1)} %get-tuple-element.113.refs_3_.refs_2_), channel_id=1, source_target_pairs={{0,16},{16,0},{1,17},{17,1},{2,18},{18,2},{3,19},{19,3},{4,20},{20... | collective-permute-start | bytes 921608 | tf_op jit(solution)/shard_map/ppermute | solution.py:27
  15.2 8.8 %modulation.1 = (f32[2240,128]{1,0:T(8,128)}, f32[400,512]{1,0:T(8,128)}, f32[400,384]{1,0:T(8,128)}, f32[1568,128]{1,0:T(8,128)}, f32[400,384]{1,0:T(8,128)}, /...) custom-call(f32[2240,128]{1,0:T(8,128)S(1)} %get-tuple-element.114.r, ...), custom_call_target="tpu_custom_call" | custom-call | flops 8800000000 | bytes 4734976 | tf_op jit(solution)/shard_map/modulation/pallas_call | solution.py:1141
  26.0 2.6 %all-to-all-done = bf16[8,112,384]{2,1,0:T(8,128)(2,1)S(1)} async-done(((bf16[8,112,384]{2,1,0:T(8,128)(2,1)}), bf16[8,112,384]{2,1,0:T(8,128)(2,1)S(1)}, u32[]{:S(2)}, u32[]{:S(2)}) %all-to-all-start) | async-done | bytes 688160 | tf_op jit(solution)/shard_map/all_to_all | solution.py:31
  28.6 4.1 %feed.2 = (bf16[400,384]{1,0:T(8,128)(2,1)S(1)}, bf16[400,384]{1,0:T(8,128)(2,1)S(1)}, bf16[400,384]{1,0:T(8,128)(2,1)S(1)}, bf16[400,384]{1,0:T(8,128)(2,1)S(1)...) custom-call(bf16[896,384]{1,0:T(8,128)(2,1)S(1)} %bitcast.48, bf16[400,384]{1,0:T(8,128)(2,1)} %get-tuple-element.120.refs_1_, ...), custom_call_target="tpu_custom_call" | custom-call | flops 6600000000 | bytes 1916928 | tf_op jit(solution)/shard_map/feed/pallas_call | solution.py:1141
  32.7 1.3 %collective-permute-done.refs_1_ = bf16[400,384]{1,0:T(8,128)(2,1)S(1)} collective-permute-done((bf16[400,384]{1,0:T(8,128)(2,1)}, bf16[400,384]{1,0:T(8,128)(2,1)S(1)}, u32[]{:S(2)}, u32[]{:S(2)}) %collective-permute-start) | collective-permute-done | bytes 307232 | tf_op jit(solution)/shard_map/ppermute | solution.py:27
  36.5 5.0 %feed.3 = (bf16[400,384]{1,0:T(8,128)(2,1)S(1)}, bf16[400,384]{1,0:T(8,128)(2,1)S(1)}, bf16[800,384]{1,0:T(8,128)(2,1)S(1)}, f32[400,384]{1,0:T(8,128)}, f32[400...) custom-call(bf16[896,384]{1,0:T(8,128)(2,1)S(1)} %bitcast.49, ...), custom_call_target="tpu_custom_call" | custom-call | flops 6600000000 | bytes 4337664 | tf_op jit(solution)/shard_map/feed/pallas_call | solution.py:1141
  41.9 1.7 %collective-permute-done.8.refs_2_ = bf16[800,384]{1,0:T(8,128)(2,1)S(1)} collective-permute-done((bf16[800,384]{1,0:T(8,128)(2,1)S(1)}, bf16[800,384]{1,0:T(8,128)(2,1)S(1)}, u32[]{:S(2)}, u32[]{:S(2)}) %collective-permute-start.8) | collective-permute-done | bytes 614432 | tf_op jit(solution)/shard_map/ppermute | solution.py:27
  45.4 6.0 %all-to-all-start.1 = ((bf16[8,96,384]{2,1,0:T(8,128)(2,1)}), bf16[8,96,384]{2,1,0:T(8,128)(2,1)S(1)}, u32[]{:S(2)}, u32[]{:S(2)}) async-start(bf16[8,96,384]{2,1,0:T(8,128)(2,1)} %bitcast.19), calls=%async_computation.1 | async-start | bytes 1179648 | tf_op jit(solution)/shard_map/all_to_all | solution.py:31
  51.4 2.6 %collective-permute-done.9.refs_5_ = bf16[400,384]{1,0:T(8,128)(2,1)S(1)} collective-permute-done((bf16[400,384]{1,0:T(8,128)(2,1)S(1)}, bf16[400,384]{1,0:T(8,128)(2,1)S(1)}, u32[]{:S(2)}, u32[]{:S(2)}) %collective-permute-start.9) | collective-permute-done | bytes 307232 | tf_op jit(solution)/shard_map/ppermute | solution.py:27
  54.0 5.1 %heads.1 = (f32[400,384]{1,0:T(8,128)}, bf16[400,384]{1,0:T(8,128)(2,1)}, f32[400,384]{1,0:T(8,128)S(1)}, bf16[16,40,384]{2,1,0:T(8,128)(2,1)S(1)}, bf16[16,40,3...) custom-call(s32[1]{0:T(128)} %bitcast.refs_0_, ...), custom_call_target="tpu_custom_call" | custom-call | flops 5500000256 | bytes 11603972 | tf_op jit(solution)/shard_map/heads/pallas_call | solution.py:1141
  59.8 6.8 %levels_back.1 = (f32[2240,128]{1,0:T(8,128)}, f32[2240,128]{1,0:T(8,128)}, f32[2240,128]{1,0:T(8,128)}, bf16[400,384]{1,0:T(8,128)(2,1)}, bf16[400,128]{1,0:T(8,128)(2,1)}) custom-call(f32[96,384]{1,0:T(8,128)S(1)} %get-tuple-element.149.refs_0_, f32[400,512]{1,0:T(8,128)S(1)} %get-tuple-element.150.refs_1_, f32[400,384]{1,0:T(8,128)S(1)} %get-tuple-element.151.refs_2_, ...), custom_call_target="tpu_custom_call" | custom-call | flops 8800000000 | bytes 7438336 | tf_op jit(solution)/shard_map/levels_back/pallas_call | solution.py:1141
  67.7 4.1 %all-to-all-start.2 = ((bf16[4,160,384]{2,1,0:T(8,128)(2,1)}), bf16[4,160,384]{2,1,0:T(8,128)(2,1)S(1)}, u32[]{:S(2)}, u32[]{:S(2)}) async-start(bf16[4,160,384]{2,1,0:T(8,128)(2,1)} %bitcast.25), calls=%async_computation.2 | async-start | bytes 983040 | tf_op jit(solution)/shard_map/all_to_all | solution.py:31
  71.8 10.6 %exit.1 = (f32[400,384]{1,0:T(8,128)}, bf16[16,16,384]{2,1,0:T(8,128)(2,1)S(1)}, bf16[16,16,384]{2,1,0:T(8,128)(2,1)S(1)}) custom-call(s32[3]{0:T(128)S(1)} %pad_add_fusion.1.refs_0_, f32[2240,128]{1,0:T(8,128)} %get-tuple-element.146.refs_21_.refs_1_, f32[2240,128]{1,0:T(8,128)} %get-tuple-element.159.refs_2_, ...), custom_call_target="tpu_custom_call" | custom-call | flops 9900000256 | bytes 8946700 | tf_op jit(solution)/shard_map/exit/pallas_call | solution.py:1141
  84.0 2.1 %collective-permute-start.13 = (bf16[8,16,384]{2,1,0:T(8,128)(2,1)S(1)}, bf16[8,16,384]{2,1,0:T(8,128)(2,1)S(1)}, u32[]{:S(2)}, u32[]{:S(2)}) collective-permute-start(bf16[8,16,384]{2,1,0:T(8,128)(2,1)S(1)} %slice.6), channel_id=1, source_target_pairs={{0,16},{16,0},{1,17},{17,1},{2,18},{18,2},{3,19},{19,3},{4,20},{20... | collective-permute-start | bytes 294920 | tf_op jit(solution)/shard_map/ppermute | solution.py:27
  86.1 2.7 %finish.1 = (f32[1176,128]{1,0:T(8,128)}, f32[1176,128]{1,0:T(8,128)}) custom-call(f32[400,384]{1,0:T(8,128)} %get-tuple-element.148.refs_0_, f32[400,384]{1,0:T(8,128)} %get-tuple-element.180.refs_1_, f32[96,384]{1,0:T(8,128)} %get-tuple-element.112.refs_1_.refs_14_.refs_9_.refs_2_, f32[400,384]{1,0:T(8,128)} %get-tuple-element.119.refs_3_, ...), custom_call_target="tpu_custom_call" | custom-call | flops 3300000000 | bytes 2912256 | tf_op jit(solution)/shard_map/finish/pallas_call | solution.py:1141
  89.3 1.8 %collective-permute-start.14 = (bf16[4,16,384]{2,1,0:T(8,128)(2,1)S(1)}, bf16[4,16,384]{2,1,0:T(8,128)(2,1)S(1)}, u32[]{:S(2)}, u32[]{:S(2)}) collective-permute-start(bf16[4,16,384]{2,1,0:T(8,128)(2,1)S(1)} %slice.8), channel_id=1, source_target_pairs={{0,1},{1,0},{2,3},{3,2},{4,5},{5,4},{6,7},{7,6},{8,9},{9,8},{10,11... | collective-permute-start | bytes 147464 | tf_op jit(solution)/shard_map/ppermute | solution.py:27
  91.1 2.4 %collective-permute-done.14.second = bf16[4,16,384]{2,1,0:T(8,128)(2,1)S(1)} collective-permute-done((bf16[4,16,384]{2,1,0:T(8,128)(2,1)S(1)}, bf16[4,16,384]{2,1,0:T(8,128)(2,1)S(1)}, u32[]{:S(2)}, u32[]{:S(2)}) %collective-permute-start.14) | collective-permute-done | bytes 49184 | tf_op jit(solution)/shard_map/ppermute | solution.py:27
  93.5 1.5 %collective-permute-start.18 = (bf16[224,384]{1,0:T(8,128)(2,1)S(1)}, bf16[224,384]{1,0:T(8,128)(2,1)S(1)}, u32[]{:S(2)}, u32[]{:S(2)}) collective-permute-start(bf16[224,384]{1,0:T(8,128)(2,1)S(1)} %share.1.first), channel_id=1, source_target_pairs={{0,2},{2,0},{4,6},{6,4},{1,3},{3,1},{5,7},{7,5},{8,10},{10,8},{12,... | collective-permute-start | bytes 516104 | tf_op jit(solution)/shard_map/ppermute | solution.py:27
  95.0 3.9 %collective-permute-done.18.second = bf16[224,384]{1,0:T(8,128)(2,1)S(1)} collective-permute-done((bf16[224,384]{1,0:T(8,128)(2,1)S(1)}, bf16[224,384]{1,0:T(8,128)(2,1)S(1)}, u32[]{:S(2)}, u32[]{:S(2)}) %collective-permute-start.18) | collective-permute-done | bytes 172064 | tf_op jit(solution)/shard_map/ppermute | solution.py:27
  99.0 2.4 %collective-permute-start.19 = (bf16[224,384]{1,0:T(8,128)(2,1)S(1)}, bf16[224,384]{1,0:T(8,128)(2,1)S(1)}, u32[]{:S(2)}, u32[]{:S(2)}) collective-permute-start(bf16[224,384]{1,0:T(8,128)(2,1)S(1)} %add.22.first), channel_id=1, source_target_pairs={{0,4},{2,6},{4,0},{6,2},{1,5},{3,7},{5,1},{7,3},{8,12},{10,14},{12... | collective-permute-start | bytes 516104 | tf_op jit(solution)/shard_map/ppermute | solution.py:27
  101.5 2.0 %collective-permute-start.15 = (bf16[96,384]{1,0:T(8,128)(2,1)S(1)}, bf16[96,384]{1,0:T(8,128)(2,1)S(1)}, u32[]{:S(2)}, u32[]{:S(2)}) collective-permute-start(bf16[96,384]{1,0:T(8,128)(2,1)S(1)} %sum.1.piece), channel_id=1, source_target_pairs={{0,16},{16,0},{1,17},{17,1},{2,18},{18,2},{3,19},{19,3},{4,20},{20... | collective-permute-start | bytes 221192 | tf_op jit(solution)/shard_map/ppermute | solution.py:27
  103.4 2.4 %collective-permute-done.15.piece_x = bf16[96,384]{1,0:T(8,128)(2,1)S(1)} collective-permute-done((bf16[96,384]{1,0:T(8,128)(2,1)S(1)}, bf16[96,384]{1,0:T(8,128)(2,1)S(1)}, u32[]{:S(2)}, u32[]{:S(2)}) %collective-permute-start.15) | collective-permute-done | bytes 73760 | tf_op jit(solution)/shard_map/ppermute | solution.py:27
  107.3 1.8 %collective-permute-start.20 = (bf16[224,384]{1,0:T(8,128)(2,1)S(1)}, bf16[224,384]{1,0:T(8,128)(2,1)S(1)}, u32[]{:S(2)}, u32[]{:S(2)}) collective-permute-start(bf16[224,384]{1,0:T(8,128)(2,1)S(1)} %add.23.own), channel_id=1, source_target_pairs={{0,1},{1,0},{2,3},{3,2},{4,5},{5,4},{6,7},{7,6},{8,9},{9,8},{10,11... | collective-permute-start | bytes 516104 | tf_op jit(solution)/shard_map/ppermute | solution.py:27
  109.1 1.5 %collective-permute-start.21 = (bf16[224,384]{1,0:T(8,128)(2,1)S(1)}, bf16[224,384]{1,0:T(8,128)(2,1)S(1)}, u32[]{:S(2)}, u32[]{:S(2)}) collective-permute-start(bf16[224,384]{1,0:T(8,128)(2,1)S(1)} %add.23.own), channel_id=1, source_target_pairs={{0,16},{16,0},{1,17},{17,1},{2,18},{18,2},{3,19},{19,3},{4,20},{20... | collective-permute-start | bytes 516104 | tf_op jit(solution)/shard_map/ppermute | solution.py:27
  110.6 3.2 %collective-permute-done.20.own_b = bf16[224,384]{1,0:T(8,128)(2,1)S(1)} collective-permute-done((bf16[224,384]{1,0:T(8,128)(2,1)S(1)}, bf16[224,384]{1,0:T(8,128)(2,1)S(1)}, u32[]{:S(2)}, u32[]{:S(2)}) %collective-permute-start.20) | collective-permute-done | bytes 172064 | tf_op jit(solution)/shard_map/ppermute | solution.py:27
  113.8 1.7 %collective-permute-start.22 = (bf16[224,384]{1,0:T(8,128)(2,1)S(1)}, bf16[224,384]{1,0:T(8,128)(2,1)S(1)}, u32[]{:S(2)}, u32[]{:S(2)}) collective-permute-start(bf16[224,384]{1,0:T(8,128)(2,1)S(1)} %collective-permute-done.20.own_b), channel_id=1, source_target_pairs={{0,16},{16,0},{1,17},{17,1},{2,18},{18,2},{3,19},{19,3},{4,20},{20... | collective-permute-start | bytes 516104 | tf_op jit(solution)/shard_map/ppermute | solution.py:27
  116.1 3.4 %collective-permute-done.22.own_both = bf16[224,384]{1,0:T(8,128)(2,1)S(1)} collective-permute-done((bf16[224,384]{1,0:T(8,128)(2,1)S(1)}, bf16[224,384]{1,0:T(8,128)(2,1)S(1)}, u32[]{:S(2)}, u32[]{:S(2)}) %collective-permute-start.22) | collective-permute-done | bytes 172064 | tf_op jit(solution)/shard_map/ppermute | solution.py:27
  119.6 1.3 %collective-permute-done.26.core_both = bf16[224,384]{1,0:T(8,128)(2,1)S(1)} collective-permute-done((bf16[224,384]{1,0:T(8,128)(2,1)S(1)}, bf16[224,384]{1,0:T(8,128)(2,1)S(1)}, u32[]{:S(2)}, u32[]{:S(2)}) %collective-permute-start.26) | collective-permute-done | bytes 172064 | tf_op jit(solution)/shard_map/ppermute | solution.py:27
  120.9 2.4 %unpack.1 = (f32[384]{0:T(512)}, f32[384]{0:T(512)}, f32[772,384]{1,0:T(8,128)}, f32[772]{0:T(1024)}, f32[9,384]{1,0:T(8,128)}, /*index=5*/f32[25,384]{1,0:T(8,1...) custom-call(s32[5]{0:T(128)S(1)} %stack.39.spots, ...), custom_call_target="tpu_custom_call" | custom-call | flops 2200000000 | bytes 1671188 | tf_op jit(solution)/shard_map/unpack/pallas_call | solution.py:1141
  (86 shorter events, 12.7 us)
Async XLA Ops:
  3.0 7.6 %copy-start = (bf16[384,772]{0,1:T(8,128)(2,1)S(1)}, bf16[384,772]{0,1:T(8,128)(2,1)}, u32[]{:S(2)}) copy-start(bf16[384,772]{0,1:T(8,128)(2,1)} %param.22) | copy-start | bytes 1778692
  3.0 7.6 %copy-start.1 = (bf16[2,14,14,384]{3,0,2,1:T(2,128)(2,1)S(1)}, bf16[2,14,14,384]{3,0,2,1:T(2,128)(2,1)}, u32[]{:S(2)}) copy-start(bf16[2,14,14,384]{3,0,2,1:T(2,128)(2,1)} %param.37) | copy-start | bytes 903172
  3.2 25.4 %all-to-all-start = ((bf16[8,112,384]{2,1,0:T(8,128)(2,1)}), bf16[8,112,384]{2,1,0:T(8,128)(2,1)S(1)}, u32[]{:S(2)}, u32[]{:S(2)}) async-start(bf16[8,112,384]{2,1,0:T(8,128)(2,1)} %bitcast.14), calls=%async_computation | async-start | bytes 1376256 | tf_op jit(solution)/shard_map/all_to_all | solution.py:31
  13.6 11.5 %collective-permute-start.4 = (bf16[400,384]{1,0:T(8,128)(2,1)}, bf16[400,384]{1,0:T(8,128)(2,1)S(1)}, u32[]{:S(2)}, u32[]{:S(2)}) collective-permute-start(bf16[400,384]{1,0:T(8,128)(2,1)} %get-tuple-element.113.refs_3_.refs_2_), channel_id=1, source_target_pairs={{0,16},{16,0},{1,17},{17,1},{2,18},{18,2},{3,19},{19,3},{4,20},{20... | collective-permute-start | bytes 921608 | tf_op jit(solution)/shard_map/ppermute | solution.py:27
  15.1 10.0 %collective-permute-start.2 = (bf16[400,384]{1,0:T(8,128)(2,1)}, bf16[400,384]{1,0:T(8,128)(2,1)S(1)}, u32[]{:S(2)}, u32[]{:S(2)}) collective-permute-start(bf16[400,384]{1,0:T(8,128)(2,1)} %get-tuple-element.113.refs_3_.refs_2_), channel_id=1, source_target_pairs={{0,8},{8,0},{1,9},{9,1},{2,10},{10,2},{3,11},{11,3},{4,12},{12,4},... | collective-permute-start | bytes 921608 | tf_op jit(solution)/shard_map/ppermute | solution.py:27
  24.0 2.0 %collective-permute-start.1 = (bf16[400,384]{1,0:T(8,128)(2,1)}, bf16[400,384]{1,0:T(8,128)(2,1)S(1)}, u32[]{:S(2)}, u32[]{:S(2)}) collective-permute-start(bf16[400,384]{1,0:T(8,128)(2,1)} %get-tuple-element.120.refs_1_), channel_id=1, source_target_pairs={{0,8},{8,0},{1,9},{9,1},{2,10},{10,2},{3,11},{11,3},{4,12},{12,4},... | collective-permute-start | bytes 921608 | tf_op jit(solution)/shard_map/ppermute | solution.py:27
  24.6 9.5 %collective-permute-start = (bf16[400,384]{1,0:T(8,128)(2,1)}, bf16[400,384]{1,0:T(8,128)(2,1)S(1)}, u32[]{:S(2)}, u32[]{:S(2)}) collective-permute-start(bf16[400,384]{1,0:T(8,128)(2,1)} %get-tuple-element.120.refs_1_), channel_id=1, source_target_pairs={{0,16},{16,0},{1,17},{17,1},{2,18},{18,2},{3,19},{19,3},{4,20},{20... | collective-permute-start | bytes 921608 | tf_op jit(solution)/shard_map/ppermute | solution.py:27
  25.1 9.4 %collective-permute-start.5 = (bf16[400,384]{1,0:T(8,128)(2,1)S(1)}, bf16[400,384]{1,0:T(8,128)(2,1)S(1)}, u32[]{:S(2)}, u32[]{:S(2)}) collective-permute-start(bf16[400,384]{1,0:T(8,128)(2,1)S(1)} %collective-permute-done.4.refs_3_), channel_id=1, source_target_pairs={{0,8},{8,0},{1,9},{9,1},{2,10},{10,2},{3,11},{11,3},{4,12},{12,4},... | collective-permute-start | bytes 921608 | tf_op jit(solution)/shard_map/ppermute | solution.py:27
  34.0 1.6 %collective-permute-start.3 = (bf16[400,384]{1,0:T(8,128)(2,1)S(1)}, bf16[400,384]{1,0:T(8,128)(2,1)S(1)}, u32[]{:S(2)}, u32[]{:S(2)}) collective-permute-start(bf16[400,384]{1,0:T(8,128)(2,1)S(1)} %collective-permute-done.refs_1_), channel_id=1, source_target_pairs={{0,8},{8,0},{1,9},{9,1},{2,10},{10,2},{3,11},{11,3},{4,12},{12,4},... | collective-permute-start | bytes 921608 | tf_op jit(solution)/shard_map/ppermute | solution.py:27
  34.0 2.0 %collective-permute-start.6 = (bf16[400,384]{1,0:T(8,128)(2,1)S(1)}, bf16[400,384]{1,0:T(8,128)(2,1)S(1)}, u32[]{:S(2)}, u32[]{:S(2)}) collective-permute-start(bf16[400,384]{1,0:T(8,128)(2,1)S(1)} %get-tuple-element.126), channel_id=1, source_target_pairs={{0,8},{8,0},{1,9},{9,1},{2,10},{10,2},{3,11},{11,3},{4,12},{12,4},... | collective-permute-start | bytes 921608 | tf_op jit(solution)/shard_map/ppermute | solution.py:27
  34.6 2.0 %collective-permute-start.7 = (bf16[400,384]{1,0:T(8,128)(2,1)S(1)}, bf16[400,384]{1,0:T(8,128)(2,1)S(1)}, u32[]{:S(2)}, u32[]{:S(2)}) collective-permute-start(bf16[400,384]{1,0:T(8,128)(2,1)S(1)} %get-tuple-element.128), channel_id=1, source_target_pairs={{0,8},{8,0},{1,9},{9,1},{2,10},{10,2},{3,11},{11,3},{4,12},{12,4},... | collective-permute-start | bytes 921608 | tf_op jit(solution)/shard_map/ppermute | solution.py:27
  41.5 2.1 %collective-permute-start.8 = (bf16[800,384]{1,0:T(8,128)(2,1)S(1)}, bf16[800,384]{1,0:T(8,128)(2,1)S(1)}, u32[]{:S(2)}, u32[]{:S(2)}) collective-permute-start(bf16[800,384]{1,0:T(8,128)(2,1)S(1)} %get-tuple-element.132), channel_id=1, source_target_pairs={{0,8},{8,0},{1,9},{9,1},{2,10},{10,2},{3,11},{11,3},{4,12},{12,4},... | collective-permute-start | bytes 1843208 | tf_op jit(solution)/shard_map/ppermute | solution.py:27
  44.6 9.4 %collective-permute-start.9 = (bf16[400,384]{1,0:T(8,128)(2,1)S(1)}, bf16[400,384]{1,0:T(8,128)(2,1)S(1)}, u32[]{:S(2)}, u32[]{:S(2)}) collective-permute-start(bf16[400,384]{1,0:T(8,128)(2,1)S(1)} %get-tuple-element.133), channel_id=1, source_target_pairs={{0,16},{16,0},{1,17},{17,1},{2,18},{18,2},{3,19},{19,3},{4,20},{20... | collective-permute-start | bytes 921608 | tf_op jit(solution)/shard_map/ppermute | solution.py:27
  45.4 22.1 %all-to-all-start.1 = ((bf16[8,96,384]{2,1,0:T(8,128)(2,1)}), bf16[8,96,384]{2,1,0:T(8,128)(2,1)S(1)}, u32[]{:S(2)}, u32[]{:S(2)}) async-start(bf16[8,96,384]{2,1,0:T(8,128)(2,1)} %bitcast.19), calls=%async_computation.1 | async-start | bytes 1179648 | tf_op jit(solution)/shard_map/all_to_all | solution.py:31
  59.2 8.6 %collective-permute-start.11 = (bf16[400,384]{1,0:T(8,128)(2,1)S(1)}, bf16[400,384]{1,0:T(8,128)(2,1)S(1)}, u32[]{:S(2)}, u32[]{:S(2)}) collective-permute-start(bf16[400,384]{1,0:T(8,128)(2,1)S(1)} %copy-done.14), channel_id=1, source_target_pairs={{0,16},{16,0},{1,17},{17,1},{2,18},{18,2},{3,19},{19,3},{4,20},{20... | collective-permute-start | bytes 921608 | tf_op jit(solution)/shard_map/ppermute | solution.py:27
  59.8 6.8 %collective-permute-start.10 = (bf16[16,40,384]{2,1,0:T(8,128)(2,1)S(1)}, bf16[16,40,384]{2,1,0:T(8,128)(2,1)S(1)}, u32[]{:S(2)}, u32[]{:S(2)}) collective-permute-start(bf16[16,40,384]{2,1,0:T(8,128)(2,1)S(1)} %get-tuple-element.164), channel_id=1, source_target_pairs={{0,8},{8,0},{1,9},{9,1},{2,10},{10,2},{3,11},{11,3},{4,12},{12,4},... | collective-permute-start | bytes 1474568 | tf_op jit(solution)/shard_map/ppermute | solution.py:27
  67.7 16.3 %all-to-all-start.2 = ((bf16[4,160,384]{2,1,0:T(8,128)(2,1)}), bf16[4,160,384]{2,1,0:T(8,128)(2,1)S(1)}, u32[]{:S(2)}, u32[]{:S(2)}) async-start(bf16[4,160,384]{2,1,0:T(8,128)(2,1)} %bitcast.25), calls=%async_computation.2 | async-start | bytes 983040 | tf_op jit(solution)/shard_map/all_to_all | solution.py:31
  82.4 1.5 %collective-permute-start.12 = (bf16[16,16,384]{2,1,0:T(8,128)(2,1)S(1)}, bf16[16,16,384]{2,1,0:T(8,128)(2,1)S(1)}, u32[]{:S(2)}, u32[]{:S(2)}) collective-permute-start(bf16[16,16,384]{2,1,0:T(8,128)(2,1)S(1)} %get-tuple-element.177), channel_id=1, source_target_pairs={{0,8},{8,0},{1,9},{9,1},{2,10},{10,2},{3,11},{11,3},{4,12},{12,4},... | collective-permute-start | bytes 589832 | tf_op jit(solution)/shard_map/ppermute | solution.py:27
  84.0 5.2 %collective-permute-start.13 = (bf16[8,16,384]{2,1,0:T(8,128)(2,1)S(1)}, bf16[8,16,384]{2,1,0:T(8,128)(2,1)S(1)}, u32[]{:S(2)}, u32[]{:S(2)}) collective-permute-start(bf16[8,16,384]{2,1,0:T(8,128)(2,1)S(1)} %slice.6), channel_id=1, source_target_pairs={{0,16},{16,0},{1,17},{17,1},{2,18},{18,2},{3,19},{19,3},{4,20},{20... | collective-permute-start | bytes 294920 | tf_op jit(solution)/shard_map/ppermute | solution.py:27
  89.3 4.2 %collective-permute-start.14 = (bf16[4,16,384]{2,1,0:T(8,128)(2,1)S(1)}, bf16[4,16,384]{2,1,0:T(8,128)(2,1)S(1)}, u32[]{:S(2)}, u32[]{:S(2)}) collective-permute-start(bf16[4,16,384]{2,1,0:T(8,128)(2,1)S(1)} %slice.8), channel_id=1, source_target_pairs={{0,1},{1,0},{2,3},{3,2},{4,5},{5,4},{6,7},{7,6},{8,9},{9,8},{10,11... | collective-permute-start | bytes 147464 | tf_op jit(solution)/shard_map/ppermute | solution.py:27
  93.5 5.5 %collective-permute-start.18 = (bf16[224,384]{1,0:T(8,128)(2,1)S(1)}, bf16[224,384]{1,0:T(8,128)(2,1)S(1)}, u32[]{:S(2)}, u32[]{:S(2)}) collective-permute-start(bf16[224,384]{1,0:T(8,128)(2,1)S(1)} %share.1.first), channel_id=1, source_target_pairs={{0,2},{2,0},{4,6},{6,4},{1,3},{3,1},{5,7},{7,5},{8,10},{10,8},{12,... | collective-permute-start | bytes 516104 | tf_op jit(solution)/shard_map/ppermute | solution.py:27
  99.0 8.3 %collective-permute-start.19 = (bf16[224,384]{1,0:T(8,128)(2,1)S(1)}, bf16[224,384]{1,0:T(8,128)(2,1)S(1)}, u32[]{:S(2)}, u32[]{:S(2)}) collective-permute-start(bf16[224,384]{1,0:T(8,128)(2,1)S(1)} %add.22.first), channel_id=1, source_target_pairs={{0,4},{2,6},{4,0},{6,2},{1,5},{3,7},{5,1},{7,3},{8,12},{10,14},{12... | collective-permute-start | bytes 516104 | tf_op jit(solution)/shard_map/ppermute | solution.py:27
  101.5 4.4 %collective-permute-start.15 = (bf16[96,384]{1,0:T(8,128)(2,1)S(1)}, bf16[96,384]{1,0:T(8,128)(2,1)S(1)}, u32[]{:S(2)}, u32[]{:S(2)}) collective-permute-start(bf16[96,384]{1,0:T(8,128)(2,1)S(1)} %sum.1.piece), channel_id=1, source_target_pairs={{0,16},{16,0},{1,17},{17,1},{2,18},{18,2},{3,19},{19,3},{4,20},{20... | collective-permute-start | bytes 221192 | tf_op jit(solution)/shard_map/ppermute | solution.py:27
  103.4 2.4 %collective-permute-start.16 = (bf16[96,384]{1,0:T(8,128)(2,1)S(1)}, bf16[96,384]{1,0:T(8,128)(2,1)S(1)}, u32[]{:S(2)}, u32[]{:S(2)}) collective-permute-start(bf16[96,384]{1,0:T(8,128)(2,1)S(1)} %sum.1.piece), channel_id=1, source_target_pairs={{0,8},{8,0},{1,9},{9,1},{2,10},{10,2},{3,11},{11,3},{4,12},{12,4},... | collective-permute-start | bytes 221192 | tf_op jit(solution)/shard_map/ppermute | solution.py:27
  105.8 1.3 %collective-permute-start.17 = (bf16[96,384]{1,0:T(8,128)(2,1)S(1)}, bf16[96,384]{1,0:T(8,128)(2,1)S(1)}, u32[]{:S(2)}, u32[]{:S(2)}) collective-permute-start(bf16[96,384]{1,0:T(8,128)(2,1)S(1)} %collective-permute-done.15.piece_x), channel_id=1, source_target_pairs={{0,8},{8,0},{1,9},{9,1},{2,10},{10,2},{3,11},{11,3},{4,12},{12,4},... | collective-permute-start | bytes 221192 | tf_op jit(solution)/shard_map/ppermute | solution.py:27
  107.3 6.5 %collective-permute-start.20 = (bf16[224,384]{1,0:T(8,128)(2,1)S(1)}, bf16[224,384]{1,0:T(8,128)(2,1)S(1)}, u32[]{:S(2)}, u32[]{:S(2)}) collective-permute-start(bf16[224,384]{1,0:T(8,128)(2,1)S(1)} %add.23.own), channel_id=1, source_target_pairs={{0,1},{1,0},{2,3},{3,2},{4,5},{5,4},{6,7},{7,6},{8,9},{9,8},{10,11... | collective-permute-start | bytes 516104 | tf_op jit(solution)/shard_map/ppermute | solution.py:27
  109.1 7.0 %collective-permute-start.21 = (bf16[224,384]{1,0:T(8,128)(2,1)S(1)}, bf16[224,384]{1,0:T(8,128)(2,1)S(1)}, u32[]{:S(2)}, u32[]{:S(2)}) collective-permute-start(bf16[224,384]{1,0:T(8,128)(2,1)S(1)} %add.23.own), channel_id=1, source_target_pairs={{0,16},{16,0},{1,17},{17,1},{2,18},{18,2},{3,19},{19,3},{4,20},{20... | collective-permute-start | bytes 516104 | tf_op jit(solution)/shard_map/ppermute | solution.py:27
  113.8 5.6 %collective-permute-start.22 = (bf16[224,384]{1,0:T(8,128)(2,1)S(1)}, bf16[224,384]{1,0:T(8,128)(2,1)S(1)}, u32[]{:S(2)}, u32[]{:S(2)}) collective-permute-start(bf16[224,384]{1,0:T(8,128)(2,1)S(1)} %collective-permute-done.20.own_b), channel_id=1, source_target_pairs={{0,16},{16,0},{1,17},{17,1},{2,18},{18,2},{3,19},{19,3},{4,20},{20... | collective-permute-start | bytes 516104 | tf_op jit(solution)/shard_map/ppermute | solution.py:27
  115.6 4.0 %collective-permute-start.23 = (bf16[224,384]{1,0:T(8,128)(2,1)S(1)}, bf16[224,384]{1,0:T(8,128)(2,1)S(1)}, u32[]{:S(2)}, u32[]{:S(2)}) collective-permute-start(bf16[224,384]{1,0:T(8,128)(2,1)S(1)} %add.23.own), channel_id=1, source_target_pairs={{0,8},{8,0},{1,9},{9,1},{2,10},{10,2},{3,11},{11,3},{4,12},{12,4},... | collective-permute-start | bytes 516104 | tf_op jit(solution)/shard_map/ppermute | solution.py:27
  115.6 4.0 %collective-permute-start.24 = (bf16[224,384]{1,0:T(8,128)(2,1)S(1)}, bf16[224,384]{1,0:T(8,128)(2,1)S(1)}, u32[]{:S(2)}, u32[]{:S(2)}) collective-permute-start(bf16[224,384]{1,0:T(8,128)(2,1)S(1)} %collective-permute-done.20.own_b), channel_id=1, source_target_pairs={{0,8},{8,0},{1,9},{9,1},{2,10},{10,2},{3,11},{11,3},{4,12},{12,4},... | collective-permute-start | bytes 516104 | tf_op jit(solution)/shard_map/ppermute | solution.py:27
  116.1 3.5 %collective-permute-start.25 = (bf16[224,384]{1,0:T(8,128)(2,1)S(1)}, bf16[224,384]{1,0:T(8,128)(2,1)S(1)}, u32[]{:S(2)}, u32[]{:S(2)}) collective-permute-start(bf16[224,384]{1,0:T(8,128)(2,1)S(1)} %collective-permute-done.21.own_x), channel_id=1, source_target_pairs={{0,8},{8,0},{1,9},{9,1},{2,10},{10,2},{3,11},{11,3},{4,12},{12,4},... | collective-permute-start | bytes 516104 | tf_op jit(solution)/shard_map/ppermute | solution.py:27
  119.5 1.4 %collective-permute-start.26 = (bf16[224,384]{1,0:T(8,128)(2,1)S(1)}, bf16[224,384]{1,0:T(8,128)(2,1)S(1)}, u32[]{:S(2)}, u32[]{:S(2)}) collective-permute-start(bf16[224,384]{1,0:T(8,128)(2,1)S(1)} %collective-permute-done.22.own_both), channel_id=1, source_target_pairs={{0,8},{8,0},{1,9},{9,1},{2,10},{10,2},{3,11},{11,3},{4,12},{12,4},... | collective-permute-start | bytes 516104 | tf_op jit(solution)/shard_map/ppermute | solution.py:27
  (13 other events, 96.1 us)
